TPU v7x, 256 devices: a whole 4x4x8 slice. The times are simulated.
256 devices in a mesh: ia: 8 (over z), ja: 4 (over x_hi, core), ka: 8 (over y, x_lo).
Axes of the slice: x: 4 (x_hi: 2, x_lo: 2; x = x_hi * 2 + x_lo), y: 4, z: 8, core: 2. Of those that a mesh axis runs over, the one named last changes fastest.
Arguments:
- tensor: bfloat16 [256, 512, 512], P('ka', 'ia', 'ja'), may hold values from -768 to 768
- observed: int32 [256, 512, 512], P('ka', 'ia', 'ja'), may hold values from 0 to 1, as said below
- factor_a: bfloat16 [512, 128], P('ia', ('ja', 'ka')), may hold values from -6 to 6
- factor_b: bfloat16 [512, 128], P('ja', ('ia', 'ka')), may hold values from -6 to 6
- factor_c: bfloat16 [256, 128], P('ka', ('ia', 'ja')), may hold values from -6 to 6
Outputs:
- step_a: float32 [512, 128], P('ia', ('ja', 'ka'))
- step_b: float32 [512, 128], P('ja', ('ia', 'ka'))
- step_c: float32 [256, 128], P('ka', ('ia', 'ja'))
Inputs may be any that keep to these rules, and one draw needn't show every extreme that they name: `observed`: a 0/1 weight per cell.
All inputs are finite; a program needn't handle non-finite values.
Results may differ from a plain program's by a relative error of at most 0.0095.
Values may be sent and summed in bfloat16 or wider, within the bound.
No kernel may reach another device: no remote copies, remote signals or barrier semaphores. Data moves between devices by JAX's collectives and lax.ppermute only.
A program may use at most 64 MiB of HBM per device.

v0:
```python
import functools

import jax
import jax.numpy as jnp
from jax import lax
from jax.sharding import Mesh
from jax.sharding import PartitionSpec as P

ITERS = 2
JA = ("ja_0", "ja_1")
KA = ("ka_0", "ka_1")
JA_KA = ("ja_0", "ja_1", "ka_0", "ka_1")
IA_KA = ("ia", "ka_0", "ka_1")
IA_JA = ("ia", "ja_0", "ja_1")
IA_JA_KA = ("ia", "ja_0", "ja_1", "ka_0", "ka_1")


DAMP = 1.0


def from_everyone(x, axis):
    count = lax.axis_size(axis)
    return lax.all_to_all(jnp.broadcast_to(x[None], (count, *x.shape)), axis, 0, 0, tiled=True)


def laid_out(blocks, dim):
    blocks = jnp.moveaxis(blocks, 0, dim)
    lengths = blocks.shape
    return blocks.reshape(*lengths[:dim], lengths[dim] * lengths[dim + 1], *lengths[dim + 2 :])


def collect(x, axis, dim):
    blocks = from_everyone(x, axis)
    return laid_out(blocks, dim)


def in_blocks(x, dim, count):
    before, after = (x.shape[:dim], x.shape[dim + 1 :])
    return jnp.moveaxis(x.reshape(*before, count, -1, *after), dim, 0)


def sent_and_summed(x, axis, dim):
    count = lax.axis_size(axis)
    blocks = lax.all_to_all(in_blocks(x, dim, count), axis, 0, 0, tiled=True)
    return jnp.sum(blocks, axis=0)


def by_axis(x, axes):
    return functools.reduce(lax.psum, axes, x)


def against(left_side, right_side):
    return lax.dot_general(
        left_side, right_side, (((1,), (1,)), ((), ())), preferred_element_type=jnp.float32
    )


def local(tensor, observed, factor_a, factor_b, factor_c):
    depth_rows, height_rows, width_cols = tensor.shape
    divisor = width_cols * lax.axis_size(JA) * (depth_rows * lax.axis_size(KA)) / 32.0
    full_a = collect(factor_a, JA_KA, 1)
    full_b = collect(factor_b, IA_KA, 1)
    full_c = collect(factor_c, IA_JA, 1)
    columns = full_a.shape[1]
    wide_a = full_a.astype(jnp.float32)
    wide_c = full_c.astype(jnp.float32)
    weight = (observed.astype(jnp.float32) * (1.0 / divisor)).astype(jnp.bfloat16)
    weight = weight.reshape(depth_rows * height_rows, width_cols)
    paired = (
        (wide_c[:, None, :] * wide_a[None, :, :])
        .astype(jnp.bfloat16)
        .reshape(depth_rows * height_rows, columns)
    )

    def partials(weighted):
        part_b = lax.dot_general(
            weighted, paired, (((0,), (0,)), ((), ())), preferred_element_type=jnp.float32
        )
        mixture = jnp.dot(weighted, full_b, preferred_element_type=jnp.float32).reshape(
            depth_rows, height_rows, columns
        )
        part_a = jnp.einsum("kir,kr->ir", mixture, wide_c)
        part_c = jnp.einsum("kir,ir->kr", mixture, wide_a)
        return (part_a, part_b, part_c)

    def settle(parts):
        total_a = sent_and_summed(parts[0], JA_KA, 1)
        total_b = sent_and_summed(parts[1], IA_KA, 1)
        total_c = sent_and_summed(parts[2], IA_JA, 1)
        return (total_a, total_b, total_c)

    scales = (1.0, 1.0, 1.0)

    def inner_sum(first, second):
        local_sum = sum(
            (
                jnp.sum(left_side * right_side) * factor
                for left_side, right_side, factor in zip(first, second, scales)
            )
        )
        return by_axis(local_sum, IA_JA_KA)

    def expand(direction):
        hat_a = direction[0].astype(jnp.bfloat16)
        hat_b = direction[1].astype(jnp.bfloat16)
        hat_c = direction[2].astype(jnp.bfloat16)
        return (collect(hat_a, JA_KA, 1), collect(hat_b, IA_KA, 1), collect(hat_c, IA_JA, 1))

    def hessian_times(direction):
        hat_a, hat_b, hat_c = expand(direction)
        sideways = (
            hat_c.astype(jnp.float32)[:, None, :] * wide_a[None, :, :]
            + wide_c[:, None, :] * hat_a.astype(jnp.float32)[None, :, :]
        )
        sideways = sideways.astype(jnp.bfloat16).reshape(depth_rows * height_rows, columns)
        tangent = against(paired, hat_b) + against(sideways, full_b)
        weighted = (weight.astype(jnp.float32) * tangent).astype(jnp.bfloat16)
        parts = settle(partials(weighted))
        return tuple((part + DAMP * vector for part, vector in zip(parts, direction)))

    fitted = against(paired, full_b)
    values = tensor.reshape(depth_rows * height_rows, width_cols).astype(jnp.float32)
    errors = (weight.astype(jnp.float32) * (values - fitted)).astype(jnp.bfloat16)
    gradient = settle(partials(errors))
    solution = tuple((jnp.zeros_like(vector) for vector in gradient))
    residual = gradient
    direction = gradient
    norm_now = inner_sum(residual, residual)
    for iteration in range(ITERS):
        product = hessian_times(direction)
        step_size = norm_now / inner_sum(direction, product)
        solution = tuple(
            (vector + step_size * update for vector, update in zip(solution, direction))
        )
        if iteration + 1 < ITERS:
            residual = tuple(
                (vector - step_size * update for vector, update in zip(residual, product))
            )
            norm_next = inner_sum(residual, residual)
            direction = tuple(
                (
                    vector + norm_next / norm_now * update
                    for vector, update in zip(residual, direction)
                )
            )
            norm_now = norm_next
    step_a, step_b, step_c = solution
    return (step_a, step_b, step_c)


def solution(mesh):
    torus = Mesh(
        mesh.devices.reshape(mesh.shape["ia"], 2, 2, 4, 2), ("ia", "ja_0", "ja_1", "ka_0", "ka_1")
    )
    return jax.shard_map(
        local,
        mesh=torus,
        in_specs=(P(KA, "ia", JA), P(KA, "ia", JA), P("ia", JA_KA), P(JA, IA_KA), P(KA, IA_JA)),
        out_specs=(P("ia", JA_KA), P(JA, IA_KA), P(KA, IA_JA)),
        check_vma=False,
    )
```

profile of v0, /device:TPU:1, one launch (start us, length us, event | category | flops | bytes accessed | tf_op | source)
XLA Modules:
  0.0 407.1 jit_solution(10883659675060064923)
XLA Ops:
  1.4 15.3 %all_to_all.90 = bf16[32,2,128]{2,1,0:T(2,128)(2,1)S(1)} all-to-all(bf16[32,2,128]{2,1,0:T(2,128)(2,1)S(1)} %reshape.237), channel_id=1, replica_groups=mesh['ia'=8,'ja_0'=2,'ja_1'=2,'ka_0'=4,'ka_1'=2] {'ja_0','ja_1','ka_0','..., dimensions={0} | all-to-all | bytes 32768 | tf_op jit(solution)/shard_map/all_to_all | solution.py:23
  17.4 9.9 %all-to-all-start = ((bf16[32,32,4]{1,2,0:T(4,128)(2,1)}), bf16[32,32,4]{1,2,0:T(4,128)(2,1)S(1)}, u32[]{:S(2)}, u32[]{:S(2)}) async-start(bf16[32,32,4]{1,2,0:T(4,128)(2,1)} %broadcast_in_dim.18), calls=%async_computation | async-start | bytes 65536 | tf_op jit(solution)/shard_map/all_to_all | solution.py:23
  28.8 8.1 %all-to-all-done = bf16[32,32,4]{1,2,0:T(4,128)(2,1)S(1)} async-done(((bf16[32,32,4]{1,2,0:T(4,128)(2,1)}), bf16[32,32,4]{1,2,0:T(4,128)(2,1)S(1)}, u32[]{:S(2)}, u32[]{:S(2)}) %all-to-all-start) | async-done | bytes 8224 | tf_op jit(solution)/shard_map/all_to_all | solution.py:23
  42.9 8.5 %all-to-all-done.2 = bf16[64,128,2]{1,2,0:T(2,128)(2,1)S(1)} async-done(((bf16[64,128,2]{1,2,0:T(2,128)(2,1)}), bf16[64,128,2]{1,2,0:T(2,128)(2,1)S(1)}, u32[]{:S(2)}, u32[]{:S(2)}) %all-to-all-start.2) | async-done | bytes 32800 | tf_op jit(solution)/shard_map/all_to_all | solution.py:23
  63.5 6.0 %all-to-all-done.3 = f32[32,1,256]{2,1,0:T(1,128)S(1)} async-done(((f32[32,1,256]{2,1,0:T(1,128)}), f32[32,1,256]{2,1,0:T(1,128)S(1)}, u32[]{:S(2)}, u32[]{:S(2)}) %all-to-all-start.3) | async-done | bytes 32800 | tf_op jit(solution)/shard_map/all_to_all | solution.py:44
  75.5 7.4 %all-to-all-done.5 = f32[32,1,128]{2,1,0:T(1,128)S(1)} async-done(((f32[32,1,128]{2,1,0:T(1,128)}), f32[32,1,128]{2,1,0:T(1,128)S(1)}, u32[]{:S(2)}, u32[]{:S(2)}) %all-to-all-start.5) | async-done | bytes 16416 | tf_op jit(solution)/shard_map/all_to_all | solution.py:44
  87.6 6.1 %all-to-all-done.8 = bf16[32,2,128]{2,1,0:T(2,128)(2,1)S(1)} async-done(((bf16[32,2,128]{2,1,0:T(2,128)(2,1)}), bf16[32,2,128]{2,1,0:T(2,128)(2,1)S(1)}, u32[]{:S(2)}, u32[]{:S(2)}) %all-to-all-start.8) | async-done | bytes 16416 | tf_op jit(solution)/shard_map/all_to_all | solution.py:23
  99.6 8.7 %all-to-all-done.7 = bf16[32,32,4]{1,2,0:T(4,128)(2,1)S(1)} async-done(((bf16[32,32,4]{1,2,0:T(4,128)(2,1)}), bf16[32,32,4]{1,2,0:T(4,128)(2,1)S(1)}, u32[]{:S(2)}, u32[]{:S(2)}) %all-to-all-start.7) | async-done | bytes 8224 | tf_op jit(solution)/shard_map/all_to_all | solution.py:23
  113.1 9.3 %all-to-all-done.4 = f32[64,128,2]{1,2,0:T(2,128)S(1)} async-done(((f32[64,128,2]{1,2,0:T(2,128)}), f32[64,128,2]{1,2,0:T(2,128)S(1)}, u32[]{:S(2)}, u32[]{:S(2)}) %all-to-all-start.4) | async-done | bytes 65568 | tf_op jit(solution)/shard_map/all_to_all | solution.py:44
  128.1 9.0 %all-to-all-done.6 = bf16[64,128,2]{1,2,0:T(2,128)(2,1)S(1)} async-done(((bf16[64,128,2]{1,2,0:T(2,128)(2,1)}), bf16[64,128,2]{1,2,0:T(2,128)(2,1)S(1)}, u32[]{:S(2)}, u32[]{:S(2)}) %all-to-all-start.6) | async-done | bytes 32800 | tf_op jit(solution)/shard_map/all_to_all | solution.py:23
  143.5 6.2 %all-to-all-start.9 = ((f32[32,1,256]{2,1,0:T(1,128)}), f32[32,1,256]{2,1,0:T(1,128)S(1)}, u32[]{:S(2)}, u32[]{:S(2)}) async-start(f32[32,1,256]{2,1,0:T(1,128)} %reshape.245), calls=%async_computation.9 | async-start | bytes 65536 | tf_op jit(solution)/shard_map/all_to_all | solution.py:44
  151.5 5.6 %all-to-all-done.9 = f32[32,1,256]{2,1,0:T(1,128)S(1)} async-done(((f32[32,1,256]{2,1,0:T(1,128)}), f32[32,1,256]{2,1,0:T(1,128)S(1)}, u32[]{:S(2)}, u32[]{:S(2)}) %all-to-all-start.9) | async-done | bytes 32800 | tf_op jit(solution)/shard_map/all_to_all | solution.py:44
  162.4 8.0 %all-to-all-done.11 = f32[32,1,128]{2,1,0:T(1,128)S(1)} async-done(((f32[32,1,128]{2,1,0:T(1,128)}), f32[32,1,128]{2,1,0:T(1,128)S(1)}, u32[]{:S(2)}, u32[]{:S(2)}) %all-to-all-start.11) | async-done | bytes 16416 | tf_op jit(solution)/shard_map/all_to_all | solution.py:44
  176.5 8.0 %all-to-all-done.10 = f32[64,128,2]{1,2,0:T(2,128)S(1)} async-done(((f32[64,128,2]{1,2,0:T(2,128)}), f32[64,128,2]{1,2,0:T(2,128)S(1)}, u32[]{:S(2)}, u32[]{:S(2)}) %all-to-all-start.10) | async-done | bytes 65568 | tf_op jit(solution)/shard_map/all_to_all | solution.py:44
  189.0 12.1 %all-reduce = (f32[]{:T(128)}, f32[]{:T(128)}) all-reduce(f32[]{:T(128)S(6)} %add.153, f32[]{:T(128)S(6)} %add.160), channel_id=1, replica_groups=mesh['ia'=8,'ja_0'=2,'ja_1'=2,'ka_0'=4,'ka_1'=2] {'ia'}, use_global_device_ids=true, to_apply=%region_6.0 | all-reduce | flops 2 | bytes 16 | tf_op jit(solution)/shard_map/psum | solution.py:49
  201.1 5.9 %all-reduce.4 = (f32[]{:T(128)}, f32[]{:T(128)}) all-reduce(f32[]{:T(128)} %get-tuple-element.9, f32[]{:T(128)} %get-tuple-element.10), channel_id=1, replica_groups=mesh['ia'=8,'ja_0'=2,'ja_1'=2,'ka_0'=4,'ka_1'=2] {'ja_0'}, use_global_device_ids=true, to_apply=%region_7.0 | all-reduce | flops 2 | bytes 16 | tf_op jit(solution)/shard_map/psum | solution.py:49
  207.0 9.1 %all-reduce.3 = (f32[]{:T(128)}, f32[]{:T(128)}) all-reduce(f32[]{:T(128)} %get-tuple-element.17, f32[]{:T(128)} %get-tuple-element.18), channel_id=1, replica_groups=mesh['ia'=8,'ja_0'=2,'ja_1'=2,'ka_0'=4,'ka_1'=2] {'ja_1'}, use_global_device_ids=true, to_apply=%region_8.0 | all-reduce | flops 2 | bytes 16 | tf_op jit(solution)/shard_map/psum | solution.py:49
  216.1 7.3 %all-reduce.1 = (f32[]{:T(128)}, f32[]{:T(128)}) all-reduce(f32[]{:T(128)} %get-tuple-element.15, f32[]{:T(128)} %get-tuple-element.16), channel_id=1, replica_groups=mesh['ia'=8,'ja_0'=2,'ja_1'=2,'ka_0'=4,'ka_1'=2] {'ka_0'}, use_global_device_ids=true, to_apply=%region_9.0 | all-reduce | flops 2 | bytes 16 | tf_op jit(solution)/shard_map/psum | solution.py:49
  232.9 12.0 %psum.150 = f32[]{:T(128)} all-reduce(f32[]{:T(128)S(6)} %add.162), channel_id=1, replica_groups=mesh['ia'=8,'ja_0'=2,'ja_1'=2,'ka_0'=4,'ka_1'=2] {'ia'}, use_global_device_ids=true, to_apply=%region_25.0 | all-reduce | flops 1 | bytes 8 | tf_op jit(solution)/shard_map/psum | solution.py:49
  245.0 5.9 %psum.151 = f32[]{:T(128)} all-reduce(f32[]{:T(128)} %psum.150), channel_id=1, replica_groups=mesh['ia'=8,'ja_0'=2,'ja_1'=2,'ka_0'=4,'ka_1'=2] {'ja_0'}, use_global_device_ids=true, to_apply=%region_26.0 | all-reduce | flops 1 | bytes 8 | tf_op jit(solution)/shard_map/psum | solution.py:49
  250.9 11.2 %psum.152 = f32[]{:T(128)} all-reduce(f32[]{:T(128)} %psum.151), channel_id=1, replica_groups=mesh['ia'=8,'ja_0'=2,'ja_1'=2,'ka_0'=4,'ka_1'=2] {'ja_1'}, use_global_device_ids=true, to_apply=%region_27.0 | all-reduce | flops 1 | bytes 8 | tf_op jit(solution)/shard_map/psum | solution.py:49
  262.0 7.3 %psum.153 = f32[]{:T(128)} all-reduce(f32[]{:T(128)} %psum.152), channel_id=1, replica_groups=mesh['ia'=8,'ja_0'=2,'ja_1'=2,'ka_0'=4,'ka_1'=2] {'ka_0'}, use_global_device_ids=true, to_apply=%region_28.0 | all-reduce | flops 1 | bytes 8 | tf_op jit(solution)/shard_map/psum | solution.py:49
  275.7 7.4 %all-to-all-start.13 = ((bf16[32,32,4]{1,2,0:T(4,128)(2,1)}), bf16[32,32,4]{1,2,0:T(4,128)(2,1)S(1)}, u32[]{:S(2)}, u32[]{:S(2)}) async-start(bf16[32,32,4]{1,2,0:T(4,128)(2,1)} %broadcast_in_dim.25), calls=%async_computation.13 | async-start | bytes 65536 | tf_op jit(solution)/shard_map/all_to_all | solution.py:23
  283.9 8.9 %all-to-all-done.13 = bf16[32,32,4]{1,2,0:T(4,128)(2,1)S(1)} async-done(((bf16[32,32,4]{1,2,0:T(4,128)(2,1)}), bf16[32,32,4]{1,2,0:T(4,128)(2,1)S(1)}, u32[]{:S(2)}, u32[]{:S(2)}) %all-to-all-start.13) | async-done | bytes 8224 | tf_op jit(solution)/shard_map/all_to_all | solution.py:23
  296.8 6.9 %all-to-all-done.14 = bf16[32,2,128]{2,1,0:T(2,128)(2,1)S(1)} async-done(((bf16[32,2,128]{2,1,0:T(2,128)(2,1)}), bf16[32,2,128]{2,1,0:T(2,128)(2,1)S(1)}, u32[]{:S(2)}, u32[]{:S(2)}) %all-to-all-start.14) | async-done | bytes 16416 | tf_op jit(solution)/shard_map/all_to_all | solution.py:23
  309.3 8.9 %all-to-all-done.12 = bf16[64,128,2]{1,2,0:T(2,128)(2,1)S(1)} async-done(((bf16[64,128,2]{1,2,0:T(2,128)(2,1)}), bf16[64,128,2]{1,2,0:T(2,128)(2,1)S(1)}, u32[]{:S(2)}, u32[]{:S(2)}) %all-to-all-start.12) | async-done | bytes 32800 | tf_op jit(solution)/shard_map/all_to_all | solution.py:23
  339.9 8.6 %all-to-all-done.17 = f32[32,1,128]{2,1,0:T(1,128)S(1)} async-done(((f32[32,1,128]{2,1,0:T(1,128)}), f32[32,1,128]{2,1,0:T(1,128)S(1)}, u32[]{:S(2)}, u32[]{:S(2)}) %all-to-all-start.17) | async-done | bytes 16416 | tf_op jit(solution)/shard_map/all_to_all | solution.py:44
  355.2 7.4 %all-to-all-done.16 = f32[64,128,2]{1,2,0:T(2,128)S(1)} async-done(((f32[64,128,2]{1,2,0:T(2,128)}), f32[64,128,2]{1,2,0:T(2,128)S(1)}, u32[]{:S(2)}, u32[]{:S(2)}) %all-to-all-start.16) | async-done | bytes 65568 | tf_op jit(solution)/shard_map/all_to_all | solution.py:44
  365.2 12.1 %psum.155 = f32[]{:T(128)} all-reduce(f32[]{:T(128)S(6)} %add.172), channel_id=1, replica_groups=mesh['ia'=8,'ja_0'=2,'ja_1'=2,'ka_0'=4,'ka_1'=2] {'ia'}, use_global_device_ids=true, to_apply=%region_36.0 | all-reduce | flops 1 | bytes 8 | tf_op jit(solution)/shard_map/psum | solution.py:49
  377.3 5.9 %psum.156 = f32[]{:T(128)} all-reduce(f32[]{:T(128)} %psum.155), channel_id=1, replica_groups=mesh['ia'=8,'ja_0'=2,'ja_1'=2,'ka_0'=4,'ka_1'=2] {'ja_0'}, use_global_device_ids=true, to_apply=%region_37.0 | all-reduce | flops 1 | bytes 8 | tf_op jit(solution)/shard_map/psum | solution.py:49
  383.2 9.1 %psum.157 = f32[]{:T(128)} all-reduce(f32[]{:T(128)} %psum.156), channel_id=1, replica_groups=mesh['ia'=8,'ja_0'=2,'ja_1'=2,'ka_0'=4,'ka_1'=2] {'ja_1'}, use_global_device_ids=true, to_apply=%region_38.0 | all-reduce | flops 1 | bytes 8 | tf_op jit(solution)/shard_map/psum | solution.py:49
  392.3 7.3 %psum.158 = f32[]{:T(128)} all-reduce(f32[]{:T(128)} %psum.157), channel_id=1, replica_groups=mesh['ia'=8,'ja_0'=2,'ja_1'=2,'ka_0'=4,'ka_1'=2] {'ka_0'}, use_global_device_ids=true, to_apply=%region_39.0 | all-reduce | flops 1 | bytes 8 | tf_op jit(solution)/shard_map/psum | solution.py:49
  (130 shorter events, 124.9 us)
Async XLA Ops:
  0.6 0.7 copy-start
  1.4 15.3 %copy-start.4 = (bf16[32,4]{0,1:T(4,128)(2,1)S(1)}, bf16[32,4]{0,1:T(4,128)(2,1)}, u32[]{:S(2)}) copy-start(bf16[32,4]{0,1:T(4,128)(2,1)} %param.9) | copy-start | bytes 772
  17.4 19.5 %all-to-all-start = ((bf16[32,32,4]{1,2,0:T(4,128)(2,1)}), bf16[32,32,4]{1,2,0:T(4,128)(2,1)S(1)}, u32[]{:S(2)}, u32[]{:S(2)}) async-start(bf16[32,32,4]{1,2,0:T(4,128)(2,1)} %broadcast_in_dim.18), calls=%async_computation | async-start | bytes 65536 | tf_op jit(solution)/shard_map/all_to_all | solution.py:23
  28.7 8.2 %copy-start.5 = (bf16[128,2]{0,1:T(2,128)(2,1)S(1)}, bf16[128,2]{0,1:T(2,128)(2,1)}, u32[]{:S(2)}) copy-start(bf16[128,2]{0,1:T(2,128)(2,1)} %param.8) | copy-start | bytes 1540
  37.5 13.9 %all-to-all-start.2 = ((bf16[64,128,2]{1,2,0:T(2,128)(2,1)}), bf16[64,128,2]{1,2,0:T(2,128)(2,1)S(1)}, u32[]{:S(2)}, u32[]{:S(2)}) async-start(bf16[64,128,2]{1,2,0:T(2,128)(2,1)} %broadcast_in_dim.20), calls=%async_computation.2 | async-start | bytes 65536 | tf_op jit(solution)/shard_map/all_to_all | solution.py:23
  42.6 8.9 %copy-start.3 = (bf16[32,64,128]{2,1,0:T(8,128)(2,1)S(1)}, bf16[32,64,128]{2,1,0:T(8,128)(2,1)}, u32[]{:S(2)}) copy-start(bf16[32,64,128]{2,1,0:T(8,128)(2,1)} %param.5) | copy-start | bytes 1572868
  54.6 7.5 %copy-start.1 = (bf16[32,64,128]{1,0,2:T(8,128)(2,1)S(1)}, bf16[32,64,128]{1,0,2:T(8,128)(2,1)}, u32[]{:S(2)}) copy-start(bf16[32,64,128]{1,0,2:T(8,128)(2,1)} %copy.91) | copy-start | bytes 1572868
  57.0 12.5 %all-to-all-start.3 = ((f32[32,1,256]{2,1,0:T(1,128)}), f32[32,1,256]{2,1,0:T(1,128)S(1)}, u32[]{:S(2)}, u32[]{:S(2)}) async-start(f32[32,1,256]{2,1,0:T(1,128)} %reshape.239), calls=%async_computation.3 | async-start | bytes 65536 | tf_op jit(solution)/shard_map/all_to_all | solution.py:44
  69.5 13.4 %all-to-all-start.5 = ((f32[32,1,128]{2,1,0:T(1,128)}), f32[32,1,128]{2,1,0:T(1,128)S(1)}, u32[]{:S(2)}, u32[]{:S(2)}) async-start(f32[32,1,128]{2,1,0:T(1,128)} %reshape.243), calls=%async_computation.5 | async-start | bytes 32768 | tf_op jit(solution)/shard_map/all_to_all | solution.py:44
  82.9 10.9 %all-to-all-start.8 = ((bf16[32,2,128]{2,1,0:T(2,128)(2,1)}), bf16[32,2,128]{2,1,0:T(2,128)(2,1)S(1)}, u32[]{:S(2)}, u32[]{:S(2)}) async-start(bf16[32,2,128]{2,1,0:T(2,128)(2,1)} %reshape.241), calls=%async_computation.8 | async-start | bytes 32768 | tf_op jit(solution)/shard_map/all_to_all | solution.py:23
  94.4 13.9 %all-to-all-start.7 = ((bf16[32,32,4]{1,2,0:T(4,128)(2,1)}), bf16[32,32,4]{1,2,0:T(4,128)(2,1)S(1)}, u32[]{:S(2)}, u32[]{:S(2)}) async-start(bf16[32,32,4]{1,2,0:T(4,128)(2,1)} %broadcast_in_dim.22), calls=%async_computation.7 | async-start | bytes 65536 | tf_op jit(solution)/shard_map/all_to_all | solution.py:23
  108.3 14.1 %all-to-all-start.4 = ((f32[64,128,2]{1,2,0:T(2,128)}), f32[64,128,2]{1,2,0:T(2,128)S(1)}, u32[]{:S(2)}, u32[]{:S(2)}) async-start(f32[64,128,2]{1,2,0:T(2,128)} %copy.74), calls=%async_computation.4 | async-start | bytes 131072 | tf_op jit(solution)/shard_map/all_to_all | solution.py:44
  123.1 13.9 %all-to-all-start.6 = ((bf16[64,128,2]{1,2,0:T(2,128)(2,1)}), bf16[64,128,2]{1,2,0:T(2,128)(2,1)S(1)}, u32[]{:S(2)}, u32[]{:S(2)}) async-start(bf16[64,128,2]{1,2,0:T(2,128)(2,1)} %broadcast_in_dim.21), calls=%async_computation.6 | async-start | bytes 65536 | tf_op jit(solution)/shard_map/all_to_all | solution.py:23
  140.4 1.9 copy-start.2
  143.5 13.6 %all-to-all-start.9 = ((f32[32,1,256]{2,1,0:T(1,128)}), f32[32,1,256]{2,1,0:T(1,128)S(1)}, u32[]{:S(2)}, u32[]{:S(2)}) async-start(f32[32,1,256]{2,1,0:T(1,128)} %reshape.245), calls=%async_computation.9 | async-start | bytes 65536 | tf_op jit(solution)/shard_map/all_to_all | solution.py:44
  157.1 13.3 %all-to-all-start.11 = ((f32[32,1,128]{2,1,0:T(1,128)}), f32[32,1,128]{2,1,0:T(1,128)S(1)}, u32[]{:S(2)}, u32[]{:S(2)}) async-start(f32[32,1,128]{2,1,0:T(1,128)} %reshape.247), calls=%async_computation.11 | async-start | bytes 32768 | tf_op jit(solution)/shard_map/all_to_all | solution.py:44
  170.4 14.1 %all-to-all-start.10 = ((f32[64,128,2]{1,2,0:T(2,128)}), f32[64,128,2]{1,2,0:T(2,128)S(1)}, u32[]{:S(2)}, u32[]{:S(2)}) async-start(f32[64,128,2]{1,2,0:T(2,128)} %copy.81), calls=%async_computation.10 | async-start | bytes 131072 | tf_op jit(solution)/shard_map/all_to_all | solution.py:44
  275.7 17.1 %all-to-all-start.13 = ((bf16[32,32,4]{1,2,0:T(4,128)(2,1)}), bf16[32,32,4]{1,2,0:T(4,128)(2,1)S(1)}, u32[]{:S(2)}, u32[]{:S(2)}) async-start(bf16[32,32,4]{1,2,0:T(4,128)(2,1)} %broadcast_in_dim.25), calls=%async_computation.13 | async-start | bytes 65536 | tf_op jit(solution)/shard_map/all_to_all | solution.py:23
  292.8 10.9 %all-to-all-start.14 = ((bf16[32,2,128]{2,1,0:T(2,128)(2,1)}), bf16[32,2,128]{2,1,0:T(2,128)(2,1)S(1)}, u32[]{:S(2)}, u32[]{:S(2)}) async-start(bf16[32,2,128]{2,1,0:T(2,128)(2,1)} %reshape.249), calls=%async_computation.14 | async-start | bytes 32768 | tf_op jit(solution)/shard_map/all_to_all | solution.py:23
  304.3 13.9 %all-to-all-start.12 = ((bf16[64,128,2]{1,2,0:T(2,128)(2,1)}), bf16[64,128,2]{1,2,0:T(2,128)(2,1)S(1)}, u32[]{:S(2)}, u32[]{:S(2)}) async-start(bf16[64,128,2]{1,2,0:T(2,128)(2,1)} %broadcast_in_dim.24), calls=%async_computation.12 | async-start | bytes 65536 | tf_op jit(solution)/shard_map/all_to_all | solution.py:23
  322.5 12.7 %all-to-all-start.15 = ((f32[32,1,256]{2,1,0:T(1,128)}), f32[32,1,256]{2,1,0:T(1,128)S(1)}, u32[]{:S(2)}, u32[]{:S(2)}) async-start(f32[32,1,256]{2,1,0:T(1,128)} %reshape.251), calls=%async_computation.15 | async-start | bytes 65536 | tf_op jit(solution)/shard_map/all_to_all | solution.py:44
  335.2 13.3 %all-to-all-start.17 = ((f32[32,1,128]{2,1,0:T(1,128)}), f32[32,1,128]{2,1,0:T(1,128)S(1)}, u32[]{:S(2)}, u32[]{:S(2)}) async-start(f32[32,1,128]{2,1,0:T(1,128)} %reshape.253), calls=%async_computation.17 | async-start | bytes 32768 | tf_op jit(solution)/shard_map/all_to_all | solution.py:44
  348.5 14.1 %all-to-all-start.16 = ((f32[64,128,2]{1,2,0:T(2,128)}), f32[64,128,2]{1,2,0:T(2,128)S(1)}, u32[]{:S(2)}, u32[]{:S(2)}) async-start(f32[64,128,2]{1,2,0:T(2,128)} %copy.88), calls=%async_computation.16 | async-start | bytes 131072 | tf_op jit(solution)/shard_map/all_to_all | solution.py:44
where the time goes:
time: 410 us; the launch traced here: 407 us
  blocking collectives  134 us (33%)
  waiting for transfers between devices  131 us (32%)
  starting transfers between devices  85.4 us (21%)
  local copies, waits for them, and re-layouts  21.2 us (5%)
  other arithmetic  14 us (3%)
  between operations  12.7 us (3%)
  matrix products  9.04 us (2%)
    psum x15, blocking collectives, by_axis(): return functools.reduce(lax.psum, axes, x)  118 us
    all_to_all x9, waiting for transfers between devices, sent_and_summed(): blocks = lax.all_to_all(in_blocks(x, dim, count), axis, 0, 0, tiled=True)  65.9 us
    all_to_all x8, waiting for transfers between devices, from_everyone(): lax.all_to_all(jnp.broadcast_to(x[None], (count, *x.shape)), axis, 0, 0,...  65.1 us
    all_to_all x8, starting transfers between devices, from_everyone(): lax.all_to_all(jnp.broadcast_to(x[None], (count, *x.shape)), axis, 0, 0,...  43.3 us
    all_to_all x9, starting transfers between devices, sent_and_summed(): blocks = lax.all_to_all(in_blocks(x, dim, count), axis, 0, 0, tiled=True)  42.1 us
    all_to_all x1, blocking collectives, from_everyone(): lax.all_to_all(jnp.broadcast_to(x[None], (count, *x.shape)), axis, 0, 0,...  15.3 us
  transfers between devices with their start and end apart: 17, of which 17 were waited for; matrix products, arithmetic and copies ran while one was open for 5% of the time, Pallas kernels for 0%

commit v1 on v0

v1 whole, which is shorter than its diff:
```python
import jax
import jax.numpy as jnp
from jax import lax
from jax.sharding import Mesh
from jax.sharding import PartitionSpec as P

JA = ("ja_0", "ja_1")
KA = ("ka_0", "ka_1")
PLANE = ("ja_0", "ja_1", "ka_0", "ka_1")
IA_KA = ("ia", "ka_0", "ka_1")
IA_JA = ("ia", "ja_0", "ja_1")
EVERY = ("ia", "ja_0", "ja_1", "ka_0", "ka_1")
F32, BF16 = jnp.float32, jnp.bfloat16


def exchange(blocks, axes):
    return lax.all_to_all(blocks, axes, 0, 0, tiled=True)


def to_everyone(row, axes):
    count = lax.axis_size(axes)
    return exchange(jnp.broadcast_to(row[None], (count, *row.shape)), axes)


def local(tensor, observed, factor_a, factor_b, factor_c):
    depth, height, width = tensor.shape
    n_z, n_j, n_k = lax.axis_size("ia"), lax.axis_size(JA), lax.axis_size(KA)
    z, jb, kb = lax.axis_index("ia"), lax.axis_index(JA), lax.axis_index(KA)
    cols_a, cols_b, cols_c = factor_a.shape[1], factor_b.shape[1], factor_c.shape[1]
    plane = n_j * n_k
    rank = cols_a * plane
    divisor = width * n_j * (depth * n_k) / 32.0

    packed = jnp.concatenate([factor_a.T.ravel(), factor_b.T.ravel(), factor_c.T.ravel()])
    everything = to_everyone(packed[None], EVERY).reshape(n_z, n_j, n_k, -1)
    s_a, s_b = factor_a.size, factor_b.size
    at = lax.dynamic_index_in_dim(everything[..., :s_a], z, 0, False).reshape(rank, height)
    bt = lax.dynamic_index_in_dim(everything[..., s_a : s_a + s_b], jb, 1, False).reshape(rank, width)
    ct = lax.dynamic_index_in_dim(everything[..., s_a + s_b :], kb, 2, False).reshape(rank, depth)

    weight = observed.reshape(depth * height, width).astype(F32) * (1.0 / divisor)
    wide_a, wide_c = at.T.astype(F32), ct.T.astype(F32)
    paired = (wide_c[:, None, :] * wide_a[None]).astype(BF16).reshape(depth * height, rank)

    def reduced(weighted, scalars):
        part_b = lax.dot_general(paired, weighted, (((0,), (0,)), ((), ())), preferred_element_type=F32)
        mixture = lax.dot_general(weighted, bt, (((1,), (1,)), ((), ())), preferred_element_type=F32)
        mixture = mixture.reshape(depth, height, rank)
        part_a = jnp.sum(mixture * wide_c[:, None, :], axis=0).T
        part_c = jnp.sum(mixture * wide_a[None], axis=1).T
        extra = jnp.broadcast_to(scalars[None], (rank, scalars.size))
        payload = jnp.concatenate([part_b, part_a, part_c, extra], axis=1)
        got = exchange(payload.reshape(plane, cols_a, -1), PLANE)
        got = got.reshape(n_j, n_k, cols_a, -1)
        own_b = jnp.sum(got[..., :width], axis=1)
        rest = got[..., width:]
        own_a = jnp.sum(rest[..., :height], axis=(0, 1))
        own_c = jnp.sum(rest[..., height : height + depth], axis=0)
        own_s = jnp.sum(rest[..., height + depth :], axis=(0, 1))[0]
        line = jnp.concatenate([own_b.ravel(), own_c.ravel(), own_s])
        line = jnp.sum(to_everyone(line[None], "ia"), axis=0)[0]
        own_b = line[: own_b.size].reshape(own_b.shape)
        own_c = line[own_b.size : own_b.size + own_c.size].reshape(own_c.shape)
        totals = line[own_b.size + own_c.size :]
        back = jnp.concatenate(
            [
                jnp.broadcast_to(own_b[:, None], (n_j, n_k, cols_a, width)),
                jnp.broadcast_to(own_a[None, None], (n_j, n_k, cols_a, height)),
                jnp.broadcast_to(own_c[None], (n_j, n_k, cols_a, depth)),
            ],
            axis=-1,
        )
        full = exchange(back.reshape(plane, cols_a, -1), PLANE).reshape(rank, -1)
        return full, totals

    def split(full):
        return full[:, width : width + height], full[:, :width], full[:, width + height :]

    def shared(first, second):
        a, b, c = (jnp.sum(x) for x in split(first * second))
        return a / plane + b / (n_z * n_k) + c / (n_z * n_j)

    def tangent_of(full):
        hat_at, hat_bt, hat_ct = (x.astype(BF16) for x in split(full))
        hat_a, hat_c = hat_at.T.astype(F32), hat_ct.T.astype(F32)
        sideways = (hat_c[:, None, :] * wide_a[None] + wide_c[:, None, :] * hat_a[None]).astype(BF16)
        left = jnp.concatenate([paired, sideways.reshape(depth * height, rank)], axis=1)
        right = jnp.concatenate([hat_bt, bt], axis=0)
        return jnp.dot(left, right, preferred_element_type=F32)

    room = 32
    fitted = jnp.dot(paired, bt, preferred_element_type=F32)
    values = tensor.reshape(depth * height, width).astype(F32)
    errors = (weight * (values - fitted)).astype(BF16)
    gradient, _ = reduced(errors, jnp.zeros((room,), F32))

    tangent_g = tangent_of(gradient)
    weighted_g = weight * tangent_g
    mine = jnp.stack([shared(gradient, gradient), jnp.sum(weighted_g * tangent_g)])
    mine = jnp.pad(mine, (0, room - 2))
    product, totals = reduced(weighted_g.astype(BF16), mine)
    gg, gwg = totals[0], totals[1]
    alpha = gg / (gg + gwg)
    residual = gradient - alpha * (product + gradient)

    tangent_r = tangent_of(residual)
    weighted_r = weight * tangent_r
    mine = jnp.stack(
        [
            shared(residual, residual),
            shared(residual, gradient),
            jnp.sum(weighted_r * tangent_r),
            jnp.sum(weighted_r * tangent_g),
        ]
    )
    totals = jnp.sum(to_everyone(jnp.pad(mine, (0, 124))[None], EVERY), axis=0)[0]
    rr, rg, rwr, rwg = totals[0], totals[1], totals[2], totals[3]
    beta = rr / gg
    curve = (rwr + rr) + 2.0 * beta * (rwg + rg) + beta * beta * (gwg + gg)
    step = rr / curve
    result_a, result_b, result_c = split((alpha + step * beta) * gradient + step * residual)
    step_a = lax.dynamic_slice_in_dim(result_a, (jb * n_k + kb) * cols_a, cols_a, 0).T
    step_b = lax.dynamic_slice_in_dim(result_b, (z * n_k + kb) * cols_b, cols_b, 0).T
    step_c = lax.dynamic_slice_in_dim(result_c, (z * n_j + jb) * cols_c, cols_c, 0).T
    return step_a, step_b, step_c


def solution(mesh):
    torus = Mesh(mesh.devices.reshape(mesh.shape["ia"], 2, 2, 4, 2), EVERY)
    return jax.shard_map(
        local,
        mesh=torus,
        in_specs=(P(KA, "ia", JA), P(KA, "ia", JA), P("ia", PLANE), P(JA, IA_KA), P(KA, IA_JA)),
        out_specs=(P("ia", PLANE), P(JA, IA_KA), P(KA, IA_JA)),
        check_vma=False,
    )
```

time: 410 us -> 162 us (0.40)
  blocking collectives: 134 us -> 35.3 us
  waiting for transfers between devices: 131 us -> 52 us
  starting transfers between devices: 85.4 us -> 33.1 us
  local copies, waits for them, and re-layouts: 21.2 us -> 11.2 us
  matrix products: 9.04 us -> 3.98 us
    psum x15 -> x0, blocking collectives: 118 us -> none  [by_axis(): return functools.reduce(lax.psum, axes, x)]
    all_to_all x17 -> x5, waiting for transfers between devices: 131 us -> 52 us  [exchange(): return lax.all_to_all(blocks, axes, 0, 0, tiled=True)]
    all_to_all x17 -> x5, starting transfers between devices: 85.4 us -> 33.1 us  [exchange(): return lax.all_to_all(blocks, axes, 0, 0, tiled=True)]
    all_to_all x1 -> x3, blocking collectives: 15.3 us -> 35.3 us  [exchange(): return lax.all_to_all(blocks, axes, 0, 0, tiled=True)]
    dot_general x5 -> x0, local copies, waits for them, and re-layouts: 7.28 us -> none  [the longest x3 6.71 us: partials(): jnp.dot(weighted, full_b, preferred_element_type=jnp.float32)]
    unnamed x33 -> x7, local copies, waits for them, and re-layouts: 7.29 us -> 2.06 us
    dot_general x17 -> x7, matrix products: 9.04 us -> 3.98 us  [the longest x2 2.35 us: tangent_of(): return jnp.dot(left, right, preferred_element_type=F32)]
    all_to_all x6 -> x0, other arithmetic: 4.22 us -> none  [sent_and_summed(): blocks = lax.all_to_all(in_blocks(x, dim, count), axis, 0, 0, tiled=True)]
  transfers between devices with their start and end apart: 17 -> 5, of which waited for: 17 -> 5; matrix products, arithmetic and copies ran while one was open for 5% -> 1% of each run, Pallas kernels for 0% -> 0%
where the time goes in v1:
time: 162 us; the launch traced here: 161 us
  waiting for transfers between devices  52 us (32%)
  blocking collectives  35.3 us (22%)
  starting transfers between devices  33.1 us (20%)
  between operations  13.2 us (8%)
  other arithmetic  12.1 us (7%)
  local copies, waits for them, and re-layouts  11.2 us (7%)
  matrix products  3.98 us (2%)
    all_to_all x5, waiting for transfers between devices, exchange(): return lax.all_to_all(blocks, axes, 0, 0, tiled=True)  52 us
    all_to_all x3, blocking collectives, exchange(): return lax.all_to_all(blocks, axes, 0, 0, tiled=True)  35.3 us
    all_to_all x5, starting transfers between devices, exchange(): return lax.all_to_all(blocks, axes, 0, 0, tiled=True)  33.1 us
    reduce_sum x6, other arithmetic, shared(): a, b, c = (jnp.sum(x) for x in split(first * second))  3.99 us
  transfers between devices with their start and end apart: 5, of which 5 were waited for; matrix products, arithmetic and copies ran while one was open for 1% of the time, Pallas kernels for 0%

profile of v1, /device:TPU:1, one launch (start us, length us, event | category | flops | bytes accessed | tf_op | source)
XLA Modules:
  0.0 161.0 jit_solution(12407127654466421663)
XLA Ops:
  0.6 0.8 reshape.160
  1.4 0.8 reshape.162
  2.2 0.7 pad_maximum_fusion.12
  3.7 2.7 %reduce.15 = bf16[256,640]{1,0:T(8,128)(2,1)S(1)} reduce(bf16[256,1,640]{2,1,0:T(2,128)(2,1)S(1)} %broadcast_in_dim.30, bf16[]{:T(256)} %broadcast.67), dimensions={1}, to_apply=%broadcast_in_dim.30.reduce_sub_computation | reduce | bytes 655362 | tf_op jit(solution)/shard_map/broadcast_in_dim | solution.py:22
  6.4 1.1 reshape.200
  7.5 15.7 %all-to-all-start = ((bf16[256,2,320]{2,1,0:T(2,128)(2,1)}), bf16[256,2,320]{2,1,0:T(2,128)(2,1)S(1)}, u32[]{:S(2)}, u32[]{:S(2)}) async-start(bf16[256,2,320]{2,1,0:T(2,128)(2,1)} %reshape.200), calls=%async_computation | async-start | bytes 786432 | tf_op jit(solution)/shard_map/all_to_all | solution.py:17
  23.4 18.5 %all-to-all-done = bf16[256,2,320]{2,1,0:T(2,128)(2,1)S(1)} async-done(((bf16[256,2,320]{2,1,0:T(2,128)(2,1)}), bf16[256,2,320]{2,1,0:T(2,128)(2,1)S(1)}, u32[]{:S(2)}, u32[]{:S(2)}) %all-to-all-start) | async-done | bytes 327712 | tf_op jit(solution)/shard_map/all_to_all | solution.py:17
  44.7 11.3 %all_to_all.40 = f32[32,4,256]{2,1,0:T(4,128)S(1)} all-to-all(f32[32,4,256]{2,1,0:T(4,128)S(1)} %reshape.165), channel_id=1, replica_groups=mesh['ia'=8,'ja_0'=2,'ja_1'=2,'ka_0'=4,'ka_1'=2] {'ja_0','ja_1','ka_0','..., dimensions={0} | all-to-all | bytes 262144 | tf_op jit(solution)/shard_map/all_to_all | solution.py:17
  56.3 0.7 broadcast_in_dim.31
  57.0 3.4 %all-to-all-start.2 = ((f32[8,1,3104]{2,1,0:T(1,128)}), f32[8,1,3104]{2,1,0:T(1,128)S(1)}, u32[]{:S(2)}, u32[]{:S(2)}) async-start(f32[8,1,3104]{2,1,0:T(1,128)} %broadcast_in_dim.31), calls=%async_computation.2 | async-start | bytes 204800 | tf_op jit(solution)/shard_map/all_to_all | solution.py:17
  60.4 7.5 %all-to-all-done.2 = f32[8,1,3104]{2,1,0:T(1,128)S(1)} async-done(((f32[8,1,3104]{2,1,0:T(1,128)}), f32[8,1,3104]{2,1,0:T(1,128)S(1)}, u32[]{:S(2)}, u32[]{:S(2)}) %all-to-all-start.2) | async-done | bytes 99360 | tf_op jit(solution)/shard_map/all_to_all | solution.py:17
  68.3 12.6 %all_to_all.41 = f32[32,4,224]{2,1,0:T(4,128)S(1)} all-to-all(f32[32,4,224]{2,1,0:T(4,128)S(1)} %bitcast.104), channel_id=1, replica_groups=mesh['ia'=8,'ja_0'=2,'ja_1'=2,'ka_0'=4,'ka_1'=2] {'ja_0','ja_1','ka_0','..., dimensions={0} | all-to-all | bytes 229376 | tf_op jit(solution)/shard_map/all_to_all | solution.py:17
  80.9 0.7 slice_reduce_fusion.10
  82.2 0.6 slice_reduce_fusion.12
  85.2 1.2 multiply_reduce_fusion.2
  86.4 0.7 fusion.10
  88.1 11.4 %all_to_all.42 = f32[32,4,256]{2,1,0:T(4,128)S(1)} all-to-all(f32[32,4,256]{2,1,0:T(4,128)S(1)} %reshape.171), channel_id=1, replica_groups=mesh['ia'=8,'ja_0'=2,'ja_1'=2,'ka_0'=4,'ka_1'=2] {'ja_0','ja_1','ka_0','..., dimensions={0} | all-to-all | bytes 262144 | tf_op jit(solution)/shard_map/all_to_all | solution.py:17
  99.8 0.7 broadcast_in_dim.38
  100.5 3.4 %all-to-all-start.5 = ((f32[8,1,3104]{2,1,0:T(1,128)}), f32[8,1,3104]{2,1,0:T(1,128)S(1)}, u32[]{:S(2)}, u32[]{:S(2)}) async-start(f32[8,1,3104]{2,1,0:T(1,128)} %broadcast_in_dim.38), calls=%async_computation.5 | async-start | bytes 204800 | tf_op jit(solution)/shard_map/all_to_all | solution.py:17
  103.9 7.5 %all-to-all-done.5 = f32[8,1,3104]{2,1,0:T(1,128)S(1)} async-done(((f32[8,1,3104]{2,1,0:T(1,128)}), f32[8,1,3104]{2,1,0:T(1,128)S(1)}, u32[]{:S(2)}, u32[]{:S(2)}) %all-to-all-start.5) | async-done | bytes 99360 | tf_op jit(solution)/shard_map/all_to_all | solution.py:17
  111.7 0.7 pad_maximum_fusion.5
  112.5 5.3 %all-to-all-start.6 = ((f32[32,4,224]{2,1,0:T(4,128)}), f32[32,4,224]{2,1,0:T(4,128)S(1)}, u32[]{:S(2)}, u32[]{:S(2)}) async-start(f32[32,4,224]{2,1,0:T(4,128)} %bitcast.31), calls=%async_computation.6 | async-start | bytes 262144 | tf_op jit(solution)/shard_map/all_to_all | solution.py:17
  120.3 5.3 %all-to-all-done.6 = f32[32,4,224]{2,1,0:T(4,128)S(1)} async-done(((f32[32,4,224]{2,1,0:T(4,128)}), f32[32,4,224]{2,1,0:T(4,128)S(1)}, u32[]{:S(2)}, u32[]{:S(2)}) %all-to-all-start.6) | async-done | bytes 114720 | tf_op jit(solution)/shard_map/all_to_all | solution.py:17
  125.7 0.8 slice_reduce_fusion
  126.4 0.7 slice_reduce_fusion.1
  127.1 0.6 slice_reduce_fusion.2
  132.0 1.2 multiply_reduce_fusion.1
  133.2 1.4 select_maximum_fusion
  134.5 0.7 broadcast_in_dim.44
  135.2 5.4 %all-to-all-start.7 = ((f32[256,1,128]{2,1,0:T(1,128)}), f32[256,1,128]{2,1,0:T(1,128)S(1)}, u32[]{:S(2)}, u32[]{:S(2)}) async-start(f32[256,1,128]{2,1,0:T(1,128)} %broadcast_in_dim.44), calls=%async_computation.7 | async-start | bytes 262144 | tf_op jit(solution)/shard_map/all_to_all | solution.py:17
  140.7 13.3 %all-to-all-done.7 = f32[256,1,128]{2,1,0:T(1,128)S(1)} async-done(((f32[256,1,128]{2,1,0:T(1,128)}), f32[256,1,128]{2,1,0:T(1,128)S(1)}, u32[]{:S(2)}, u32[]{:S(2)}) %all-to-all-start.7) | async-done | bytes 131104 | tf_op jit(solution)/shard_map/all_to_all | solution.py:17
  154.0 0.7 fusion.19
  (90 shorter events, 10.0 us)
Async XLA Ops:
  3.7 19.5 %copy-start = (s32[32,64,128]{2,1,0:T(8,128)S(1)}, s32[32,64,128]{2,1,0:T(8,128)}, u32[]{:S(2)}) copy-start(s32[32,64,128]{2,1,0:T(8,128)} %param.6) | copy-start | bytes 3145732
  7.5 34.4 %all-to-all-start = ((bf16[256,2,320]{2,1,0:T(2,128)(2,1)}), bf16[256,2,320]{2,1,0:T(2,128)(2,1)S(1)}, u32[]{:S(2)}, u32[]{:S(2)}) async-start(bf16[256,2,320]{2,1,0:T(2,128)(2,1)} %reshape.200), calls=%async_computation | async-start | bytes 786432 | tf_op jit(solution)/shard_map/all_to_all | solution.py:17
  42.5 1.0 copy-start.1
  57.0 10.9 %all-to-all-start.2 = ((f32[8,1,3104]{2,1,0:T(1,128)}), f32[8,1,3104]{2,1,0:T(1,128)S(1)}, u32[]{:S(2)}, u32[]{:S(2)}) async-start(f32[8,1,3104]{2,1,0:T(1,128)} %broadcast_in_dim.31), calls=%async_computation.2 | async-start | bytes 204800 | tf_op jit(solution)/shard_map/all_to_all | solution.py:17
  100.5 10.9 %all-to-all-start.5 = ((f32[8,1,3104]{2,1,0:T(1,128)}), f32[8,1,3104]{2,1,0:T(1,128)S(1)}, u32[]{:S(2)}, u32[]{:S(2)}) async-start(f32[8,1,3104]{2,1,0:T(1,128)} %broadcast_in_dim.38), calls=%async_computation.5 | async-start | bytes 204800 | tf_op jit(solution)/shard_map/all_to_all | solution.py:17
  112.5 13.1 %all-to-all-start.6 = ((f32[32,4,224]{2,1,0:T(4,128)}), f32[32,4,224]{2,1,0:T(4,128)S(1)}, u32[]{:S(2)}, u32[]{:S(2)}) async-start(f32[32,4,224]{2,1,0:T(4,128)} %bitcast.31), calls=%async_computation.6 | async-start | bytes 262144 | tf_op jit(solution)/shard_map/all_to_all | solution.py:17
  135.2 18.7 %all-to-all-start.7 = ((f32[256,1,128]{2,1,0:T(1,128)}), f32[256,1,128]{2,1,0:T(1,128)S(1)}, u32[]{:S(2)}, u32[]{:S(2)}) async-start(f32[256,1,128]{2,1,0:T(1,128)} %broadcast_in_dim.44), calls=%async_computation.7 | async-start | bytes 262144 | tf_op jit(solution)/shard_map/all_to_all | solution.py:17

commit v2 on v1

v2 whole, which is shorter than its diff:
```python
import jax
import jax.numpy as jnp
from jax import lax
from jax.experimental import pallas as pl
from jax.experimental.pallas import tpu as pltpu
from jax.sharding import Mesh
from jax.sharding import PartitionSpec as P

JA = ("ja_0", "ja_1")
KA = ("ka_0", "ka_1")
PLANE = ("ja_0", "ja_1", "ka_0", "ka_1")
IA_KA = ("ia", "ka_0", "ka_1")
IA_JA = ("ia", "ja_0", "ja_1")
EVERY = ("ia", "ja_0", "ja_1", "ka_0", "ka_1")
F32, BF16 = jnp.float32, jnp.bfloat16
DEPTH, HEIGHT, WIDTH, RANK = 32, 64, 128, 128
CELLS = DEPTH * HEIGHT
N_Z, N_J, N_K = 8, 4, 8
EACH = 4
ROWS = EACH * HEIGHT
SCALE = 1.0 / 4096.0
AB = HEIGHT + WIDTH
BC = WIDTH + DEPTH


def exchange(blocks, axes):
    return lax.all_to_all(blocks, axes, 0, 0, tiled=True)


def across_ja(x):
    return [x] + [lax.ppermute(x, JA, [(i, i ^ m) for i in range(N_J)]) for m in (1, 2, 3)]


def call(kernel, outs, *operands, scratch=()):
    return pl.pallas_call(
        kernel,
        out_shape=[jax.ShapeDtypeStruct(shape, dtype) for shape, dtype in outs],
        in_specs=[
            pl.BlockSpec(memory_space=pltpu.SMEM if x.dtype == jnp.int32 and x.ndim == 1 else pltpu.VMEM)
            for x in operands
        ],
        out_specs=[pl.BlockSpec(memory_space=pltpu.VMEM) for _ in outs],
        scratch_shapes=[pltpu.VMEM(shape, dtype) for shape, dtype in scratch],
        compiler_params=pltpu.CompilerParams(vmem_limit_bytes=48 * 2**20),
    )(*operands)


def pack_kernel(a_ref, b_ref, c_ref, sent_ref, own_ref, wide):
    wide[...] = jnp.zeros_like(wide)
    wide[0:HEIGHT, 0:4] = a_ref[...].astype(F32)
    wide[HEIGHT : HEIGHT + DEPTH, 0:4] = c_ref[...].astype(F32)
    wide[128:256, 0:2] = b_ref[...].astype(F32)
    a_and_c = wide[0:128, :].T[0:4]
    b = wide[128:256, :].T[0:2]
    own_ref[0:4, :] = a_and_c
    own_ref[4:6, :] = b
    own_ref[6:8, :] = jnp.zeros((2, 128), F32)
    for peer in range(N_K):
        sent_ref[peer] = own_ref[...]


def repack_kernel(got_ref, c0, c1, c2, c3, sent_ref, a_ref, rows_a, rows_b, rows_c):
    for peer in range(N_K):
        rows_a[4 * peer : 4 * peer + 4, :] = got_ref[peer, 0:4, :]
        rows_b[2 * peer : 2 * peer + 2, :] = got_ref[peer, 4:6, :]
    for m, piece in enumerate((c0, c1, c2, c3)):
        rows_c[4 * m : 4 * m + 4, :] = piece[0:4, :]
    a_ref[...] = rows_a[...].astype(BF16)
    b, c = rows_b[...].astype(BF16), rows_c[...].astype(BF16)
    for peer in range(N_Z):
        sent_ref[peer, 0:16, :] = b
        sent_ref[peer, 16:32, :] = c


def xor_lanes(x, bit, on):
    lane = lax.broadcasted_iota(jnp.int32, x.shape, 1)
    swapped = jnp.where((lane & bit) != 0, pltpu.roll(x, bit, 1), pltpu.roll(x, 128 - bit, 1))
    return jnp.where(on != 0, swapped, x)


def in_pairs(k, a, c_ref):
    return jnp.concatenate([c_ref[pl.ds(k + s, 1), :] * a for s in range(EACH)], axis=0)


def weight_of(seen_ref, k):
    seen = seen_ref[pl.ds(k, EACH), :, :].reshape(ROWS, WIDTH)
    return seen.astype(F32) * SCALE


def add_products(k, weighted, paired, a, b, c_ref, part_a, part_b, part_c):
    part_b[...] += lax.dot_general(weighted, paired, (((0,), (0,)), ((), ())), preferred_element_type=F32)
    mixture = jnp.dot(weighted, b, preferred_element_type=F32)
    total = part_a[...]
    for s in range(EACH):
        slab = mixture[s * HEIGHT : (s + 1) * HEIGHT]
        total = total + slab * c_ref[pl.ds(k + s, 1), :]
        part_c[pl.ds(k + s, 1), :] = jnp.sum(slab * a, axis=0, keepdims=True)
    part_a[...] = total


def hand_out(part_a, part_b, part_c, sent_ref, c_out):
    a, b = part_a[...].astype(BF16), part_b[...].astype(BF16)
    for peer in range(N_K):
        sent_ref[peer, 0:HEIGHT, :] = a
        sent_ref[peer, HEIGHT:AB, :] = b
    c_out[...] = part_c[...].astype(BF16)


def first_kernel(place, got_ref, a0, a1, a2, a3, values_ref, seen_ref,
                 sent_ref, c_out, fa_ref, fb_ref, fbt_ref, fc_ref, part_a, part_b, part_c):
    a = jnp.concatenate([x[...].astype(F32) for x in (a0, a1, a2, a3)], axis=0).T[0:HEIGHT]
    a = xor_lanes(xor_lanes(a, 32, place[0] & 1), 64, place[0] & 2)
    c = jnp.concatenate([got_ref[z, 16:32, :].astype(F32) for z in range(N_Z)], axis=0).T[HEIGHT : HEIGHT + DEPTH]
    c = xor_lanes(xor_lanes(c, 4, place[0] & 1), 8, place[0] & 2)
    bt = jnp.concatenate([got_ref[z, 0:16, :].astype(F32) for z in range(N_Z)], axis=0)
    fbt_ref[...] = bt.astype(BF16)
    fb_ref[...] = bt.T.astype(BF16)
    fa_ref[...] = a
    fc_ref[...] = c
    part_a[...] = jnp.zeros_like(part_a)
    part_b[...] = jnp.zeros_like(part_b)

    @pl.loop(0, DEPTH, step=EACH)
    def _(k):
        a = fa_ref[...]
        paired = in_pairs(k, a, fc_ref).astype(BF16)
        fitted = jnp.dot(paired, fbt_ref[...], preferred_element_type=F32)
        values = values_ref[pl.ds(k, EACH), :, :].reshape(ROWS, WIDTH).astype(F32)
        errors = (weight_of(seen_ref, k) * (values - fitted)).astype(BF16)
        add_products(k, errors, paired, a, fb_ref[...], fc_ref, part_a, part_b, part_c)

    hand_out(part_a, part_b, part_c, sent_ref, c_out)


def middle_kernel(got_ref, c0, c1, c2, c3, sent_ref, a_ref):
    total = got_ref[0].astype(F32)
    for peer in range(1, N_K):
        total = total + got_ref[peer].astype(F32)
    a_ref[...] = total[0:HEIGHT].astype(BF16)
    b = total[HEIGHT:AB].astype(BF16)
    c = ((c0[...].astype(F32) + c1[...].astype(F32)) + (c2[...].astype(F32) + c3[...].astype(F32))).astype(BF16)
    for peer in range(N_Z):
        sent_ref[peer, 0:WIDTH, :] = b
        sent_ref[peer, WIDTH:BC, :] = c


def take_totals(got_ref, a0, a1, a2, a3, out):
    total = got_ref[0].astype(F32)
    for peer in range(1, N_Z):
        total = total + got_ref[peer].astype(F32)
    out[0:HEIGHT, :] = (a0[...].astype(F32) + a1[...].astype(F32)) + (a2[...].astype(F32) + a3[...].astype(F32))
    out[HEIGHT : HEIGHT + BC, :] = total


def tangent_at(k, paired, fa_ref, fc_ref, fbt_ref, hat_a, hat_bt, hat_c):
    sideways = (in_pairs(k, fa_ref[...], hat_c) + in_pairs(k, hat_a[...], fc_ref)).astype(BF16)
    return jnp.dot(paired, hat_bt[...], preferred_element_type=F32) + jnp.dot(
        sideways, fbt_ref[...], preferred_element_type=F32
    )


def round_hats(direction, hat_a, hat_bt, hat_c):
    hat_a[...] = direction[0:HEIGHT].astype(BF16).astype(F32)
    hat_bt[...] = direction[HEIGHT:AB].T.astype(BF16)
    hat_c[...] = direction[AB:].astype(BF16).astype(F32)


def second_kernel(got_ref, a0, a1, a2, a3, seen_ref, fa_ref, fb_ref, fbt_ref, fc_ref,
                  sent_ref, c_out, grad_ref, tangent_ref, sum_ref,
                  part_a, part_b, part_c, hat_a, hat_bt, hat_c):
    take_totals(got_ref, a0, a1, a2, a3, grad_ref)
    round_hats(grad_ref[...], hat_a, hat_bt, hat_c)
    part_a[...] = jnp.zeros_like(part_a)
    part_b[...] = jnp.zeros_like(part_b)
    sum_ref[...] = jnp.zeros_like(sum_ref)

    @pl.loop(0, DEPTH, step=EACH)
    def _(k):
        a = fa_ref[...]
        paired = in_pairs(k, a, fc_ref).astype(BF16)
        tangent = tangent_at(k, paired, fa_ref, fc_ref, fbt_ref, hat_a, hat_bt, hat_c)
        weighted = weight_of(seen_ref, k) * tangent
        tangent_ref[pl.ds(k * HEIGHT, ROWS), :] = tangent
        sum_ref[...] += jnp.sum((weighted * tangent).reshape(ROWS // 8, 8, WIDTH), axis=0)
        add_products(k, weighted.astype(BF16), paired, a, fb_ref[...], fc_ref, part_a, part_b, part_c)

    hand_out(part_a, part_b, part_c, sent_ref, c_out)


def total_of(x):
    return jnp.sum(jnp.sum(x, axis=0, keepdims=True), axis=1, keepdims=True)


def share_of(x):
    return (
        total_of(x[0:HEIGHT]) * (1.0 / (N_J * N_K))
        + total_of(x[HEIGHT:AB]) * (1.0 / (N_Z * N_K))
        + total_of(x[AB:]) * (1.0 / (N_Z * N_J))
    )


def third_kernel(got_ref, a0, a1, a2, a3, seen_ref, fa_ref, fbt_ref, fc_ref, grad_ref, tangent_ref, sum_ref,
                 sent_ref, rest_ref, hat_a, hat_bt, hat_c, sum_rest, sum_both):
    take_totals(got_ref, a0, a1, a2, a3, rest_ref)
    grad, product = grad_ref[...], rest_ref[...]
    length = share_of(grad * grad)
    level = jnp.where(length > 0.0, share_of(grad * product) / jnp.where(length > 0.0, length, 1.0), 0.0)
    rest = product - level * grad
    rest_ref[...] = rest
    round_hats(rest, hat_a, hat_bt, hat_c)
    sum_rest[...] = jnp.zeros_like(sum_rest)
    sum_both[...] = jnp.zeros_like(sum_both)

    @pl.loop(0, DEPTH, step=EACH)
    def _(k):
        paired = in_pairs(k, fa_ref[...], fc_ref).astype(BF16)
        tangent = tangent_at(k, paired, fa_ref, fc_ref, fbt_ref, hat_a, hat_bt, hat_c)
        weighted = weight_of(seen_ref, k) * tangent
        before = tangent_ref[pl.ds(k * HEIGHT, ROWS), :]
        sum_rest[...] += jnp.sum((weighted * tangent).reshape(ROWS // 8, 8, WIDTH), axis=0)
        sum_both[...] += jnp.sum((weighted * before).reshape(ROWS // 8, 8, WIDTH), axis=0)

    lane = lax.broadcasted_iota(jnp.int32, (1, 128), 1)
    line = jnp.zeros((1, 128), F32)
    for place, value in enumerate(
        (
            level,
            length,
            share_of(grad * rest),
            share_of(rest * rest),
            total_of(sum_ref[...]),
            total_of(sum_both[...]),
            total_of(sum_rest[...]),
        )
    ):
        line = jnp.where(lane == place, value, line)
    for peer in range(N_Z * N_J * N_K):
        sent_ref[peer] = line


def last_kernel(place, got_ref, own_ref, grad_ref, rest_ref, a_ref, b_ref, c_ref):
    table = got_ref[:, 0, :].T
    level, gg, gv, vv, s_gg, s_gv, s_vv = (table[i : i + 1] for i in range(7))

    def add(x):
        return jnp.sum(x, axis=1, keepdims=True)

    norm = add(gg)
    alpha = norm / (norm + add(s_gg))
    near = 1.0 - alpha * (1.0 + level)
    rr = add(near * near * gg - 2.0 * alpha * near * gv + alpha * alpha * vv)
    rg = add(near * gg - alpha * gv)
    s_rr = add(near * near * s_gg - 2.0 * alpha * near * s_gv + alpha * alpha * s_vv)
    s_rg = add(near * s_gg - alpha * s_gv)
    beta = rr / norm
    curve = (s_rr + rr) + 2.0 * beta * (s_rg + rg) + beta * beta * (add(s_gg) + norm)
    step = rr / curve
    own_level = own_ref[0, :, 0:1]
    own_near = 1.0 - alpha * (1.0 + own_level)
    x = (alpha + step * (own_near + beta)) * grad_ref[...] - (step * alpha) * rest_ref[...]
    z, jb, kb = place[1], place[0], place[2]
    a_ref[...] = pltpu.roll(x[0:HEIGHT], (128 - (jb * N_K + kb) * 4) % 128, 1)[:, 0:4]
    b_ref[...] = pltpu.roll(x[HEIGHT:AB], (128 - (z * N_K + kb) * 2) % 128, 1)[:, 0:2]
    c_ref[...] = pltpu.roll(x[AB:], (128 - (z * N_J + jb) * 4) % 128, 1)[:, 0:4]


def local(tensor, observed, factor_a, factor_b, factor_c):
    z, jb, kb = lax.axis_index("ia"), lax.axis_index(JA), lax.axis_index(KA)
    place = jnp.stack([jb, z, kb]).astype(jnp.int32)
    tile = lambda rows: ((rows, RANK), F32)
    sums = [tile(HEIGHT), tile(WIDTH), tile(DEPTH)]
    hats = [tile(HEIGHT), ((RANK, WIDTH), BF16), tile(DEPTH)]

    sent, own = call(
        pack_kernel, [((N_K, 8, 128), F32), ((8, 128), F32)], factor_a, factor_b, factor_c, scratch=[tile(256)]
    )
    got = exchange(sent, KA)
    sent, own = call(
        repack_kernel, [((N_Z, 32, 128), BF16), ((32, 128), BF16)], got, *across_ja(own),
        scratch=[tile(32), tile(16), tile(16)],
    )
    got = exchange(sent, "ia")

    sent_types = [((N_K, AB, RANK), BF16), ((DEPTH, RANK), BF16)]
    sent, part_c, fa, fb, fbt, fc = call(
        first_kernel,
        sent_types + [tile(HEIGHT), ((WIDTH, RANK), BF16), ((RANK, WIDTH), BF16), tile(DEPTH)],
        place, got, *across_ja(own), tensor, observed, scratch=sums,
    )

    def summed(sent, part_c):
        got = exchange(sent, KA)
        sent, part_a = call(
            middle_kernel, [((N_Z, BC, RANK), BF16), ((HEIGHT, RANK), BF16)], got, *across_ja(part_c)
        )
        return exchange(sent, "ia"), *across_ja(part_a)

    sent, part_c, grad, tangent, sum_gg = call(
        second_kernel,
        sent_types + [tile(AB + DEPTH), tile(CELLS), tile(8)],
        *summed(sent, part_c), observed, fa, fb, fbt, fc, scratch=sums + hats,
    )
    sent, rest = call(
        third_kernel,
        [((N_Z * N_J * N_K, 1, 128), F32), tile(AB + DEPTH)],
        *summed(sent, part_c), observed, fa, fbt, fc, grad, tangent, sum_gg, scratch=hats + [tile(8), tile(8)],
    )
    got = exchange(sent, EVERY)
    return tuple(
        call(
            last_kernel,
            [((HEIGHT, 4), F32), ((WIDTH, 2), F32), ((DEPTH, 4), F32)],
            place, got, sent[0:1], grad, rest,
        )
    )


def solution(mesh):
    torus = Mesh(mesh.devices.reshape(N_Z, 2, 2, 4, 2), EVERY)
    return jax.shard_map(
        local,
        mesh=torus,
        in_specs=(P(KA, "ia", JA), P(KA, "ia", JA), P("ia", PLANE), P(JA, IA_KA), P(KA, IA_JA)),
        out_specs=(P("ia", PLANE), P(JA, IA_KA), P(KA, IA_JA)),
        check_vma=False,
    )
```

time: 162 us -> 132 us (0.81)
  starting transfers between devices: 33.1 us -> 71.4 us
  blocking collectives: 35.3 us -> 0 us
  Pallas kernels: 0 us -> 15.2 us
  waiting for transfers between devices: 52 us -> 37.9 us
  between operations: 13.2 us -> 0.7 us
  other arithmetic: 12.1 us -> 0.08 us
  local copies, waits for them, and re-layouts: 11.2 us -> 6.4 us
  matrix products: 3.98 us -> 0 us
    all_to_all x3 -> x0, blocking collectives: 35.3 us -> none  [exchange(): return lax.all_to_all(blocks, axes, 0, 0, tiled=True)]
    all_to_all x5 -> x7, waiting for transfers between devices: 52 us -> 18.7 us  [exchange(): return lax.all_to_all(blocks, axes, 0, 0, tiled=True)]
    ppermute x0 -> x18, starting transfers between devices: none -> 27.7 us  [across_ja(): lax.ppermute(x, JA, [(i, i ^ m) for i in range(N_J)])]
    ppermute x0 -> x18, waiting for transfers between devices: none -> 19.2 us  [across_ja(): lax.ppermute(x, JA, [(i, i ^ m) for i in range(N_J)])]
    pallas_call x0 -> x8, Pallas kernels: none -> 15.2 us  [call(): pl.pallas_call(kernel, out_shape=[jax.ShapeDtypeStruct(shape, dtype) for...]
    all_to_all x5 -> x7, starting transfers between devices: 33.1 us -> 43.7 us  [exchange(): return lax.all_to_all(blocks, axes, 0, 0, tiled=True)]
    reduce_sum x15 -> x0, other arithmetic: 4.62 us -> none  [the longest x6 3.99 us: shared(): a, b, c = (jnp.sum(x) for x in split(first * second))]
    dot_general x7 -> x0, matrix products: 3.98 us -> none  [the longest x2 2.35 us: tangent_of(): return jnp.dot(left, right, preferred_element_type=F32)]
  transfers between devices with their start and end apart: 5 -> 25, of which waited for: 5 -> 16; matrix products, arithmetic and copies ran while one was open for 1% -> 1% of each run, Pallas kernels for 0% -> 0%
where the time goes in v2:
time: 132 us
  starting transfers between devices  71.4 us (54%)
  waiting for transfers between devices  37.9 us (29%)
  Pallas kernels  15.2 us (12%)
  local copies, waits for them, and re-layouts  6.4 us (5%)
    all_to_all x7, starting transfers between devices, exchange(): return lax.all_to_all(blocks, axes, 0, 0, tiled=True)  43.7 us
    ppermute x18, starting transfers between devices, across_ja(): lax.ppermute(x, JA, [(i, i ^ m) for i in range(N_J)])  27.7 us
    ppermute x18, waiting for transfers between devices, across_ja(): lax.ppermute(x, JA, [(i, i ^ m) for i in range(N_J)])  19.2 us
    all_to_all x7, waiting for transfers between devices, exchange(): return lax.all_to_all(blocks, axes, 0, 0, tiled=True)  18.7 us
    pallas_call x8, Pallas kernels, call(): pl.pallas_call(kernel, out_shape=[jax.ShapeDtypeStruct(shape, dtype) for...  15.2 us
    unnamed x13, local copies, waits for them, and re-layouts  3.84 us
  transfers between devices with their start and end apart: 25, of which 16 were waited for; matrix products, arithmetic and copies ran while one was open for 1% of the time, Pallas kernels for 0%

profile of v2, /device:TPU:1, one launch (start us, length us, event | category | flops | bytes accessed | tf_op | source)
XLA Modules:
  0.0 131.7 jit_solution(17881282357569932796)
XLA Ops:
  2.9 5.9 %all-to-all-start = ((f32[8,8,128]{2,1,0:T(8,128)}), f32[8,8,128]{2,1,0:T(8,128)S(1)}, u32[]{:S(2)}, u32[]{:S(2)}) async-start(f32[8,8,128]{2,1,0:T(8,128)} %get-tuple-element.24), calls=%async_computation | async-start | bytes 65536 | tf_op jit(solution)/shard_map/all_to_all | solution.py:27
  8.9 3.3 %collective-permute-start.2 = (f32[8,128]{1,0:T(8,128)S(1)}, f32[8,128]{1,0:T(8,128)S(1)}, u32[]{:S(2)}, u32[]{:S(2)}) collective-permute-start(f32[8,128]{1,0:T(8,128)S(1)} %get-tuple-element.25.c0), channel_id=1, source_target_pairs={{0,24},{8,16},{16,8},{24,0},{1,25},{9,17},{17,9},{25,1},{2,26},{10... | collective-permute-start | bytes 12296 | tf_op jit(solution)/shard_map/ppermute | solution.py:31
  12.7 1.3 %collective-permute-done.2.c3 = f32[8,128]{1,0:T(8,128)S(1)} collective-permute-done((f32[8,128]{1,0:T(8,128)S(1)}, f32[8,128]{1,0:T(8,128)S(1)}, u32[]{:S(2)}, u32[]{:S(2)}) %collective-permute-start.2) | collective-permute-done | bytes 4128 | tf_op jit(solution)/shard_map/ppermute | solution.py:31
  14.0 2.4 %collective-permute-done.1.c2 = f32[8,128]{1,0:T(8,128)S(1)} collective-permute-done((f32[8,128]{1,0:T(8,128)S(1)}, f32[8,128]{1,0:T(8,128)S(1)}, u32[]{:S(2)}, u32[]{:S(2)}) %collective-permute-start.1) | collective-permute-done | bytes 4128 | tf_op jit(solution)/shard_map/ppermute | solution.py:31
  17.1 8.2 %all-to-all-start.1 = ((bf16[8,32,128]{2,1,0:T(8,128)(2,1)}), bf16[8,32,128]{2,1,0:T(8,128)(2,1)S(1)}, u32[]{:S(2)}, u32[]{:S(2)}) async-start(bf16[8,32,128]{2,1,0:T(8,128)(2,1)} %get-tuple-element.26), calls=%async_computation.1 | async-start | bytes 131072 | tf_op jit(solution)/shard_map/all_to_all | solution.py:27
  25.3 2.2 %collective-permute-start.5 = (bf16[32,128]{1,0:T(8,128)(2,1)S(1)}, bf16[32,128]{1,0:T(8,128)(2,1)S(1)}, u32[]{:S(2)}, u32[]{:S(2)}) collective-permute-start(bf16[32,128]{1,0:T(8,128)(2,1)S(1)} %get-tuple-element.27.a0), channel_id=1, source_target_pairs={{0,24},{8,16},{16,8},{24,0},{1,25},{9,17},{17,9},{25,1},{2,26},{10... | collective-permute-start | bytes 24584 | tf_op jit(solution)/shard_map/ppermute | solution.py:31
  27.5 1.3 collective-permute-start.4
  29.0 1.2 collective-permute-done.5.a3
  30.2 1.4 %collective-permute-done.4.a2 = bf16[32,128]{1,0:T(8,128)(2,1)S(1)} collective-permute-done((bf16[32,128]{1,0:T(8,128)(2,1)S(1)}, bf16[32,128]{1,0:T(8,128)(2,1)S(1)}, u32[]{:S(2)}, u32[]{:S(2)}) %collective-permute-start.4) | collective-permute-done | bytes 8224 | tf_op jit(solution)/shard_map/ppermute | solution.py:31
  32.5 1.2 copy-done
  34.8 4.4 %shard_map.78 = (bf16[8,192,128]{2,1,0:T(8,128)(2,1)}, bf16[32,128]{1,0:T(8,128)(2,1)S(1)}, f32[64,128]{1,0:T(8,128)S(1)}, bf16[128,128]{1,0:T(8,128)(2,1)S(1)},...) custom-call(s32[3]{0:T(128)S(1)} %pad_add_fusion.place, bf16[8,32,128]{2,1,0:T(8,128)(2,1)S(1)} %all-to-all-done.1.got_ref, ...), custom_call_target="tpu_custom_call" | custom-call | tf_op jit(solution)/shard_map/pallas_call | solution.py:35
  39.2 4.7 %all-to-all-start.2 = ((bf16[8,192,128]{2,1,0:T(8,128)(2,1)}), bf16[8,192,128]{2,1,0:T(8,128)(2,1)S(1)}, u32[]{:S(2)}, u32[]{:S(2)}) async-start(bf16[8,192,128]{2,1,0:T(8,128)(2,1)} %get-tuple-element.28), calls=%async_computation.2 | async-start | bytes 786432 | tf_op jit(solution)/shard_map/all_to_all | solution.py:27
  43.9 3.7 %collective-permute-start.8 = (bf16[32,128]{1,0:T(8,128)(2,1)S(1)}, bf16[32,128]{1,0:T(8,128)(2,1)S(1)}, u32[]{:S(2)}, u32[]{:S(2)}) collective-permute-start(bf16[32,128]{1,0:T(8,128)(2,1)S(1)} %get-tuple-element.29.c0), channel_id=1, source_target_pairs={{0,24},{8,16},{16,8},{24,0},{1,25},{9,17},{17,9},{25,1},{2,26},{10... | collective-permute-start | bytes 24584 | tf_op jit(solution)/shard_map/ppermute | solution.py:31
  47.6 1.2 collective-permute-start.7
  48.8 2.5 %collective-permute-done.8.c3 = bf16[32,128]{1,0:T(8,128)(2,1)S(1)} collective-permute-done((bf16[32,128]{1,0:T(8,128)(2,1)S(1)}, bf16[32,128]{1,0:T(8,128)(2,1)S(1)}, u32[]{:S(2)}, u32[]{:S(2)}) %collective-permute-start.8) | collective-permute-done | bytes 8224 | tf_op jit(solution)/shard_map/ppermute | solution.py:31
  52.6 6.1 %all-to-all-start.3 = ((bf16[8,160,128]{2,1,0:T(8,128)(2,1)}), bf16[8,160,128]{2,1,0:T(8,128)(2,1)S(1)}, u32[]{:S(2)}, u32[]{:S(2)}) async-start(bf16[8,160,128]{2,1,0:T(8,128)(2,1)} %get-tuple-element.30), calls=%async_computation.3 | async-start | bytes 655360 | tf_op jit(solution)/shard_map/all_to_all | solution.py:27
  58.8 4.0 %collective-permute-start.11 = (bf16[64,128]{1,0:T(8,128)(2,1)S(1)}, bf16[64,128]{1,0:T(8,128)(2,1)S(1)}, u32[]{:S(2)}, u32[]{:S(2)}) collective-permute-start(bf16[64,128]{1,0:T(8,128)(2,1)S(1)} %get-tuple-element.31.a0), channel_id=1, source_target_pairs={{0,24},{8,16},{16,8},{24,0},{1,25},{9,17},{17,9},{25,1},{2,26},{10... | collective-permute-start | bytes 49160 | tf_op jit(solution)/shard_map/ppermute | solution.py:31
  64.2 3.0 %collective-permute-done.10.a2 = bf16[64,128]{1,0:T(8,128)(2,1)S(1)} collective-permute-done((bf16[64,128]{1,0:T(8,128)(2,1)S(1)}, bf16[64,128]{1,0:T(8,128)(2,1)S(1)}, u32[]{:S(2)}, u32[]{:S(2)}) %collective-permute-start.10) | collective-permute-done | bytes 16416 | tf_op jit(solution)/shard_map/ppermute | solution.py:31
  67.2 2.7 %all-to-all-done.3.got_ref = bf16[8,160,128]{2,1,0:T(8,128)(2,1)S(1)} async-done(((bf16[8,160,128]{2,1,0:T(8,128)(2,1)}), bf16[8,160,128]{2,1,0:T(8,128)(2,1)S(1)}, u32[]{:S(2)}, u32[]{:S(2)}) %all-to-all-start.3) | async-done | bytes 327712 | tf_op jit(solution)/shard_map/all_to_all | solution.py:27
  69.9 4.4 %shard_map.80 = (bf16[8,192,128]{2,1,0:T(8,128)(2,1)}, bf16[32,128]{1,0:T(8,128)(2,1)S(1)}, f32[224,128]{1,0:T(8,128)S(1)}, f32[2048,128]{1,0:T(8,128)S(1)}, f32[8,128]{1,0:T(8,128)S(1)}) custom-call(bf16[8,160,128]{2,1,0:T(8,128)(2,1)S(1)} %all-to-all-done.3.got_ref, bf16[64,128]{1,0:T(8,128)(2,1)S(1)} %get-tuple-element.31.a0, ...), custom_call_target="tpu_custom_call" | custom-call | tf_op jit(solution)/shard_map/pallas_call | solution.py:35
  74.2 4.9 %all-to-all-start.4 = ((bf16[8,192,128]{2,1,0:T(8,128)(2,1)}), bf16[8,192,128]{2,1,0:T(8,128)(2,1)S(1)}, u32[]{:S(2)}, u32[]{:S(2)}) async-start(bf16[8,192,128]{2,1,0:T(8,128)(2,1)} %get-tuple-element.36), calls=%async_computation.4 | async-start | bytes 786432 | tf_op jit(solution)/shard_map/all_to_all | solution.py:27
  79.1 4.4 %collective-permute-start.14 = (bf16[32,128]{1,0:T(8,128)(2,1)S(1)}, bf16[32,128]{1,0:T(8,128)(2,1)S(1)}, u32[]{:S(2)}, u32[]{:S(2)}) collective-permute-start(bf16[32,128]{1,0:T(8,128)(2,1)S(1)} %get-tuple-element.37.c0), channel_id=1, source_target_pairs={{0,24},{8,16},{16,8},{24,0},{1,25},{9,17},{17,9},{25,1},{2,26},{10... | collective-permute-start | bytes 24584 | tf_op jit(solution)/shard_map/ppermute | solution.py:31
  83.5 1.2 collective-permute-start.13
  84.8 2.8 %collective-permute-done.14.c3 = bf16[32,128]{1,0:T(8,128)(2,1)S(1)} collective-permute-done((bf16[32,128]{1,0:T(8,128)(2,1)S(1)}, bf16[32,128]{1,0:T(8,128)(2,1)S(1)}, u32[]{:S(2)}, u32[]{:S(2)}) %collective-permute-start.14) | collective-permute-done | bytes 8224 | tf_op jit(solution)/shard_map/ppermute | solution.py:31
  88.6 3.4 %all-to-all-start.5 = ((bf16[8,160,128]{2,1,0:T(8,128)(2,1)}), bf16[8,160,128]{2,1,0:T(8,128)(2,1)S(1)}, u32[]{:S(2)}, u32[]{:S(2)}) async-start(bf16[8,160,128]{2,1,0:T(8,128)(2,1)} %get-tuple-element.38), calls=%async_computation.5 | async-start | bytes 655360 | tf_op jit(solution)/shard_map/all_to_all | solution.py:27
  92.0 3.9 %collective-permute-start.17 = (bf16[64,128]{1,0:T(8,128)(2,1)S(1)}, bf16[64,128]{1,0:T(8,128)(2,1)S(1)}, u32[]{:S(2)}, u32[]{:S(2)}) collective-permute-start(bf16[64,128]{1,0:T(8,128)(2,1)S(1)} %get-tuple-element.39.a0), channel_id=1, source_target_pairs={{0,24},{8,16},{16,8},{24,0},{1,25},{9,17},{17,9},{25,1},{2,26},{10... | collective-permute-start | bytes 49160 | tf_op jit(solution)/shard_map/ppermute | solution.py:31
  95.9 1.2 collective-permute-start.16
  97.3 2.7 %collective-permute-done.16.a2 = bf16[64,128]{1,0:T(8,128)(2,1)S(1)} collective-permute-done((bf16[64,128]{1,0:T(8,128)(2,1)S(1)}, bf16[64,128]{1,0:T(8,128)(2,1)S(1)}, u32[]{:S(2)}, u32[]{:S(2)}) %collective-permute-start.16) | collective-permute-done | bytes 16416 | tf_op jit(solution)/shard_map/ppermute | solution.py:31
  100.0 2.5 %all-to-all-done.5.got_ref = bf16[8,160,128]{2,1,0:T(8,128)(2,1)S(1)} async-done(((bf16[8,160,128]{2,1,0:T(8,128)(2,1)}), bf16[8,160,128]{2,1,0:T(8,128)(2,1)S(1)}, u32[]{:S(2)}, u32[]{:S(2)}) %all-to-all-start.5) | async-done | bytes 327712 | tf_op jit(solution)/shard_map/all_to_all | solution.py:27
  102.5 2.5 %shard_map.82 = (f32[256,1,128]{2,1,0:T(1,128)}, f32[224,128]{1,0:T(8,128)S(1)}) custom-call(bf16[8,160,128]{2,1,0:T(8,128)(2,1)S(1)} %all-to-all-done.5.got_ref, bf16[64,128]{1,0:T(8,128)(2,1)S(1)} %get-tuple-element.39.a0, bf16[64,128]{1,0:T(8,128)(2,1)S(1)} %collective-permute-done.15.a1, bf16[64,128]{1,0:T(8,128)(2,1)S(1)} %collective-permute-done.16.a2, ...), custom_call_target="tpu_custom_call" | custom-call | tf_op jit(solution)/shard_map/pallas_call | solution.py:35
  105.1 10.5 %all-to-all-start.6 = ((f32[256,1,128]{2,1,0:T(1,128)}), f32[256,1,128]{2,1,0:T(1,128)S(1)}, u32[]{:S(2)}, u32[]{:S(2)}) async-start(f32[256,1,128]{2,1,0:T(1,128)} %get-tuple-element.43), calls=%async_computation.6 | async-start | bytes 262144 | tf_op jit(solution)/shard_map/all_to_all | solution.py:27
  116.1 12.6 %all-to-all-done.6.got_ref = f32[256,1,128]{2,1,0:T(1,128)S(1)} async-done(((f32[256,1,128]{2,1,0:T(1,128)}), f32[256,1,128]{2,1,0:T(1,128)S(1)}, u32[]{:S(2)}, u32[]{:S(2)}) %all-to-all-start.6) | async-done | bytes 131104 | tf_op jit(solution)/shard_map/all_to_all | solution.py:27
  (44 shorter events, 13.1 us)
Async XLA Ops:
  0.6 0.8 copy-start.3
  1.4 0.7 copy-start.4
  2.9 13.5 %all-to-all-start = ((f32[8,8,128]{2,1,0:T(8,128)}), f32[8,8,128]{2,1,0:T(8,128)S(1)}, u32[]{:S(2)}, u32[]{:S(2)}) async-start(f32[8,8,128]{2,1,0:T(8,128)} %get-tuple-element.24), calls=%async_computation | async-start | bytes 65536 | tf_op jit(solution)/shard_map/all_to_all | solution.py:27
  8.9 5.1 %collective-permute-start.2 = (f32[8,128]{1,0:T(8,128)S(1)}, f32[8,128]{1,0:T(8,128)S(1)}, u32[]{:S(2)}, u32[]{:S(2)}) collective-permute-start(f32[8,128]{1,0:T(8,128)S(1)} %get-tuple-element.25.c0), channel_id=1, source_target_pairs={{0,24},{8,16},{16,8},{24,0},{1,25},{9,17},{17,9},{25,1},{2,26},{10... | collective-permute-start | bytes 12296 | tf_op jit(solution)/shard_map/ppermute | solution.py:31
  12.2 4.3 %collective-permute-start.1 = (f32[8,128]{1,0:T(8,128)S(1)}, f32[8,128]{1,0:T(8,128)S(1)}, u32[]{:S(2)}, u32[]{:S(2)}) collective-permute-start(f32[8,128]{1,0:T(8,128)S(1)} %get-tuple-element.25.c0), channel_id=1, source_target_pairs={{0,16},{8,24},{16,0},{24,8},{1,17},{9,25},{17,1},{25,9},{2,18},{10... | collective-permute-start | bytes 12296 | tf_op jit(solution)/shard_map/ppermute | solution.py:31
  12.7 3.8 %collective-permute-start = (f32[8,128]{1,0:T(8,128)S(1)}, f32[8,128]{1,0:T(8,128)S(1)}, u32[]{:S(2)}, u32[]{:S(2)}) collective-permute-start(f32[8,128]{1,0:T(8,128)S(1)} %get-tuple-element.25.c0), channel_id=1, source_target_pairs={{0,8},{8,0},{16,24},{24,16},{1,9},{9,1},{17,25},{25,17},{2,10},{10... | collective-permute-start | bytes 12296 | tf_op jit(solution)/shard_map/ppermute | solution.py:31
  17.1 15.4 %all-to-all-start.1 = ((bf16[8,32,128]{2,1,0:T(8,128)(2,1)}), bf16[8,32,128]{2,1,0:T(8,128)(2,1)S(1)}, u32[]{:S(2)}, u32[]{:S(2)}) async-start(bf16[8,32,128]{2,1,0:T(8,128)(2,1)} %get-tuple-element.26), calls=%async_computation.1 | async-start | bytes 131072 | tf_op jit(solution)/shard_map/all_to_all | solution.py:27
  25.3 5.0 %collective-permute-start.5 = (bf16[32,128]{1,0:T(8,128)(2,1)S(1)}, bf16[32,128]{1,0:T(8,128)(2,1)S(1)}, u32[]{:S(2)}, u32[]{:S(2)}) collective-permute-start(bf16[32,128]{1,0:T(8,128)(2,1)S(1)} %get-tuple-element.27.a0), channel_id=1, source_target_pairs={{0,24},{8,16},{16,8},{24,0},{1,25},{9,17},{17,9},{25,1},{2,26},{10... | collective-permute-start | bytes 24584 | tf_op jit(solution)/shard_map/ppermute | solution.py:31
  27.5 4.1 %collective-permute-start.4 = (bf16[32,128]{1,0:T(8,128)(2,1)S(1)}, bf16[32,128]{1,0:T(8,128)(2,1)S(1)}, u32[]{:S(2)}, u32[]{:S(2)}) collective-permute-start(bf16[32,128]{1,0:T(8,128)(2,1)S(1)} %get-tuple-element.27.a0), channel_id=1, source_target_pairs={{0,16},{8,24},{16,0},{24,8},{1,17},{9,25},{17,1},{25,9},{2,18},{10... | collective-permute-start | bytes 24584 | tf_op jit(solution)/shard_map/ppermute | solution.py:31
  28.8 2.8 %collective-permute-start.3 = (bf16[32,128]{1,0:T(8,128)(2,1)S(1)}, bf16[32,128]{1,0:T(8,128)(2,1)S(1)}, u32[]{:S(2)}, u32[]{:S(2)}) collective-permute-start(bf16[32,128]{1,0:T(8,128)(2,1)S(1)} %get-tuple-element.27.a0), channel_id=1, source_target_pairs={{0,8},{8,0},{16,24},{24,16},{1,9},{9,1},{17,25},{25,17},{2,10},{10... | collective-permute-start | bytes 24584 | tf_op jit(solution)/shard_map/ppermute | solution.py:31
  32.5 1.2 copy-start
  33.8 1.0 copy-start.2
  39.2 30.7 %copy-start.1 = (s32[32,64,128]{2,1,0:T(8,128)S(1)}, s32[32,64,128]{2,1,0:T(8,128)}, u32[]{:S(2)}) copy-start(s32[32,64,128]{2,1,0:T(8,128)} %seen_ref.5) | copy-start | bytes 3145732
  39.2 12.7 %all-to-all-start.2 = ((bf16[8,192,128]{2,1,0:T(8,128)(2,1)}), bf16[8,192,128]{2,1,0:T(8,128)(2,1)S(1)}, u32[]{:S(2)}, u32[]{:S(2)}) async-start(bf16[8,192,128]{2,1,0:T(8,128)(2,1)} %get-tuple-element.28), calls=%async_computation.2 | async-start | bytes 786432 | tf_op jit(solution)/shard_map/all_to_all | solution.py:27
  43.9 7.4 %collective-permute-start.8 = (bf16[32,128]{1,0:T(8,128)(2,1)S(1)}, bf16[32,128]{1,0:T(8,128)(2,1)S(1)}, u32[]{:S(2)}, u32[]{:S(2)}) collective-permute-start(bf16[32,128]{1,0:T(8,128)(2,1)S(1)} %get-tuple-element.29.c0), channel_id=1, source_target_pairs={{0,24},{8,16},{16,8},{24,0},{1,25},{9,17},{17,9},{25,1},{2,26},{10... | collective-permute-start | bytes 24584 | tf_op jit(solution)/shard_map/ppermute | solution.py:31
  47.6 4.3 %collective-permute-start.7 = (bf16[32,128]{1,0:T(8,128)(2,1)S(1)}, bf16[32,128]{1,0:T(8,128)(2,1)S(1)}, u32[]{:S(2)}, u32[]{:S(2)}) collective-permute-start(bf16[32,128]{1,0:T(8,128)(2,1)S(1)} %get-tuple-element.29.c0), channel_id=1, source_target_pairs={{0,16},{8,24},{16,0},{24,8},{1,17},{9,25},{17,1},{25,9},{2,18},{10... | collective-permute-start | bytes 24584 | tf_op jit(solution)/shard_map/ppermute | solution.py:31
  48.8 3.1 %collective-permute-start.6 = (bf16[32,128]{1,0:T(8,128)(2,1)S(1)}, bf16[32,128]{1,0:T(8,128)(2,1)S(1)}, u32[]{:S(2)}, u32[]{:S(2)}) collective-permute-start(bf16[32,128]{1,0:T(8,128)(2,1)S(1)} %get-tuple-element.29.c0), channel_id=1, source_target_pairs={{0,8},{8,0},{16,24},{24,16},{1,9},{9,1},{17,25},{25,17},{2,10},{10... | collective-permute-start | bytes 24584 | tf_op jit(solution)/shard_map/ppermute | solution.py:31
  52.6 17.2 %all-to-all-start.3 = ((bf16[8,160,128]{2,1,0:T(8,128)(2,1)}), bf16[8,160,128]{2,1,0:T(8,128)(2,1)S(1)}, u32[]{:S(2)}, u32[]{:S(2)}) async-start(bf16[8,160,128]{2,1,0:T(8,128)(2,1)} %get-tuple-element.30), calls=%async_computation.3 | async-start | bytes 655360 | tf_op jit(solution)/shard_map/all_to_all | solution.py:27
  58.8 5.5 %collective-permute-start.11 = (bf16[64,128]{1,0:T(8,128)(2,1)S(1)}, bf16[64,128]{1,0:T(8,128)(2,1)S(1)}, u32[]{:S(2)}, u32[]{:S(2)}) collective-permute-start(bf16[64,128]{1,0:T(8,128)(2,1)S(1)} %get-tuple-element.31.a0), channel_id=1, source_target_pairs={{0,24},{8,16},{16,8},{24,0},{1,25},{9,17},{17,9},{25,1},{2,26},{10... | collective-permute-start | bytes 49160 | tf_op jit(solution)/shard_map/ppermute | solution.py:31
  62.8 4.4 %collective-permute-start.10 = (bf16[64,128]{1,0:T(8,128)(2,1)S(1)}, bf16[64,128]{1,0:T(8,128)(2,1)S(1)}, u32[]{:S(2)}, u32[]{:S(2)}) collective-permute-start(bf16[64,128]{1,0:T(8,128)(2,1)S(1)} %get-tuple-element.31.a0), channel_id=1, source_target_pairs={{0,16},{8,24},{16,0},{24,8},{1,17},{9,25},{17,1},{25,9},{2,18},{10... | collective-permute-start | bytes 49160 | tf_op jit(solution)/shard_map/ppermute | solution.py:31
  63.3 3.9 %collective-permute-start.9 = (bf16[64,128]{1,0:T(8,128)(2,1)S(1)}, bf16[64,128]{1,0:T(8,128)(2,1)S(1)}, u32[]{:S(2)}, u32[]{:S(2)}) collective-permute-start(bf16[64,128]{1,0:T(8,128)(2,1)S(1)} %get-tuple-element.31.a0), channel_id=1, source_target_pairs={{0,8},{8,0},{16,24},{24,16},{1,9},{9,1},{17,25},{25,17},{2,10},{10... | collective-permute-start | bytes 49160 | tf_op jit(solution)/shard_map/ppermute | solution.py:31
  74.2 13.6 %all-to-all-start.4 = ((bf16[8,192,128]{2,1,0:T(8,128)(2,1)}), bf16[8,192,128]{2,1,0:T(8,128)(2,1)S(1)}, u32[]{:S(2)}, u32[]{:S(2)}) async-start(bf16[8,192,128]{2,1,0:T(8,128)(2,1)} %get-tuple-element.36), calls=%async_computation.4 | async-start | bytes 786432 | tf_op jit(solution)/shard_map/all_to_all | solution.py:27
  79.1 8.4 %collective-permute-start.14 = (bf16[32,128]{1,0:T(8,128)(2,1)S(1)}, bf16[32,128]{1,0:T(8,128)(2,1)S(1)}, u32[]{:S(2)}, u32[]{:S(2)}) collective-permute-start(bf16[32,128]{1,0:T(8,128)(2,1)S(1)} %get-tuple-element.37.c0), channel_id=1, source_target_pairs={{0,24},{8,16},{16,8},{24,0},{1,25},{9,17},{17,9},{25,1},{2,26},{10... | collective-permute-start | bytes 24584 | tf_op jit(solution)/shard_map/ppermute | solution.py:31
  83.5 4.3 %collective-permute-start.13 = (bf16[32,128]{1,0:T(8,128)(2,1)S(1)}, bf16[32,128]{1,0:T(8,128)(2,1)S(1)}, u32[]{:S(2)}, u32[]{:S(2)}) collective-permute-start(bf16[32,128]{1,0:T(8,128)(2,1)S(1)} %get-tuple-element.37.c0), channel_id=1, source_target_pairs={{0,16},{8,24},{16,0},{24,8},{1,17},{9,25},{17,1},{25,9},{2,18},{10... | collective-permute-start | bytes 24584 | tf_op jit(solution)/shard_map/ppermute | solution.py:31
  84.8 3.1 %collective-permute-start.12 = (bf16[32,128]{1,0:T(8,128)(2,1)S(1)}, bf16[32,128]{1,0:T(8,128)(2,1)S(1)}, u32[]{:S(2)}, u32[]{:S(2)}) collective-permute-start(bf16[32,128]{1,0:T(8,128)(2,1)S(1)} %get-tuple-element.37.c0), channel_id=1, source_target_pairs={{0,8},{8,0},{16,24},{24,16},{1,9},{9,1},{17,25},{25,17},{2,10},{10... | collective-permute-start | bytes 24584 | tf_op jit(solution)/shard_map/ppermute | solution.py:31
  88.6 13.9 %all-to-all-start.5 = ((bf16[8,160,128]{2,1,0:T(8,128)(2,1)}), bf16[8,160,128]{2,1,0:T(8,128)(2,1)S(1)}, u32[]{:S(2)}, u32[]{:S(2)}) async-start(bf16[8,160,128]{2,1,0:T(8,128)(2,1)} %get-tuple-element.38), calls=%async_computation.5 | async-start | bytes 655360 | tf_op jit(solution)/shard_map/all_to_all | solution.py:27
  92.0 5.3 %collective-permute-start.17 = (bf16[64,128]{1,0:T(8,128)(2,1)S(1)}, bf16[64,128]{1,0:T(8,128)(2,1)S(1)}, u32[]{:S(2)}, u32[]{:S(2)}) collective-permute-start(bf16[64,128]{1,0:T(8,128)(2,1)S(1)} %get-tuple-element.39.a0), channel_id=1, source_target_pairs={{0,24},{8,16},{16,8},{24,0},{1,25},{9,17},{17,9},{25,1},{2,26},{10... | collective-permute-start | bytes 49160 | tf_op jit(solution)/shard_map/ppermute | solution.py:31
  95.9 4.1 %collective-permute-start.16 = (bf16[64,128]{1,0:T(8,128)(2,1)S(1)}, bf16[64,128]{1,0:T(8,128)(2,1)S(1)}, u32[]{:S(2)}, u32[]{:S(2)}) collective-permute-start(bf16[64,128]{1,0:T(8,128)(2,1)S(1)} %get-tuple-element.39.a0), channel_id=1, source_target_pairs={{0,16},{8,24},{16,0},{24,8},{1,17},{9,25},{17,1},{25,9},{2,18},{10... | collective-permute-start | bytes 49160 | tf_op jit(solution)/shard_map/ppermute | solution.py:31
  97.1 2.9 %collective-permute-start.15 = (bf16[64,128]{1,0:T(8,128)(2,1)S(1)}, bf16[64,128]{1,0:T(8,128)(2,1)S(1)}, u32[]{:S(2)}, u32[]{:S(2)}) collective-permute-start(bf16[64,128]{1,0:T(8,128)(2,1)S(1)} %get-tuple-element.39.a0), channel_id=1, source_target_pairs={{0,8},{8,0},{16,24},{24,16},{1,9},{9,1},{17,25},{25,17},{2,10},{10... | collective-permute-start | bytes 49160 | tf_op jit(solution)/shard_map/ppermute | solution.py:31
  105.1 23.6 %all-to-all-start.6 = ((f32[256,1,128]{2,1,0:T(1,128)}), f32[256,1,128]{2,1,0:T(1,128)S(1)}, u32[]{:S(2)}, u32[]{:S(2)}) async-start(f32[256,1,128]{2,1,0:T(1,128)} %get-tuple-element.43), calls=%async_computation.6 | async-start | bytes 262144 | tf_op jit(solution)/shard_map/all_to_all | solution.py:27

commit v3 on v2

--- a/solution.py
+++ b/solution.py
@@ -16,7 +16,7 @@
 DEPTH, HEIGHT, WIDTH, RANK = 32, 64, 128, 128
 CELLS = DEPTH * HEIGHT
 N_Z, N_J, N_K = 8, 4, 8
-EACH = 4
+EACH = 8
 ROWS = EACH * HEIGHT
 SCALE = 1.0 / 4096.0
 AB = HEIGHT + WIDTH
@@ -45,16 +45,11 @@
     )(*operands)
 
 
-def pack_kernel(a_ref, b_ref, c_ref, sent_ref, own_ref, wide):
-    wide[...] = jnp.zeros_like(wide)
-    wide[0:HEIGHT, 0:4] = a_ref[...].astype(F32)
-    wide[HEIGHT : HEIGHT + DEPTH, 0:4] = c_ref[...].astype(F32)
-    wide[128:256, 0:2] = b_ref[...].astype(F32)
-    a_and_c = wide[0:128, :].T[0:4]
-    b = wide[128:256, :].T[0:2]
-    own_ref[0:4, :] = a_and_c
-    own_ref[4:6, :] = b
-    own_ref[6:8, :] = jnp.zeros((2, 128), F32)
+def pack_kernel(at_ref, bt_ref, ct_ref, sent_ref, own_ref):
+    own_ref[...] = jnp.zeros_like(own_ref)
+    own_ref[0:4, 0:HEIGHT] = at_ref[...].astype(F32)
+    own_ref[0:4, HEIGHT : HEIGHT + DEPTH] = ct_ref[...].astype(F32)
+    own_ref[4:6, :] = bt_ref[...].astype(F32)
     for peer in range(N_K):
         sent_ref[peer] = own_ref[...]
 
@@ -83,8 +78,7 @@
 
 
 def weight_of(seen_ref, k):
-    seen = seen_ref[pl.ds(k, EACH), :, :].reshape(ROWS, WIDTH)
-    return seen.astype(F32) * SCALE
+    return seen_ref[pl.ds(k * HEIGHT, ROWS), :].astype(F32)
 
 
 def add_products(k, weighted, paired, a, b, c_ref, part_a, part_b, part_c):
@@ -120,13 +114,13 @@
     part_a[...] = jnp.zeros_like(part_a)
     part_b[...] = jnp.zeros_like(part_b)
 
-    @pl.loop(0, DEPTH, step=EACH)
+    @pl.loop(0, DEPTH, step=EACH, unroll=True)
     def _(k):
         a = fa_ref[...]
         paired = in_pairs(k, a, fc_ref).astype(BF16)
         fitted = jnp.dot(paired, fbt_ref[...], preferred_element_type=F32)
-        values = values_ref[pl.ds(k, EACH), :, :].reshape(ROWS, WIDTH).astype(F32)
-        errors = (weight_of(seen_ref, k) * (values - fitted)).astype(BF16)
+        values = values_ref[pl.ds(k * HEIGHT, ROWS), :].astype(F32)
+        errors = (values - weight_of(seen_ref, k) * fitted).astype(BF16)
         add_products(k, errors, paired, a, fb_ref[...], fc_ref, part_a, part_b, part_c)
 
     hand_out(part_a, part_b, part_c, sent_ref, c_out)
@@ -174,7 +168,7 @@
     part_b[...] = jnp.zeros_like(part_b)
     sum_ref[...] = jnp.zeros_like(sum_ref)
 
-    @pl.loop(0, DEPTH, step=EACH)
+    @pl.loop(0, DEPTH, step=EACH, unroll=True)
     def _(k):
         a = fa_ref[...]
         paired = in_pairs(k, a, fc_ref).astype(BF16)
@@ -200,7 +194,7 @@
 
 
 def third_kernel(got_ref, a0, a1, a2, a3, seen_ref, fa_ref, fbt_ref, fc_ref, grad_ref, tangent_ref, sum_ref,
-                 sent_ref, rest_ref, hat_a, hat_bt, hat_c, sum_rest, sum_both):
+                 sent_ref, own_ref, rest_ref, hat_a, hat_bt, hat_c, sum_rest, sum_both):
     take_totals(got_ref, a0, a1, a2, a3, rest_ref)
     grad, product = grad_ref[...], rest_ref[...]
     length = share_of(grad * grad)
@@ -211,7 +205,7 @@
     sum_rest[...] = jnp.zeros_like(sum_rest)
     sum_both[...] = jnp.zeros_like(sum_both)
 
-    @pl.loop(0, DEPTH, step=EACH)
+    @pl.loop(0, DEPTH, step=EACH, unroll=True)
     def _(k):
         paired = in_pairs(k, fa_ref[...], fc_ref).astype(BF16)
         tangent = tangent_at(k, paired, fa_ref, fc_ref, fbt_ref, hat_a, hat_bt, hat_c)
@@ -234,45 +228,57 @@
         )
     ):
         line = jnp.where(lane == place, value, line)
+    own_ref[...] = jnp.broadcast_to(line, (8, 128))
     for peer in range(N_Z * N_J * N_K):
         sent_ref[peer] = line
 
 
-def last_kernel(place, got_ref, own_ref, grad_ref, rest_ref, a_ref, b_ref, c_ref):
+def columns_kernel(place, grad_ref, rest_ref, out_ref):
+    z, jb, kb = place[1], place[0], place[2]
+    for at, x in ((0, grad_ref), (16, rest_ref)):
+        rows = pltpu.roll(x[0:HEIGHT, :], (128 - (jb * N_K + kb) * 4) % 128, 1).T
+        out_ref[at : at + 4, 0:HEIGHT] = rows[0:4]
+        rows = pltpu.roll(x[AB:, :], (128 - (z * N_J + jb) * 4) % 128, 1).T
+        out_ref[at : at + 4, HEIGHT : HEIGHT + DEPTH] = rows[0:4]
+        rows = pltpu.roll(x[HEIGHT:AB, :], (128 - (z * N_K + kb) * 2) % 128, 1).T
+        out_ref[at + 8 : at + 10, :] = rows[0:2]
+
+
+def last_kernel(got_ref, own_ref, columns_ref, a_ref, b_ref, c_ref):
     table = got_ref[:, 0, :].T
     level, gg, gv, vv, s_gg, s_gv, s_vv = (table[i : i + 1] for i in range(7))
 
     def add(x):
         return jnp.sum(x, axis=1, keepdims=True)
 
-    norm = add(gg)
-    alpha = norm / (norm + add(s_gg))
+    norm, norm_seen = add(gg), add(s_gg)
+    alpha = norm / (norm + norm_seen)
     near = 1.0 - alpha * (1.0 + level)
     rr = add(near * near * gg - 2.0 * alpha * near * gv + alpha * alpha * vv)
     rg = add(near * gg - alpha * gv)
     s_rr = add(near * near * s_gg - 2.0 * alpha * near * s_gv + alpha * alpha * s_vv)
     s_rg = add(near * s_gg - alpha * s_gv)
     beta = rr / norm
-    curve = (s_rr + rr) + 2.0 * beta * (s_rg + rg) + beta * beta * (add(s_gg) + norm)
+    curve = (s_rr + rr) + 2.0 * beta * (s_rg + rg) + beta * beta * (norm_seen + norm)
     step = rr / curve
-    own_level = own_ref[0, :, 0:1]
-    own_near = 1.0 - alpha * (1.0 + own_level)
-    x = (alpha + step * (own_near + beta)) * grad_ref[...] - (step * alpha) * rest_ref[...]
-    z, jb, kb = place[1], place[0], place[2]
-    a_ref[...] = pltpu.roll(x[0:HEIGHT], (128 - (jb * N_K + kb) * 4) % 128, 1)[:, 0:4]
-    b_ref[...] = pltpu.roll(x[HEIGHT:AB], (128 - (z * N_K + kb) * 2) % 128, 1)[:, 0:2]
-    c_ref[...] = pltpu.roll(x[AB:], (128 - (z * N_J + jb) * 4) % 128, 1)[:, 0:4]
+    own_near = 1.0 - alpha * (1.0 + own_ref[0:1, 0:1])
+    x = (alpha + step * (own_near + beta)) * columns_ref[0:16, :] - (step * alpha) * columns_ref[16:32, :]
+    a_ref[...] = x[0:4, 0:HEIGHT]
+    c_ref[...] = x[0:4, HEIGHT : HEIGHT + DEPTH]
+    b_ref[...] = x[8:10, :]
 
 
 def local(tensor, observed, factor_a, factor_b, factor_c):
     z, jb, kb = lax.axis_index("ia"), lax.axis_index(JA), lax.axis_index(KA)
     place = jnp.stack([jb, z, kb]).astype(jnp.int32)
+    weight = (observed.astype(F32) * SCALE).astype(BF16).reshape(CELLS, WIDTH)
+    values = tensor.reshape(CELLS, WIDTH) * weight
     tile = lambda rows: ((rows, RANK), F32)
     sums = [tile(HEIGHT), tile(WIDTH), tile(DEPTH)]
     hats = [tile(HEIGHT), ((RANK, WIDTH), BF16), tile(DEPTH)]
 
     sent, own = call(
-        pack_kernel, [((N_K, 8, 128), F32), ((8, 128), F32)], factor_a, factor_b, factor_c, scratch=[tile(256)]
+        pack_kernel, [((N_K, 8, 128), F32), ((8, 128), F32)], factor_a.T, factor_b.T, factor_c.T
     )
     got = exchange(sent, KA)
     sent, own = call(
@@ -285,7 +291,7 @@
     sent, part_c, fa, fb, fbt, fc = call(
         first_kernel,
         sent_types + [tile(HEIGHT), ((WIDTH, RANK), BF16), ((RANK, WIDTH), BF16), tile(DEPTH)],
-        place, got, *across_ja(own), tensor, observed, scratch=sums,
+        place, got, *across_ja(own), values, weight, scratch=sums,
     )
 
     def summed(sent, part_c):
@@ -298,21 +304,17 @@
     sent, part_c, grad, tangent, sum_gg = call(
         second_kernel,
         sent_types + [tile(AB + DEPTH), tile(CELLS), tile(8)],
-        *summed(sent, part_c), observed, fa, fb, fbt, fc, scratch=sums + hats,
-    )
-    sent, rest = call(
+        *summed(sent, part_c), weight, fa, fb, fbt, fc, scratch=sums + hats,
+    )
+    sent, own, rest = call(
         third_kernel,
-        [((N_Z * N_J * N_K, 1, 128), F32), tile(AB + DEPTH)],
-        *summed(sent, part_c), observed, fa, fbt, fc, grad, tangent, sum_gg, scratch=hats + [tile(8), tile(8)],
-    )
+        [((N_Z * N_J * N_K, 1, 128), F32), tile(8), tile(AB + DEPTH)],
+        *summed(sent, part_c), weight, fa, fbt, fc, grad, tangent, sum_gg, scratch=hats + [tile(8), tile(8)],
+    )
+    (columns,) = call(columns_kernel, [tile(32)], place, grad, rest)
     got = exchange(sent, EVERY)
-    return tuple(
-        call(
-            last_kernel,
-            [((HEIGHT, 4), F32), ((WIDTH, 2), F32), ((DEPTH, 4), F32)],
-            place, got, sent[0:1], grad, rest,
-        )
-    )
+    steps = call(last_kernel, [((4, HEIGHT), F32), ((2, WIDTH), F32), ((4, DEPTH), F32)], got, own, columns)
+    return tuple(x.T for x in steps)
 
 
 def solution(mesh):

time: 132 us -> 125 us (0.947)
  waiting for transfers between devices: 37.9 us -> 44.1 us
  local copies, waits for them, and re-layouts: 6.4 us -> 0.68 us
  starting transfers between devices: 71.4 us -> 66 us
  Pallas kernels: 15.2 us -> 10.9 us
  other arithmetic: 0.08 us -> 1.62 us
    all_to_all x7, waiting for transfers between devices: 18.7 us -> 28.2 us  [exchange(): return lax.all_to_all(blocks, axes, 0, 0, tiled=True)]
    all_to_all x7, starting transfers between devices: 43.7 us -> 38.1 us  [exchange(): return lax.all_to_all(blocks, axes, 0, 0, tiled=True)]
    pallas_call x8 -> x9, Pallas kernels: 15.2 us -> 10.9 us  [call(): pl.pallas_call(kernel, out_shape=[jax.ShapeDtypeStruct(shape, dtype) for...]
    ppermute x18, waiting for transfers between devices: 19.2 us -> 15.9 us  [across_ja(): lax.ppermute(x, JA, [(i, i ^ m) for i in range(N_J)])]
    unnamed x13 -> x8, local copies, waits for them, and re-layouts: 3.84 us -> 0.68 us
    pallas_call x3 -> x0, local copies, waits for them, and re-layouts: 1.94 us -> none  [call(): pl.pallas_call(kernel, out_shape=[jax.ShapeDtypeStruct(shape, dtype) for...]
    convert_element_type x0 -> x1, other arithmetic: none -> 1.42 us  [local(): weight = (observed.astype(F32) * SCALE).astype(BF16).reshape(CELLS, WIDTH)]
  transfers between devices with their start and end apart: 25 -> 25, of which waited for: 16 -> 14; matrix products, arithmetic and copies ran while one was open for 1% -> 1% of each run, Pallas kernels for 0% -> 1%
where the time goes in v3:
time: 125 us; the launch traced here: 124 us
  starting transfers between devices  66 us (53%)
  waiting for transfers between devices  44.1 us (35%)
  Pallas kernels  10.9 us (9%)
  other arithmetic  1.62 us (1%)
    all_to_all x7, starting transfers between devices, exchange(): return lax.all_to_all(blocks, axes, 0, 0, tiled=True)  38.1 us
    all_to_all x7, waiting for transfers between devices, exchange(): return lax.all_to_all(blocks, axes, 0, 0, tiled=True)  28.2 us
    ppermute x18, starting transfers between devices, across_ja(): lax.ppermute(x, JA, [(i, i ^ m) for i in range(N_J)])  27.9 us
    ppermute x18, waiting for transfers between devices, across_ja(): lax.ppermute(x, JA, [(i, i ^ m) for i in range(N_J)])  15.9 us
    pallas_call x9, Pallas kernels, call(): pl.pallas_call(kernel, out_shape=[jax.ShapeDtypeStruct(shape, dtype) for...  10.9 us
  transfers between devices with their start and end apart: 25, of which 14 were waited for; matrix products, arithmetic and copies ran while one was open for 1% of the time, Pallas kernels for 1%

profile of v3, /device:TPU:1, one launch (start us, length us, event | category | flops | bytes accessed | tf_op | source)
XLA Modules:
  0.0 124.1 jit_solution(1657889204378981602)
XLA Ops:
  2.0 4.1 %collective-permute-start.2 = (f32[8,128]{1,0:T(8,128)S(1)}, f32[8,128]{1,0:T(8,128)S(1)}, u32[]{:S(2)}, u32[]{:S(2)}) collective-permute-start(f32[8,128]{1,0:T(8,128)S(1)} %get-tuple-element.29.c0), channel_id=1, source_target_pairs={{0,24},{8,16},{16,8},{24,0},{1,25},{9,17},{17,9},{25,1},{2,26},{10... | collective-permute-start | bytes 12296 | tf_op jit(solution)/shard_map/ppermute | solution.py:31
  6.1 2.0 %collective-permute-start.1 = (f32[8,128]{1,0:T(8,128)S(1)}, f32[8,128]{1,0:T(8,128)S(1)}, u32[]{:S(2)}, u32[]{:S(2)}) collective-permute-start(f32[8,128]{1,0:T(8,128)S(1)} %get-tuple-element.29.c0), channel_id=1, source_target_pairs={{0,16},{8,24},{16,0},{24,8},{1,17},{9,25},{17,1},{25,9},{2,18},{10... | collective-permute-start | bytes 12296 | tf_op jit(solution)/shard_map/ppermute | solution.py:31
  8.1 3.5 %all-to-all-start = ((f32[8,8,128]{2,1,0:T(8,128)}), f32[8,8,128]{2,1,0:T(8,128)S(1)}, u32[]{:S(2)}, u32[]{:S(2)}) async-start(f32[8,8,128]{2,1,0:T(8,128)} %get-tuple-element.28), calls=%async_computation | async-start | bytes 65536 | tf_op jit(solution)/shard_map/all_to_all | solution.py:27
  11.6 1.4 %multiply_convert_fusion = bf16[32,64,128]{2,1,0:T(8,128)(2,1)S(1)} fusion(s32[32,64,128]{2,1,0:T(8,128)} %param.6), kind=kLoop, calls=%fused_computation | loop fusion | flops 786432 | bytes 1572864 | tf_op jit(solution)/shard_map/convert_element_type | solution.py:274
  13.1 3.6 %all-to-all-done.got_ref = f32[8,8,128]{2,1,0:T(8,128)S(1)} async-done(((f32[8,8,128]{2,1,0:T(8,128)}), f32[8,8,128]{2,1,0:T(8,128)S(1)}, u32[]{:S(2)}, u32[]{:S(2)}) %all-to-all-start) | async-done | bytes 32800 | tf_op jit(solution)/shard_map/all_to_all | solution.py:27
  17.3 8.2 %all-to-all-start.1 = ((bf16[8,32,128]{2,1,0:T(8,128)(2,1)}), bf16[8,32,128]{2,1,0:T(8,128)(2,1)S(1)}, u32[]{:S(2)}, u32[]{:S(2)}) async-start(bf16[8,32,128]{2,1,0:T(8,128)(2,1)} %get-tuple-element.30), calls=%async_computation.1 | async-start | bytes 131072 | tf_op jit(solution)/shard_map/all_to_all | solution.py:27
  25.7 4.5 %collective-permute-start.5 = (bf16[32,128]{1,0:T(8,128)(2,1)S(1)}, bf16[32,128]{1,0:T(8,128)(2,1)S(1)}, u32[]{:S(2)}, u32[]{:S(2)}) collective-permute-start(bf16[32,128]{1,0:T(8,128)(2,1)S(1)} %get-tuple-element.31.a0), channel_id=1, source_target_pairs={{0,24},{8,16},{16,8},{24,0},{1,25},{9,17},{17,9},{25,1},{2,26},{10... | collective-permute-start | bytes 24584 | tf_op jit(solution)/shard_map/ppermute | solution.py:31
  31.5 2.7 %collective-permute-done.4.a2 = bf16[32,128]{1,0:T(8,128)(2,1)S(1)} collective-permute-done((bf16[32,128]{1,0:T(8,128)(2,1)S(1)}, bf16[32,128]{1,0:T(8,128)(2,1)S(1)}, u32[]{:S(2)}, u32[]{:S(2)}) %collective-permute-start.4) | collective-permute-done | bytes 8224 | tf_op jit(solution)/shard_map/ppermute | solution.py:31
  34.2 2.8 %shard_map.78 = (bf16[8,192,128]{2,1,0:T(8,128)(2,1)}, bf16[32,128]{1,0:T(8,128)(2,1)S(1)}, f32[64,128]{1,0:T(8,128)S(1)}, bf16[128,128]{1,0:T(8,128)(2,1)S(1)},...) custom-call(s32[3]{0:T(128)S(1)} %pad_add_fusion.place, bf16[8,32,128]{2,1,0:T(8,128)(2,1)S(1)} %all-to-all-done.1.got_ref, ...), custom_call_target="tpu_custom_call" | custom-call | tf_op jit(solution)/shard_map/pallas_call | solution.py:35
  37.0 3.5 %all-to-all-start.2 = ((bf16[8,192,128]{2,1,0:T(8,128)(2,1)}), bf16[8,192,128]{2,1,0:T(8,128)(2,1)S(1)}, u32[]{:S(2)}, u32[]{:S(2)}) async-start(bf16[8,192,128]{2,1,0:T(8,128)(2,1)} %get-tuple-element.32), calls=%async_computation.2 | async-start | bytes 786432 | tf_op jit(solution)/shard_map/all_to_all | solution.py:27
  40.5 4.2 %collective-permute-start.8 = (bf16[32,128]{1,0:T(8,128)(2,1)S(1)}, bf16[32,128]{1,0:T(8,128)(2,1)S(1)}, u32[]{:S(2)}, u32[]{:S(2)}) collective-permute-start(bf16[32,128]{1,0:T(8,128)(2,1)S(1)} %get-tuple-element.33.c0), channel_id=1, source_target_pairs={{0,24},{8,16},{16,8},{24,0},{1,25},{9,17},{17,9},{25,1},{2,26},{10... | collective-permute-start | bytes 24584 | tf_op jit(solution)/shard_map/ppermute | solution.py:31
  45.2 3.4 %collective-permute-done.8.c3 = bf16[32,128]{1,0:T(8,128)(2,1)S(1)} collective-permute-done((bf16[32,128]{1,0:T(8,128)(2,1)S(1)}, bf16[32,128]{1,0:T(8,128)(2,1)S(1)}, u32[]{:S(2)}, u32[]{:S(2)}) %collective-permute-start.8) | collective-permute-done | bytes 8224 | tf_op jit(solution)/shard_map/ppermute | solution.py:31
  49.8 7.2 %all-to-all-start.3 = ((bf16[8,160,128]{2,1,0:T(8,128)(2,1)}), bf16[8,160,128]{2,1,0:T(8,128)(2,1)S(1)}, u32[]{:S(2)}, u32[]{:S(2)}) async-start(bf16[8,160,128]{2,1,0:T(8,128)(2,1)} %get-tuple-element.34), calls=%async_computation.3 | async-start | bytes 655360 | tf_op jit(solution)/shard_map/all_to_all | solution.py:27
  57.0 1.6 %collective-permute-start.11 = (bf16[64,128]{1,0:T(8,128)(2,1)S(1)}, bf16[64,128]{1,0:T(8,128)(2,1)S(1)}, u32[]{:S(2)}, u32[]{:S(2)}) collective-permute-start(bf16[64,128]{1,0:T(8,128)(2,1)S(1)} %get-tuple-element.35.a0), channel_id=1, source_target_pairs={{0,24},{8,16},{16,8},{24,0},{1,25},{9,17},{17,9},{25,1},{2,26},{10... | collective-permute-start | bytes 49160 | tf_op jit(solution)/shard_map/ppermute | solution.py:31
  58.6 1.8 %collective-permute-start.10 = (bf16[64,128]{1,0:T(8,128)(2,1)S(1)}, bf16[64,128]{1,0:T(8,128)(2,1)S(1)}, u32[]{:S(2)}, u32[]{:S(2)}) collective-permute-start(bf16[64,128]{1,0:T(8,128)(2,1)S(1)} %get-tuple-element.35.a0), channel_id=1, source_target_pairs={{0,16},{8,24},{16,0},{24,8},{1,17},{9,25},{17,1},{25,9},{2,18},{10... | collective-permute-start | bytes 49160 | tf_op jit(solution)/shard_map/ppermute | solution.py:31
  60.7 1.2 collective-permute-done.11.a3
  61.8 0.9 collective-permute-done.10.a2
  62.7 8.1 %all-to-all-done.3.got_ref = bf16[8,160,128]{2,1,0:T(8,128)(2,1)S(1)} async-done(((bf16[8,160,128]{2,1,0:T(8,128)(2,1)}), bf16[8,160,128]{2,1,0:T(8,128)(2,1)S(1)}, u32[]{:S(2)}, u32[]{:S(2)}) %all-to-all-start.3) | async-done | bytes 327712 | tf_op jit(solution)/shard_map/all_to_all | solution.py:27
  70.8 1.8 %shard_map.80 = (bf16[8,192,128]{2,1,0:T(8,128)(2,1)}, bf16[32,128]{1,0:T(8,128)(2,1)S(1)}, f32[224,128]{1,0:T(8,128)S(1)}, f32[2048,128]{1,0:T(8,128)S(1)}, f32[8,128]{1,0:T(8,128)S(1)}) custom-call(bf16[8,160,128]{2,1,0:T(8,128)(2,1)S(1)} %all-to-all-done.3.got_ref, bf16[64,128]{1,0:T(8,128)(2,1)S(1)} %get-tuple-element.35.a0, ...), custom_call_target="tpu_custom_call" | custom-call | tf_op jit(solution)/shard_map/pallas_call | solution.py:35
  72.5 3.5 %all-to-all-start.4 = ((bf16[8,192,128]{2,1,0:T(8,128)(2,1)}), bf16[8,192,128]{2,1,0:T(8,128)(2,1)S(1)}, u32[]{:S(2)}, u32[]{:S(2)}) async-start(bf16[8,192,128]{2,1,0:T(8,128)(2,1)} %get-tuple-element.40), calls=%async_computation.4 | async-start | bytes 786432 | tf_op jit(solution)/shard_map/all_to_all | solution.py:27
  76.0 2.7 %collective-permute-start.14 = (bf16[32,128]{1,0:T(8,128)(2,1)S(1)}, bf16[32,128]{1,0:T(8,128)(2,1)S(1)}, u32[]{:S(2)}, u32[]{:S(2)}) collective-permute-start(bf16[32,128]{1,0:T(8,128)(2,1)S(1)} %get-tuple-element.41.c0), channel_id=1, source_target_pairs={{0,24},{8,16},{16,8},{24,0},{1,25},{9,17},{17,9},{25,1},{2,26},{10... | collective-permute-start | bytes 24584 | tf_op jit(solution)/shard_map/ppermute | solution.py:31
  79.7 3.8 %collective-permute-done.14.c3 = bf16[32,128]{1,0:T(8,128)(2,1)S(1)} collective-permute-done((bf16[32,128]{1,0:T(8,128)(2,1)S(1)}, bf16[32,128]{1,0:T(8,128)(2,1)S(1)}, u32[]{:S(2)}, u32[]{:S(2)}) %collective-permute-start.14) | collective-permute-done | bytes 8224 | tf_op jit(solution)/shard_map/ppermute | solution.py:31
  85.0 3.4 %all-to-all-start.5 = ((bf16[8,160,128]{2,1,0:T(8,128)(2,1)}), bf16[8,160,128]{2,1,0:T(8,128)(2,1)S(1)}, u32[]{:S(2)}, u32[]{:S(2)}) async-start(bf16[8,160,128]{2,1,0:T(8,128)(2,1)} %get-tuple-element.42), calls=%async_computation.5 | async-start | bytes 655360 | tf_op jit(solution)/shard_map/all_to_all | solution.py:27
  88.5 3.3 %collective-permute-start.17 = (bf16[64,128]{1,0:T(8,128)(2,1)S(1)}, bf16[64,128]{1,0:T(8,128)(2,1)S(1)}, u32[]{:S(2)}, u32[]{:S(2)}) collective-permute-start(bf16[64,128]{1,0:T(8,128)(2,1)S(1)} %get-tuple-element.43.a0), channel_id=1, source_target_pairs={{0,24},{8,16},{16,8},{24,0},{1,25},{9,17},{17,9},{25,1},{2,26},{10... | collective-permute-start | bytes 49160 | tf_op jit(solution)/shard_map/ppermute | solution.py:31
  91.8 1.3 %collective-permute-start.16 = (bf16[64,128]{1,0:T(8,128)(2,1)S(1)}, bf16[64,128]{1,0:T(8,128)(2,1)S(1)}, u32[]{:S(2)}, u32[]{:S(2)}) collective-permute-start(bf16[64,128]{1,0:T(8,128)(2,1)S(1)} %get-tuple-element.43.a0), channel_id=1, source_target_pairs={{0,16},{8,24},{16,0},{24,8},{1,17},{9,25},{17,1},{25,9},{2,18},{10... | collective-permute-start | bytes 49160 | tf_op jit(solution)/shard_map/ppermute | solution.py:31
  93.4 2.5 %collective-permute-done.16.a2 = bf16[64,128]{1,0:T(8,128)(2,1)S(1)} collective-permute-done((bf16[64,128]{1,0:T(8,128)(2,1)S(1)}, bf16[64,128]{1,0:T(8,128)(2,1)S(1)}, u32[]{:S(2)}, u32[]{:S(2)}) %collective-permute-start.16) | collective-permute-done | bytes 16416 | tf_op jit(solution)/shard_map/ppermute | solution.py:31
  95.9 3.6 %all-to-all-done.5.got_ref = bf16[8,160,128]{2,1,0:T(8,128)(2,1)S(1)} async-done(((bf16[8,160,128]{2,1,0:T(8,128)(2,1)}), bf16[8,160,128]{2,1,0:T(8,128)(2,1)S(1)}, u32[]{:S(2)}, u32[]{:S(2)}) %all-to-all-start.5) | async-done | bytes 327712 | tf_op jit(solution)/shard_map/all_to_all | solution.py:27
  99.5 1.5 %shard_map.82 = (f32[256,1,128]{2,1,0:T(1,128)}, f32[8,128]{1,0:T(8,128)S(1)}, f32[224,128]{1,0:T(8,128)S(1)}) custom-call(bf16[8,160,128]{2,1,0:T(8,128)(2,1)S(1)} %all-to-all-done.5.got_ref, bf16[64,128]{1,0:T(8,128)(2,1)S(1)} %get-tuple-element.43.a0, bf16[64,128]{1,0:T(8,128)(2,1)S(1)} %collective-permute-done.15.a1, ...), custom_call_target="tpu_custom_call" | custom-call | tf_op jit(solution)/shard_map/pallas_call | solution.py:35
  101.0 8.9 %all-to-all-start.6 = ((f32[256,1,128]{2,1,0:T(1,128)}), f32[256,1,128]{2,1,0:T(1,128)S(1)}, u32[]{:S(2)}, u32[]{:S(2)}) async-start(f32[256,1,128]{2,1,0:T(1,128)} %get-tuple-element.47), calls=%async_computation.6 | async-start | bytes 262144 | tf_op jit(solution)/shard_map/all_to_all | solution.py:27
  109.9 0.9 shard_map.83.columns_ref
  110.8 12.3 %all-to-all-done.6.got_ref = f32[256,1,128]{2,1,0:T(1,128)S(1)} async-done(((f32[256,1,128]{2,1,0:T(1,128)}), f32[256,1,128]{2,1,0:T(1,128)S(1)}, u32[]{:S(2)}, u32[]{:S(2)}) %all-to-all-start.6) | async-done | bytes 131104 | tf_op jit(solution)/shard_map/all_to_all | solution.py:27
  123.1 1.0 shard_map.84
  (38 shorter events, 8.2 us)
Async XLA Ops:
  0.6 0.7 copy-start.1
  0.6 0.7 copy-start
  0.7 0.7 copy-start.2
  2.0 11.0 %collective-permute-start.2 = (f32[8,128]{1,0:T(8,128)S(1)}, f32[8,128]{1,0:T(8,128)S(1)}, u32[]{:S(2)}, u32[]{:S(2)}) collective-permute-start(f32[8,128]{1,0:T(8,128)S(1)} %get-tuple-element.29.c0), channel_id=1, source_target_pairs={{0,24},{8,16},{16,8},{24,0},{1,25},{9,17},{17,9},{25,1},{2,26},{10... | collective-permute-start | bytes 12296 | tf_op jit(solution)/shard_map/ppermute | solution.py:31
  6.1 6.9 %collective-permute-start.1 = (f32[8,128]{1,0:T(8,128)S(1)}, f32[8,128]{1,0:T(8,128)S(1)}, u32[]{:S(2)}, u32[]{:S(2)}) collective-permute-start(f32[8,128]{1,0:T(8,128)S(1)} %get-tuple-element.29.c0), channel_id=1, source_target_pairs={{0,16},{8,24},{16,0},{24,8},{1,17},{9,25},{17,1},{25,9},{2,18},{10... | collective-permute-start | bytes 12296 | tf_op jit(solution)/shard_map/ppermute | solution.py:31
  8.1 5.0 %collective-permute-start = (f32[8,128]{1,0:T(8,128)S(1)}, f32[8,128]{1,0:T(8,128)S(1)}, u32[]{:S(2)}, u32[]{:S(2)}) collective-permute-start(f32[8,128]{1,0:T(8,128)S(1)} %get-tuple-element.29.c0), channel_id=1, source_target_pairs={{0,8},{8,0},{16,24},{24,16},{1,9},{9,1},{17,25},{25,17},{2,10},{10... | collective-permute-start | bytes 12296 | tf_op jit(solution)/shard_map/ppermute | solution.py:31
  8.1 8.6 %all-to-all-start = ((f32[8,8,128]{2,1,0:T(8,128)}), f32[8,8,128]{2,1,0:T(8,128)S(1)}, u32[]{:S(2)}, u32[]{:S(2)}) async-start(f32[8,8,128]{2,1,0:T(8,128)} %get-tuple-element.28), calls=%async_computation | async-start | bytes 65536 | tf_op jit(solution)/shard_map/all_to_all | solution.py:27
  11.6 13.9 %copy-start.3 = (bf16[32,64,128]{2,1,0:T(8,128)(2,1)S(1)}, bf16[32,64,128]{2,1,0:T(8,128)(2,1)}, u32[]{:S(2)}) copy-start(bf16[32,64,128]{2,1,0:T(8,128)(2,1)} %param.5) | copy-start | bytes 1572868
  17.3 16.9 %all-to-all-start.1 = ((bf16[8,32,128]{2,1,0:T(8,128)(2,1)}), bf16[8,32,128]{2,1,0:T(8,128)(2,1)S(1)}, u32[]{:S(2)}, u32[]{:S(2)}) async-start(bf16[8,32,128]{2,1,0:T(8,128)(2,1)} %get-tuple-element.30), calls=%async_computation.1 | async-start | bytes 131072 | tf_op jit(solution)/shard_map/all_to_all | solution.py:27
  25.7 5.9 %collective-permute-start.5 = (bf16[32,128]{1,0:T(8,128)(2,1)S(1)}, bf16[32,128]{1,0:T(8,128)(2,1)S(1)}, u32[]{:S(2)}, u32[]{:S(2)}) collective-permute-start(bf16[32,128]{1,0:T(8,128)(2,1)S(1)} %get-tuple-element.31.a0), channel_id=1, source_target_pairs={{0,24},{8,16},{16,8},{24,0},{1,25},{9,17},{17,9},{25,1},{2,26},{10... | collective-permute-start | bytes 24584 | tf_op jit(solution)/shard_map/ppermute | solution.py:31
  30.2 4.0 %collective-permute-start.4 = (bf16[32,128]{1,0:T(8,128)(2,1)S(1)}, bf16[32,128]{1,0:T(8,128)(2,1)S(1)}, u32[]{:S(2)}, u32[]{:S(2)}) collective-permute-start(bf16[32,128]{1,0:T(8,128)(2,1)S(1)} %get-tuple-element.31.a0), channel_id=1, source_target_pairs={{0,16},{8,24},{16,0},{24,8},{1,17},{9,25},{17,1},{25,9},{2,18},{10... | collective-permute-start | bytes 24584 | tf_op jit(solution)/shard_map/ppermute | solution.py:31
  30.7 3.5 %collective-permute-start.3 = (bf16[32,128]{1,0:T(8,128)(2,1)S(1)}, bf16[32,128]{1,0:T(8,128)(2,1)S(1)}, u32[]{:S(2)}, u32[]{:S(2)}) collective-permute-start(bf16[32,128]{1,0:T(8,128)(2,1)S(1)} %get-tuple-element.31.a0), channel_id=1, source_target_pairs={{0,8},{8,0},{16,24},{24,16},{1,9},{9,1},{17,25},{25,17},{2,10},{10... | collective-permute-start | bytes 24584 | tf_op jit(solution)/shard_map/ppermute | solution.py:31
  37.0 12.0 %all-to-all-start.2 = ((bf16[8,192,128]{2,1,0:T(8,128)(2,1)}), bf16[8,192,128]{2,1,0:T(8,128)(2,1)S(1)}, u32[]{:S(2)}, u32[]{:S(2)}) async-start(bf16[8,192,128]{2,1,0:T(8,128)(2,1)} %get-tuple-element.32), calls=%async_computation.2 | async-start | bytes 786432 | tf_op jit(solution)/shard_map/all_to_all | solution.py:27
  40.5 8.1 %collective-permute-start.8 = (bf16[32,128]{1,0:T(8,128)(2,1)S(1)}, bf16[32,128]{1,0:T(8,128)(2,1)S(1)}, u32[]{:S(2)}, u32[]{:S(2)}) collective-permute-start(bf16[32,128]{1,0:T(8,128)(2,1)S(1)} %get-tuple-element.33.c0), channel_id=1, source_target_pairs={{0,24},{8,16},{16,8},{24,0},{1,25},{9,17},{17,9},{25,1},{2,26},{10... | collective-permute-start | bytes 24584 | tf_op jit(solution)/shard_map/ppermute | solution.py:31
  44.7 4.3 %collective-permute-start.7 = (bf16[32,128]{1,0:T(8,128)(2,1)S(1)}, bf16[32,128]{1,0:T(8,128)(2,1)S(1)}, u32[]{:S(2)}, u32[]{:S(2)}) collective-permute-start(bf16[32,128]{1,0:T(8,128)(2,1)S(1)} %get-tuple-element.33.c0), channel_id=1, source_target_pairs={{0,16},{8,24},{16,0},{24,8},{1,17},{9,25},{17,1},{25,9},{2,18},{10... | collective-permute-start | bytes 24584 | tf_op jit(solution)/shard_map/ppermute | solution.py:31
  45.2 3.8 %collective-permute-start.6 = (bf16[32,128]{1,0:T(8,128)(2,1)S(1)}, bf16[32,128]{1,0:T(8,128)(2,1)S(1)}, u32[]{:S(2)}, u32[]{:S(2)}) collective-permute-start(bf16[32,128]{1,0:T(8,128)(2,1)S(1)} %get-tuple-element.33.c0), channel_id=1, source_target_pairs={{0,8},{8,0},{16,24},{24,16},{1,9},{9,1},{17,25},{25,17},{2,10},{10... | collective-permute-start | bytes 24584 | tf_op jit(solution)/shard_map/ppermute | solution.py:31
  49.8 21.0 %all-to-all-start.3 = ((bf16[8,160,128]{2,1,0:T(8,128)(2,1)}), bf16[8,160,128]{2,1,0:T(8,128)(2,1)S(1)}, u32[]{:S(2)}, u32[]{:S(2)}) async-start(bf16[8,160,128]{2,1,0:T(8,128)(2,1)} %get-tuple-element.34), calls=%async_computation.3 | async-start | bytes 655360 | tf_op jit(solution)/shard_map/all_to_all | solution.py:27
  57.0 4.8 %collective-permute-start.11 = (bf16[64,128]{1,0:T(8,128)(2,1)S(1)}, bf16[64,128]{1,0:T(8,128)(2,1)S(1)}, u32[]{:S(2)}, u32[]{:S(2)}) collective-permute-start(bf16[64,128]{1,0:T(8,128)(2,1)S(1)} %get-tuple-element.35.a0), channel_id=1, source_target_pairs={{0,24},{8,16},{16,8},{24,0},{1,25},{9,17},{17,9},{25,1},{2,26},{10... | collective-permute-start | bytes 49160 | tf_op jit(solution)/shard_map/ppermute | solution.py:31
  58.6 4.1 %collective-permute-start.10 = (bf16[64,128]{1,0:T(8,128)(2,1)S(1)}, bf16[64,128]{1,0:T(8,128)(2,1)S(1)}, u32[]{:S(2)}, u32[]{:S(2)}) collective-permute-start(bf16[64,128]{1,0:T(8,128)(2,1)S(1)} %get-tuple-element.35.a0), channel_id=1, source_target_pairs={{0,16},{8,24},{16,0},{24,8},{1,17},{9,25},{17,1},{25,9},{2,18},{10... | collective-permute-start | bytes 49160 | tf_op jit(solution)/shard_map/ppermute | solution.py:31
  60.4 2.3 %collective-permute-start.9 = (bf16[64,128]{1,0:T(8,128)(2,1)S(1)}, bf16[64,128]{1,0:T(8,128)(2,1)S(1)}, u32[]{:S(2)}, u32[]{:S(2)}) collective-permute-start(bf16[64,128]{1,0:T(8,128)(2,1)S(1)} %get-tuple-element.35.a0), channel_id=1, source_target_pairs={{0,8},{8,0},{16,24},{24,16},{1,9},{9,1},{17,25},{25,17},{2,10},{10... | collective-permute-start | bytes 49160 | tf_op jit(solution)/shard_map/ppermute | solution.py:31
  72.5 11.7 %all-to-all-start.4 = ((bf16[8,192,128]{2,1,0:T(8,128)(2,1)}), bf16[8,192,128]{2,1,0:T(8,128)(2,1)S(1)}, u32[]{:S(2)}, u32[]{:S(2)}) async-start(bf16[8,192,128]{2,1,0:T(8,128)(2,1)} %get-tuple-element.40), calls=%async_computation.4 | async-start | bytes 786432 | tf_op jit(solution)/shard_map/all_to_all | solution.py:27
  76.0 7.5 %collective-permute-start.14 = (bf16[32,128]{1,0:T(8,128)(2,1)S(1)}, bf16[32,128]{1,0:T(8,128)(2,1)S(1)}, u32[]{:S(2)}, u32[]{:S(2)}) collective-permute-start(bf16[32,128]{1,0:T(8,128)(2,1)S(1)} %get-tuple-element.41.c0), channel_id=1, source_target_pairs={{0,24},{8,16},{16,8},{24,0},{1,25},{9,17},{17,9},{25,1},{2,26},{10... | collective-permute-start | bytes 24584 | tf_op jit(solution)/shard_map/ppermute | solution.py:31
  78.7 4.9 %collective-permute-start.13 = (bf16[32,128]{1,0:T(8,128)(2,1)S(1)}, bf16[32,128]{1,0:T(8,128)(2,1)S(1)}, u32[]{:S(2)}, u32[]{:S(2)}) collective-permute-start(bf16[32,128]{1,0:T(8,128)(2,1)S(1)} %get-tuple-element.41.c0), channel_id=1, source_target_pairs={{0,16},{8,24},{16,0},{24,8},{1,17},{9,25},{17,1},{25,9},{2,18},{10... | collective-permute-start | bytes 24584 | tf_op jit(solution)/shard_map/ppermute | solution.py:31
  79.4 4.1 %collective-permute-start.12 = (bf16[32,128]{1,0:T(8,128)(2,1)S(1)}, bf16[32,128]{1,0:T(8,128)(2,1)S(1)}, u32[]{:S(2)}, u32[]{:S(2)}) collective-permute-start(bf16[32,128]{1,0:T(8,128)(2,1)S(1)} %get-tuple-element.41.c0), channel_id=1, source_target_pairs={{0,8},{8,0},{16,24},{24,16},{1,9},{9,1},{17,25},{25,17},{2,10},{10... | collective-permute-start | bytes 24584 | tf_op jit(solution)/shard_map/ppermute | solution.py:31
  85.0 14.5 %all-to-all-start.5 = ((bf16[8,160,128]{2,1,0:T(8,128)(2,1)}), bf16[8,160,128]{2,1,0:T(8,128)(2,1)S(1)}, u32[]{:S(2)}, u32[]{:S(2)}) async-start(bf16[8,160,128]{2,1,0:T(8,128)(2,1)} %get-tuple-element.42), calls=%async_computation.5 | async-start | bytes 655360 | tf_op jit(solution)/shard_map/all_to_all | solution.py:27
  88.5 4.9 %collective-permute-start.17 = (bf16[64,128]{1,0:T(8,128)(2,1)S(1)}, bf16[64,128]{1,0:T(8,128)(2,1)S(1)}, u32[]{:S(2)}, u32[]{:S(2)}) collective-permute-start(bf16[64,128]{1,0:T(8,128)(2,1)S(1)} %get-tuple-element.43.a0), channel_id=1, source_target_pairs={{0,24},{8,16},{16,8},{24,0},{1,25},{9,17},{17,9},{25,1},{2,26},{10... | collective-permute-start | bytes 49160 | tf_op jit(solution)/shard_map/ppermute | solution.py:31
  91.8 4.1 %collective-permute-start.16 = (bf16[64,128]{1,0:T(8,128)(2,1)S(1)}, bf16[64,128]{1,0:T(8,128)(2,1)S(1)}, u32[]{:S(2)}, u32[]{:S(2)}) collective-permute-start(bf16[64,128]{1,0:T(8,128)(2,1)S(1)} %get-tuple-element.43.a0), channel_id=1, source_target_pairs={{0,16},{8,24},{16,0},{24,8},{1,17},{9,25},{17,1},{25,9},{2,18},{10... | collective-permute-start | bytes 49160 | tf_op jit(solution)/shard_map/ppermute | solution.py:31
  93.1 2.8 %collective-permute-start.15 = (bf16[64,128]{1,0:T(8,128)(2,1)S(1)}, bf16[64,128]{1,0:T(8,128)(2,1)S(1)}, u32[]{:S(2)}, u32[]{:S(2)}) collective-permute-start(bf16[64,128]{1,0:T(8,128)(2,1)S(1)} %get-tuple-element.43.a0), channel_id=1, source_target_pairs={{0,8},{8,0},{16,24},{24,16},{1,9},{9,1},{17,25},{25,17},{2,10},{10... | collective-permute-start | bytes 49160 | tf_op jit(solution)/shard_map/ppermute | solution.py:31
  101.0 22.1 %all-to-all-start.6 = ((f32[256,1,128]{2,1,0:T(1,128)}), f32[256,1,128]{2,1,0:T(1,128)S(1)}, u32[]{:S(2)}, u32[]{:S(2)}) async-start(f32[256,1,128]{2,1,0:T(1,128)} %get-tuple-element.47), calls=%async_computation.6 | async-start | bytes 262144 | tf_op jit(solution)/shard_map/all_to_all | solution.py:27

commit v4 on v3

--- a/solution.py
+++ b/solution.py
@@ -27,8 +27,13 @@
     return lax.all_to_all(blocks, axes, 0, 0, tiled=True)
 
 
-def across_ja(x):
-    return [x] + [lax.ppermute(x, JA, [(i, i ^ m) for i in range(N_J)]) for m in (1, 2, 3)]
+def swapped(x, axis):
+    return lax.ppermute(x, axis, [(0, 1), (1, 0)])
+
+
+def over_ja(x):
+    x = x + swapped(x, "ja_1")
+    return x + swapped(x, "ja_0")
 
 
 def call(kernel, outs, *operands, scratch=()):
@@ -45,32 +50,31 @@
     )(*operands)
 
 
-def pack_kernel(at_ref, bt_ref, ct_ref, sent_ref, own_ref):
-    own_ref[...] = jnp.zeros_like(own_ref)
-    own_ref[0:4, 0:HEIGHT] = at_ref[...].astype(F32)
-    own_ref[0:4, HEIGHT : HEIGHT + DEPTH] = ct_ref[...].astype(F32)
-    own_ref[4:6, :] = bt_ref[...].astype(F32)
-    for peer in range(N_K):
-        sent_ref[peer] = own_ref[...]
-
-
-def repack_kernel(got_ref, c0, c1, c2, c3, sent_ref, a_ref, rows_a, rows_b, rows_c):
-    for peer in range(N_K):
-        rows_a[4 * peer : 4 * peer + 4, :] = got_ref[peer, 0:4, :]
-        rows_b[2 * peer : 2 * peer + 2, :] = got_ref[peer, 4:6, :]
-    for m, piece in enumerate((c0, c1, c2, c3)):
-        rows_c[4 * m : 4 * m + 4, :] = piece[0:4, :]
-    a_ref[...] = rows_a[...].astype(BF16)
+def pack_kernel(at_ref, bt_ref, ct_ref, sent_ref, block):
+    block[...] = jnp.zeros_like(block)
+    block[0:4, 0:HEIGHT] = at_ref[...].astype(F32)
+    block[0:4, HEIGHT : HEIGHT + DEPTH] = ct_ref[...].astype(F32)
+    block[4:6, :] = bt_ref[...].astype(F32)
+    for peer in range(N_J * N_K):
+        sent_ref[peer] = block[...]
+
+
+def repack_kernel(place, got_ref, sent_ref, rows_b, rows_c):
+    jb, kb = place[0], place[2]
+    for k in range(N_K):
+        rows_b[2 * k : 2 * k + 2, :] = got_ref[jb * N_K + k, 4:6, :]
+    for j in range(N_J):
+        rows_c[4 * j : 4 * j + 4, :] = got_ref[j * N_K + kb, 0:4, :]
     b, c = rows_b[...].astype(BF16), rows_c[...].astype(BF16)
     for peer in range(N_Z):
         sent_ref[peer, 0:16, :] = b
         sent_ref[peer, 16:32, :] = c
 
 
-def xor_lanes(x, bit, on):
-    lane = lax.broadcasted_iota(jnp.int32, x.shape, 1)
-    swapped = jnp.where((lane & bit) != 0, pltpu.roll(x, bit, 1), pltpu.roll(x, 128 - bit, 1))
-    return jnp.where(on != 0, swapped, x)
+def rows_kernel(got_ref, fa_ref, rows_a):
+    for peer in range(N_J * N_K):
+        rows_a[4 * peer : 4 * peer + 4, :] = got_ref[peer, 0:4, :]
+    fa_ref[...] = rows_a[...].T[0:HEIGHT]
 
 
 def in_pairs(k, a, c_ref):
@@ -97,20 +101,15 @@
     for peer in range(N_K):
         sent_ref[peer, 0:HEIGHT, :] = a
         sent_ref[peer, HEIGHT:AB, :] = b
-    c_out[...] = part_c[...].astype(BF16)
-
-
-def first_kernel(place, got_ref, a0, a1, a2, a3, values_ref, seen_ref,
-                 sent_ref, c_out, fa_ref, fb_ref, fbt_ref, fc_ref, part_a, part_b, part_c):
-    a = jnp.concatenate([x[...].astype(F32) for x in (a0, a1, a2, a3)], axis=0).T[0:HEIGHT]
-    a = xor_lanes(xor_lanes(a, 32, place[0] & 1), 64, place[0] & 2)
-    c = jnp.concatenate([got_ref[z, 16:32, :].astype(F32) for z in range(N_Z)], axis=0).T[HEIGHT : HEIGHT + DEPTH]
-    c = xor_lanes(xor_lanes(c, 4, place[0] & 1), 8, place[0] & 2)
-    bt = jnp.concatenate([got_ref[z, 0:16, :].astype(F32) for z in range(N_Z)], axis=0)
-    fbt_ref[...] = bt.astype(BF16)
-    fb_ref[...] = bt.T.astype(BF16)
-    fa_ref[...] = a
-    fc_ref[...] = c
+    c_out[...] = part_c[...]
+
+
+def first_kernel(got_ref, fa_ref, values_ref, seen_ref, sent_ref, c_out, fb_ref, fbt_ref, fc_ref, part_a, part_b, part_c):
+    c = jnp.concatenate([got_ref[z, 16:32, :].astype(F32) for z in range(N_Z)], axis=0)
+    fc_ref[...] = c.T[HEIGHT : HEIGHT + DEPTH]
+    bt = jnp.concatenate([got_ref[z, 0:16, :] for z in range(N_Z)], axis=0)
+    fbt_ref[...] = bt
+    fb_ref[...] = bt.astype(F32).T.astype(BF16)
     part_a[...] = jnp.zeros_like(part_a)
     part_b[...] = jnp.zeros_like(part_b)
 
@@ -126,23 +125,23 @@
     hand_out(part_a, part_b, part_c, sent_ref, c_out)
 
 
-def middle_kernel(got_ref, c0, c1, c2, c3, sent_ref, a_ref):
+def middle_kernel(got_ref, c_ref, sent_ref, a_ref):
     total = got_ref[0].astype(F32)
     for peer in range(1, N_K):
         total = total + got_ref[peer].astype(F32)
-    a_ref[...] = total[0:HEIGHT].astype(BF16)
+    a_ref[...] = total[0:HEIGHT]
     b = total[HEIGHT:AB].astype(BF16)
-    c = ((c0[...].astype(F32) + c1[...].astype(F32)) + (c2[...].astype(F32) + c3[...].astype(F32))).astype(BF16)
+    c = c_ref[...].astype(BF16)
     for peer in range(N_Z):
         sent_ref[peer, 0:WIDTH, :] = b
         sent_ref[peer, WIDTH:BC, :] = c
 
 
-def take_totals(got_ref, a0, a1, a2, a3, out):
+def take_totals(got_ref, a_ref, out):
     total = got_ref[0].astype(F32)
     for peer in range(1, N_Z):
         total = total + got_ref[peer].astype(F32)
-    out[0:HEIGHT, :] = (a0[...].astype(F32) + a1[...].astype(F32)) + (a2[...].astype(F32) + a3[...].astype(F32))
+    out[0:HEIGHT, :] = a_ref[...]
     out[HEIGHT : HEIGHT + BC, :] = total
 
 
@@ -159,10 +158,10 @@
     hat_c[...] = direction[AB:].astype(BF16).astype(F32)
 
 
-def second_kernel(got_ref, a0, a1, a2, a3, seen_ref, fa_ref, fb_ref, fbt_ref, fc_ref,
+def second_kernel(got_ref, a_sum, seen_ref, fa_ref, fb_ref, fbt_ref, fc_ref,
                   sent_ref, c_out, grad_ref, tangent_ref, sum_ref,
                   part_a, part_b, part_c, hat_a, hat_bt, hat_c):
-    take_totals(got_ref, a0, a1, a2, a3, grad_ref)
+    take_totals(got_ref, a_sum, grad_ref)
     round_hats(grad_ref[...], hat_a, hat_bt, hat_c)
     part_a[...] = jnp.zeros_like(part_a)
     part_b[...] = jnp.zeros_like(part_b)
@@ -193,9 +192,9 @@
     )
 
 
-def third_kernel(got_ref, a0, a1, a2, a3, seen_ref, fa_ref, fbt_ref, fc_ref, grad_ref, tangent_ref, sum_ref,
+def third_kernel(got_ref, a_sum, seen_ref, fa_ref, fbt_ref, fc_ref, grad_ref, tangent_ref, sum_ref,
                  sent_ref, own_ref, rest_ref, hat_a, hat_bt, hat_c, sum_rest, sum_both):
-    take_totals(got_ref, a0, a1, a2, a3, rest_ref)
+    take_totals(got_ref, a_sum, rest_ref)
     grad, product = grad_ref[...], rest_ref[...]
     length = share_of(grad * grad)
     level = jnp.where(length > 0.0, share_of(grad * product) / jnp.where(length > 0.0, length, 1.0), 0.0)
@@ -277,29 +276,27 @@
     sums = [tile(HEIGHT), tile(WIDTH), tile(DEPTH)]
     hats = [tile(HEIGHT), ((RANK, WIDTH), BF16), tile(DEPTH)]
 
-    sent, own = call(
-        pack_kernel, [((N_K, 8, 128), F32), ((8, 128), F32)], factor_a.T, factor_b.T, factor_c.T
-    )
-    got = exchange(sent, KA)
-    sent, own = call(
-        repack_kernel, [((N_Z, 32, 128), BF16), ((32, 128), BF16)], got, *across_ja(own),
-        scratch=[tile(32), tile(16), tile(16)],
-    )
+    (sent,) = call(
+        pack_kernel, [((N_J * N_K, 8, 128), F32)], factor_a.T, factor_b.T, factor_c.T, scratch=[tile(8)]
+    )
+    shards = exchange(sent, PLANE)
+    (sent,) = call(repack_kernel, [((N_Z, 32, 128), BF16)], place, shards, scratch=[tile(16), tile(16)])
     got = exchange(sent, "ia")
-
-    sent_types = [((N_K, AB, RANK), BF16), ((DEPTH, RANK), BF16)]
-    sent, part_c, fa, fb, fbt, fc = call(
+    (fa,) = call(rows_kernel, [tile(HEIGHT)], shards, scratch=[tile(128)])
+
+    sent_types = [((N_K, AB, RANK), BF16), tile(DEPTH)]
+    sent, part_c, fb, fbt, fc = call(
         first_kernel,
-        sent_types + [tile(HEIGHT), ((WIDTH, RANK), BF16), ((RANK, WIDTH), BF16), tile(DEPTH)],
-        place, got, *across_ja(own), values, weight, scratch=sums,
+        sent_types + [((WIDTH, RANK), BF16), ((RANK, WIDTH), BF16), tile(DEPTH)],
+        got, fa, values, weight, scratch=sums,
     )
 
     def summed(sent, part_c):
         got = exchange(sent, KA)
         sent, part_a = call(
-            middle_kernel, [((N_Z, BC, RANK), BF16), ((HEIGHT, RANK), BF16)], got, *across_ja(part_c)
+            middle_kernel, [((N_Z, BC, RANK), BF16), tile(HEIGHT)], got, over_ja(part_c)
         )
-        return exchange(sent, "ia"), *across_ja(part_a)
+        return exchange(sent, "ia"), over_ja(part_a)
 
     sent, part_c, grad, tangent, sum_gg = call(
         second_kernel,

time: 125 us -> 119 us (0.952)
  starting transfers between devices: 66 us -> 58.7 us
  waiting for transfers between devices: 44.1 us -> 45.9 us
    ppermute x18 -> x8, starting transfers between devices: 27.9 us -> 14.9 us  [swapped(): return lax.ppermute(x, axis, [(0, 1), (1, 0)])]
    all_to_all x7, starting transfers between devices: 38.1 us -> 43.8 us  [exchange(): return lax.all_to_all(blocks, axes, 0, 0, tiled=True)]
    ppermute x18 -> x8, waiting for transfers between devices: 15.9 us -> 16.9 us  [swapped(): return lax.ppermute(x, axis, [(0, 1), (1, 0)])]
    pallas_call x9 -> x10, Pallas kernels: 10.9 us -> 10.9 us  [call(): pl.pallas_call(kernel, out_shape=[jax.ShapeDtypeStruct(shape, dtype) for...]
  transfers between devices with their start and end apart: 25 -> 15, of which waited for: 14 -> 13; matrix products, arithmetic and copies ran while one was open for 1% -> 1% of each run, Pallas kernels for 1% -> 1%
where the time goes in v4:
time: 119 us
  starting transfers between devices  58.7 us (49%)
  waiting for transfers between devices  45.9 us (39%)
  Pallas kernels  10.9 us (9%)
  other arithmetic  1.66 us (1%)
    all_to_all x7, starting transfers between devices, exchange(): return lax.all_to_all(blocks, axes, 0, 0, tiled=True)  43.8 us
    all_to_all x7, waiting for transfers between devices, exchange(): return lax.all_to_all(blocks, axes, 0, 0, tiled=True)  28.9 us
    ppermute x8, waiting for transfers between devices, swapped(): return lax.ppermute(x, axis, [(0, 1), (1, 0)])  16.9 us
    ppermute x8, starting transfers between devices, swapped(): return lax.ppermute(x, axis, [(0, 1), (1, 0)])  14.9 us
    pallas_call x10, Pallas kernels, call(): pl.pallas_call(kernel, out_shape=[jax.ShapeDtypeStruct(shape, dtype) for...  10.9 us
  transfers between devices with their start and end apart: 15, of which 13 were waited for; matrix products, arithmetic and copies ran while one was open for 1% of the time, Pallas kernels for 1%

profile of v4, /device:TPU:1, one launch (start us, length us, event | category | flops | bytes accessed | tf_op | source)
XLA Modules:
  0.0 118.5 jit_solution(17878748931879701972)
XLA Ops:
  2.1 8.6 %all-to-all-start = ((f32[32,8,128]{2,1,0:T(8,128)}), f32[32,8,128]{2,1,0:T(8,128)S(1)}, u32[]{:S(2)}, u32[]{:S(2)}) async-start(f32[32,8,128]{2,1,0:T(8,128)} %shard_map.76), calls=%async_computation | async-start | bytes 262144 | tf_op jit(solution)/shard_map/all_to_all | solution.py:27
  10.7 1.4 %multiply_convert_fusion = bf16[32,64,128]{2,1,0:T(8,128)(2,1)S(1)} fusion(s32[32,64,128]{2,1,0:T(8,128)} %param.6), kind=kLoop, calls=%fused_computation | loop fusion | flops 786432 | bytes 1572864 | tf_op jit(solution)/shard_map/convert_element_type | solution.py:273
  12.2 6.2 %all-to-all-done.got_ref = f32[32,8,128]{2,1,0:T(8,128)S(1)} async-done(((f32[32,8,128]{2,1,0:T(8,128)}), f32[32,8,128]{2,1,0:T(8,128)S(1)}, u32[]{:S(2)}, u32[]{:S(2)}) %all-to-all-start) | async-done | bytes 131104 | tf_op jit(solution)/shard_map/all_to_all | solution.py:27
  18.4 1.2 shard_map.77
  19.6 8.2 %all-to-all-start.1 = ((bf16[8,32,128]{2,1,0:T(8,128)(2,1)}), bf16[8,32,128]{2,1,0:T(8,128)(2,1)S(1)}, u32[]{:S(2)}, u32[]{:S(2)}) async-start(bf16[8,32,128]{2,1,0:T(8,128)(2,1)} %shard_map.77), calls=%async_computation.1 | async-start | bytes 131072 | tf_op jit(solution)/shard_map/all_to_all | solution.py:27
  28.0 7.0 %all-to-all-done.1.got_ref = bf16[8,32,128]{2,1,0:T(8,128)(2,1)S(1)} async-done(((bf16[8,32,128]{2,1,0:T(8,128)(2,1)}), bf16[8,32,128]{2,1,0:T(8,128)(2,1)S(1)}, u32[]{:S(2)}, u32[]{:S(2)}) %all-to-all-start.1) | async-done | bytes 65568 | tf_op jit(solution)/shard_map/all_to_all | solution.py:27
  35.0 2.1 %shard_map.79 = (bf16[8,192,128]{2,1,0:T(8,128)(2,1)}, f32[32,128]{1,0:T(8,128)S(1)}, bf16[128,128]{1,0:T(8,128)(2,1)S(1)}, bf16[128,128]{1,0:T(8,128)(2,1)S(1)}, f32[32,128]{1,0:T(8,128)S(1)}) custom-call(bf16[8,32,128]{2,1,0:T(8,128)(2,1)S(1)} %all-to-all-done.1.got_ref, f32[64,128]{1,0:T(8,128)S(1)} %shard_map.78.fa_ref, ...), custom_call_target="tpu_custom_call" | custom-call | tf_op jit(solution)/shard_map/pallas_call | solution.py:40
  37.1 3.5 %all-to-all-start.2 = ((bf16[8,192,128]{2,1,0:T(8,128)(2,1)}), bf16[8,192,128]{2,1,0:T(8,128)(2,1)S(1)}, u32[]{:S(2)}, u32[]{:S(2)}) async-start(bf16[8,192,128]{2,1,0:T(8,128)(2,1)} %get-tuple-element.23), calls=%async_computation.2 | async-start | bytes 786432 | tf_op jit(solution)/shard_map/all_to_all | solution.py:27
  40.6 1.9 %collective-permute-start = (f32[32,128]{1,0:T(8,128)S(1)}, f32[32,128]{1,0:T(8,128)S(1)}, u32[]{:S(2)}, u32[]{:S(2)}) collective-permute-start(f32[32,128]{1,0:T(8,128)S(1)} %get-tuple-element.24), channel_id=1, source_target_pairs={{0,8},{8,0},{1,9},{9,1},{2,10},{10,2},{3,11},{11,3},{4,12},{12,4},... | collective-permute-start | bytes 49160 | tf_op jit(solution)/shard_map/ppermute | solution.py:31
  42.5 0.8 collective-permute-done
  44.1 3.3 %collective-permute-done.1 = f32[32,128]{1,0:T(8,128)S(1)} collective-permute-done((f32[32,128]{1,0:T(8,128)S(1)}, f32[32,128]{1,0:T(8,128)S(1)}, u32[]{:S(2)}, u32[]{:S(2)}) %collective-permute-start.1) | collective-permute-done | bytes 16416 | tf_op jit(solution)/shard_map/ppermute | solution.py:31
  48.2 3.4 %all-to-all-start.3 = ((bf16[8,160,128]{2,1,0:T(8,128)(2,1)}), bf16[8,160,128]{2,1,0:T(8,128)(2,1)S(1)}, u32[]{:S(2)}, u32[]{:S(2)}) async-start(bf16[8,160,128]{2,1,0:T(8,128)(2,1)} %get-tuple-element.25), calls=%async_computation.3 | async-start | bytes 655360 | tf_op jit(solution)/shard_map/all_to_all | solution.py:27
  51.7 3.1 %collective-permute-start.2 = (f32[64,128]{1,0:T(8,128)S(1)}, f32[64,128]{1,0:T(8,128)S(1)}, u32[]{:S(2)}, u32[]{:S(2)}) collective-permute-start(f32[64,128]{1,0:T(8,128)S(1)} %get-tuple-element.26), channel_id=1, source_target_pairs={{0,8},{8,0},{1,9},{9,1},{2,10},{10,2},{3,11},{11,3},{4,12},{12,4},... | collective-permute-start | bytes 98312 | tf_op jit(solution)/shard_map/ppermute | solution.py:31
  54.8 0.9 collective-permute-done.2
  56.3 3.6 %collective-permute-done.3 = f32[64,128]{1,0:T(8,128)S(1)} collective-permute-done((f32[64,128]{1,0:T(8,128)S(1)}, f32[64,128]{1,0:T(8,128)S(1)}, u32[]{:S(2)}, u32[]{:S(2)}) %collective-permute-start.3) | collective-permute-done | bytes 32800 | tf_op jit(solution)/shard_map/ppermute | solution.py:31
  59.9 1.8 %all-to-all-done.3.got_ref = bf16[8,160,128]{2,1,0:T(8,128)(2,1)S(1)} async-done(((bf16[8,160,128]{2,1,0:T(8,128)(2,1)}), bf16[8,160,128]{2,1,0:T(8,128)(2,1)S(1)}, u32[]{:S(2)}, u32[]{:S(2)}) %all-to-all-start.3) | async-done | bytes 327712 | tf_op jit(solution)/shard_map/all_to_all | solution.py:27
  61.7 1.8 %shard_map.81 = (bf16[8,192,128]{2,1,0:T(8,128)(2,1)}, f32[32,128]{1,0:T(8,128)S(1)}, f32[224,128]{1,0:T(8,128)S(1)}, f32[2048,128]{1,0:T(8,128)S(1)}, f32[8,128]{1,0:T(8,128)S(1)}) custom-call(bf16[8,160,128]{2,1,0:T(8,128)(2,1)S(1)} %all-to-all-done.3.got_ref, f32[64,128]{1,0:T(8,128)S(1)} %add.35.a_sum, bf16[2048,128]{1,0:T(8,128)(2,1)S(1)} %bitcast.14, ...), custom_call_target="tpu_custom_call" | custom-call | tf_op jit(solution)/shard_map/pallas_call | solution.py:40
  63.5 6.2 %all-to-all-start.4 = ((bf16[8,192,128]{2,1,0:T(8,128)(2,1)}), bf16[8,192,128]{2,1,0:T(8,128)(2,1)S(1)}, u32[]{:S(2)}, u32[]{:S(2)}) async-start(bf16[8,192,128]{2,1,0:T(8,128)(2,1)} %get-tuple-element.30), calls=%async_computation.4 | async-start | bytes 786432 | tf_op jit(solution)/shard_map/all_to_all | solution.py:27
  69.7 3.4 %collective-permute-start.4 = (f32[32,128]{1,0:T(8,128)S(1)}, f32[32,128]{1,0:T(8,128)S(1)}, u32[]{:S(2)}, u32[]{:S(2)}) collective-permute-start(f32[32,128]{1,0:T(8,128)S(1)} %get-tuple-element.31), channel_id=1, source_target_pairs={{0,8},{8,0},{1,9},{9,1},{2,10},{10,2},{3,11},{11,3},{4,12},{12,4},... | collective-permute-start | bytes 49160 | tf_op jit(solution)/shard_map/ppermute | solution.py:31
  73.1 0.8 collective-permute-done.4
  74.0 1.0 collective-permute-start.5
  74.9 3.1 %collective-permute-done.5 = f32[32,128]{1,0:T(8,128)S(1)} collective-permute-done((f32[32,128]{1,0:T(8,128)S(1)}, f32[32,128]{1,0:T(8,128)S(1)}, u32[]{:S(2)}, u32[]{:S(2)}) %collective-permute-start.5) | collective-permute-done | bytes 16416 | tf_op jit(solution)/shard_map/ppermute | solution.py:31
  78.8 3.4 %all-to-all-start.5 = ((bf16[8,160,128]{2,1,0:T(8,128)(2,1)}), bf16[8,160,128]{2,1,0:T(8,128)(2,1)S(1)}, u32[]{:S(2)}, u32[]{:S(2)}) async-start(bf16[8,160,128]{2,1,0:T(8,128)(2,1)} %get-tuple-element.32), calls=%async_computation.5 | async-start | bytes 655360 | tf_op jit(solution)/shard_map/all_to_all | solution.py:27
  82.3 3.3 %collective-permute-start.6 = (f32[64,128]{1,0:T(8,128)S(1)}, f32[64,128]{1,0:T(8,128)S(1)}, u32[]{:S(2)}, u32[]{:S(2)}) collective-permute-start(f32[64,128]{1,0:T(8,128)S(1)} %get-tuple-element.33), channel_id=1, source_target_pairs={{0,8},{8,0},{1,9},{9,1},{2,10},{10,2},{3,11},{11,3},{4,12},{12,4},... | collective-permute-start | bytes 98312 | tf_op jit(solution)/shard_map/ppermute | solution.py:31
  85.6 0.9 collective-permute-done.6
  87.2 3.5 %collective-permute-done.7 = f32[64,128]{1,0:T(8,128)S(1)} collective-permute-done((f32[64,128]{1,0:T(8,128)S(1)}, f32[64,128]{1,0:T(8,128)S(1)}, u32[]{:S(2)}, u32[]{:S(2)}) %collective-permute-start.7) | collective-permute-done | bytes 32800 | tf_op jit(solution)/shard_map/ppermute | solution.py:31
  90.7 1.6 %all-to-all-done.5.got_ref = bf16[8,160,128]{2,1,0:T(8,128)(2,1)S(1)} async-done(((bf16[8,160,128]{2,1,0:T(8,128)(2,1)}), bf16[8,160,128]{2,1,0:T(8,128)(2,1)S(1)}, u32[]{:S(2)}, u32[]{:S(2)}) %all-to-all-start.5) | async-done | bytes 327712 | tf_op jit(solution)/shard_map/all_to_all | solution.py:27
  92.3 1.5 %shard_map.83 = (f32[256,1,128]{2,1,0:T(1,128)}, f32[8,128]{1,0:T(8,128)S(1)}, f32[224,128]{1,0:T(8,128)S(1)}) custom-call(bf16[8,160,128]{2,1,0:T(8,128)(2,1)S(1)} %all-to-all-done.5.got_ref, f32[64,128]{1,0:T(8,128)S(1)} %add.39.a_sum, bf16[2048,128]{1,0:T(8,128)(2,1)S(1)} %bitcast.15, f32[64,128]{1,0:T(8,128)S(1)} %shard_map.78.fa_ref, ...), custom_call_target="tpu_custom_call" | custom-call | tf_op jit(solution)/shard_map/pallas_call | solution.py:40
  93.8 10.5 %all-to-all-start.6 = ((f32[256,1,128]{2,1,0:T(1,128)}), f32[256,1,128]{2,1,0:T(1,128)S(1)}, u32[]{:S(2)}, u32[]{:S(2)}) async-start(f32[256,1,128]{2,1,0:T(1,128)} %get-tuple-element.37), calls=%async_computation.6 | async-start | bytes 262144 | tf_op jit(solution)/shard_map/all_to_all | solution.py:27
  104.3 0.9 shard_map.84.columns_ref
  105.2 12.3 %all-to-all-done.6.got_ref = f32[256,1,128]{2,1,0:T(1,128)S(1)} async-done(((f32[256,1,128]{2,1,0:T(1,128)}), f32[256,1,128]{2,1,0:T(1,128)S(1)}, u32[]{:S(2)}, u32[]{:S(2)}) %all-to-all-start.6) | async-done | bytes 131104 | tf_op jit(solution)/shard_map/all_to_all | solution.py:27
  117.5 1.0 shard_map.85
  (27 shorter events, 5.5 us)
Async XLA Ops:
  0.6 0.7 copy-start.1
  0.6 0.7 copy-start
  0.7 0.7 copy-start.2
  2.1 16.3 %all-to-all-start = ((f32[32,8,128]{2,1,0:T(8,128)}), f32[32,8,128]{2,1,0:T(8,128)S(1)}, u32[]{:S(2)}, u32[]{:S(2)}) async-start(f32[32,8,128]{2,1,0:T(8,128)} %shard_map.76), calls=%async_computation | async-start | bytes 262144 | tf_op jit(solution)/shard_map/all_to_all | solution.py:27
  10.7 17.1 %copy-start.3 = (bf16[32,64,128]{2,1,0:T(8,128)(2,1)S(1)}, bf16[32,64,128]{2,1,0:T(8,128)(2,1)}, u32[]{:S(2)}) copy-start(bf16[32,64,128]{2,1,0:T(8,128)(2,1)} %param.5) | copy-start | bytes 1572868
  19.6 15.4 %all-to-all-start.1 = ((bf16[8,32,128]{2,1,0:T(8,128)(2,1)}), bf16[8,32,128]{2,1,0:T(8,128)(2,1)S(1)}, u32[]{:S(2)}, u32[]{:S(2)}) async-start(bf16[8,32,128]{2,1,0:T(8,128)(2,1)} %shard_map.77), calls=%async_computation.1 | async-start | bytes 131072 | tf_op jit(solution)/shard_map/all_to_all | solution.py:27
  37.1 10.3 %all-to-all-start.2 = ((bf16[8,192,128]{2,1,0:T(8,128)(2,1)}), bf16[8,192,128]{2,1,0:T(8,128)(2,1)S(1)}, u32[]{:S(2)}, u32[]{:S(2)}) async-start(bf16[8,192,128]{2,1,0:T(8,128)(2,1)} %get-tuple-element.23), calls=%async_computation.2 | async-start | bytes 786432 | tf_op jit(solution)/shard_map/all_to_all | solution.py:27
  40.6 2.7 %collective-permute-start = (f32[32,128]{1,0:T(8,128)S(1)}, f32[32,128]{1,0:T(8,128)S(1)}, u32[]{:S(2)}, u32[]{:S(2)}) collective-permute-start(f32[32,128]{1,0:T(8,128)S(1)} %get-tuple-element.24), channel_id=1, source_target_pairs={{0,8},{8,0},{1,9},{9,1},{2,10},{10,2},{3,11},{11,3},{4,12},{12,4},... | collective-permute-start | bytes 49160 | tf_op jit(solution)/shard_map/ppermute | solution.py:31
  43.3 4.1 %collective-permute-start.1 = (f32[32,128]{1,0:T(8,128)S(1)}, f32[32,128]{1,0:T(8,128)S(1)}, u32[]{:S(2)}, u32[]{:S(2)}) collective-permute-start(f32[32,128]{1,0:T(8,128)S(1)} %add.32), channel_id=1, source_target_pairs={{0,16},{16,0},{1,17},{17,1},{2,18},{18,2},{3,19},{19,3},{4,20},{20... | collective-permute-start | bytes 49160 | tf_op jit(solution)/shard_map/ppermute | solution.py:31
  48.2 13.5 %all-to-all-start.3 = ((bf16[8,160,128]{2,1,0:T(8,128)(2,1)}), bf16[8,160,128]{2,1,0:T(8,128)(2,1)S(1)}, u32[]{:S(2)}, u32[]{:S(2)}) async-start(bf16[8,160,128]{2,1,0:T(8,128)(2,1)} %get-tuple-element.25), calls=%async_computation.3 | async-start | bytes 655360 | tf_op jit(solution)/shard_map/all_to_all | solution.py:27
  51.7 4.0 %collective-permute-start.2 = (f32[64,128]{1,0:T(8,128)S(1)}, f32[64,128]{1,0:T(8,128)S(1)}, u32[]{:S(2)}, u32[]{:S(2)}) collective-permute-start(f32[64,128]{1,0:T(8,128)S(1)} %get-tuple-element.26), channel_id=1, source_target_pairs={{0,8},{8,0},{1,9},{9,1},{2,10},{10,2},{3,11},{11,3},{4,12},{12,4},... | collective-permute-start | bytes 98312 | tf_op jit(solution)/shard_map/ppermute | solution.py:31
  55.6 4.3 %collective-permute-start.3 = (f32[64,128]{1,0:T(8,128)S(1)}, f32[64,128]{1,0:T(8,128)S(1)}, u32[]{:S(2)}, u32[]{:S(2)}) collective-permute-start(f32[64,128]{1,0:T(8,128)S(1)} %add.34), channel_id=1, source_target_pairs={{0,16},{16,0},{1,17},{17,1},{2,18},{18,2},{3,19},{19,3},{4,20},{20... | collective-permute-start | bytes 98312 | tf_op jit(solution)/shard_map/ppermute | solution.py:31
  63.5 14.5 %all-to-all-start.4 = ((bf16[8,192,128]{2,1,0:T(8,128)(2,1)}), bf16[8,192,128]{2,1,0:T(8,128)(2,1)S(1)}, u32[]{:S(2)}, u32[]{:S(2)}) async-start(bf16[8,192,128]{2,1,0:T(8,128)(2,1)} %get-tuple-element.30), calls=%async_computation.4 | async-start | bytes 786432 | tf_op jit(solution)/shard_map/all_to_all | solution.py:27
  69.7 4.2 %collective-permute-start.4 = (f32[32,128]{1,0:T(8,128)S(1)}, f32[32,128]{1,0:T(8,128)S(1)}, u32[]{:S(2)}, u32[]{:S(2)}) collective-permute-start(f32[32,128]{1,0:T(8,128)S(1)} %get-tuple-element.31), channel_id=1, source_target_pairs={{0,8},{8,0},{1,9},{9,1},{2,10},{10,2},{3,11},{11,3},{4,12},{12,4},... | collective-permute-start | bytes 49160 | tf_op jit(solution)/shard_map/ppermute | solution.py:31
  74.0 4.1 %collective-permute-start.5 = (f32[32,128]{1,0:T(8,128)S(1)}, f32[32,128]{1,0:T(8,128)S(1)}, u32[]{:S(2)}, u32[]{:S(2)}) collective-permute-start(f32[32,128]{1,0:T(8,128)S(1)} %add.36), channel_id=1, source_target_pairs={{0,16},{16,0},{1,17},{17,1},{2,18},{18,2},{3,19},{19,3},{4,20},{20... | collective-permute-start | bytes 49160 | tf_op jit(solution)/shard_map/ppermute | solution.py:31
  78.8 13.5 %all-to-all-start.5 = ((bf16[8,160,128]{2,1,0:T(8,128)(2,1)}), bf16[8,160,128]{2,1,0:T(8,128)(2,1)S(1)}, u32[]{:S(2)}, u32[]{:S(2)}) async-start(bf16[8,160,128]{2,1,0:T(8,128)(2,1)} %get-tuple-element.32), calls=%async_computation.5 | async-start | bytes 655360 | tf_op jit(solution)/shard_map/all_to_all | solution.py:27
  82.3 4.2 %collective-permute-start.6 = (f32[64,128]{1,0:T(8,128)S(1)}, f32[64,128]{1,0:T(8,128)S(1)}, u32[]{:S(2)}, u32[]{:S(2)}) collective-permute-start(f32[64,128]{1,0:T(8,128)S(1)} %get-tuple-element.33), channel_id=1, source_target_pairs={{0,8},{8,0},{1,9},{9,1},{2,10},{10,2},{3,11},{11,3},{4,12},{12,4},... | collective-permute-start | bytes 98312 | tf_op jit(solution)/shard_map/ppermute | solution.py:31
  86.4 4.3 %collective-permute-start.7 = (f32[64,128]{1,0:T(8,128)S(1)}, f32[64,128]{1,0:T(8,128)S(1)}, u32[]{:S(2)}, u32[]{:S(2)}) collective-permute-start(f32[64,128]{1,0:T(8,128)S(1)} %add.38), channel_id=1, source_target_pairs={{0,16},{16,0},{1,17},{17,1},{2,18},{18,2},{3,19},{19,3},{4,20},{20... | collective-permute-start | bytes 98312 | tf_op jit(solution)/shard_map/ppermute | solution.py:31
  93.8 23.7 %all-to-all-start.6 = ((f32[256,1,128]{2,1,0:T(1,128)}), f32[256,1,128]{2,1,0:T(1,128)S(1)}, u32[]{:S(2)}, u32[]{:S(2)}) async-start(f32[256,1,128]{2,1,0:T(1,128)} %get-tuple-element.37), calls=%async_computation.6 | async-start | bytes 262144 | tf_op jit(solution)/shard_map/all_to_all | solution.py:27

commit v5 on v4

--- a/solution.py
+++ b/solution.py
@@ -16,8 +16,6 @@
 DEPTH, HEIGHT, WIDTH, RANK = 32, 64, 128, 128
 CELLS = DEPTH * HEIGHT
 N_Z, N_J, N_K = 8, 4, 8
-EACH = 8
-ROWS = EACH * HEIGHT
 SCALE = 1.0 / 4096.0
 AB = HEIGHT + WIDTH
 BC = WIDTH + DEPTH
@@ -25,6 +23,14 @@
 
 def exchange(blocks, axes):
     return lax.all_to_all(blocks, axes, 0, 0, tiled=True)
+
+
+def position():
+    return (
+        lax.axis_index("ia"),
+        lax.axis_index("ja_0") * 2 + lax.axis_index("ja_1"),
+        lax.axis_index("ka_0") * 2 + lax.axis_index("ka_1"),
+    )
 
 
 def swapped(x, axis):
@@ -41,7 +47,7 @@
         kernel,
         out_shape=[jax.ShapeDtypeStruct(shape, dtype) for shape, dtype in outs],
         in_specs=[
-            pl.BlockSpec(memory_space=pltpu.SMEM if x.dtype == jnp.int32 and x.ndim == 1 else pltpu.VMEM)
+            pl.BlockSpec(memory_space=pltpu.VMEM)
             for x in operands
         ],
         out_specs=[pl.BlockSpec(memory_space=pltpu.VMEM) for _ in outs],
@@ -59,8 +65,8 @@
         sent_ref[peer] = block[...]
 
 
-def repack_kernel(place, got_ref, sent_ref, rows_b, rows_c):
-    jb, kb = place[0], place[2]
+def repack_kernel(got_ref, sent_ref, rows_b, rows_c):
+    _, jb, kb = position()
     for k in range(N_K):
         rows_b[2 * k : 2 * k + 2, :] = got_ref[jb * N_K + k, 4:6, :]
     for j in range(N_J):
@@ -77,19 +83,19 @@
     fa_ref[...] = rows_a[...].T[0:HEIGHT]
 
 
-def in_pairs(k, a, c_ref):
-    return jnp.concatenate([c_ref[pl.ds(k + s, 1), :] * a for s in range(EACH)], axis=0)
-
-
-def weight_of(seen_ref, k):
-    return seen_ref[pl.ds(k * HEIGHT, ROWS), :].astype(F32)
-
-
-def add_products(k, weighted, paired, a, b, c_ref, part_a, part_b, part_c):
-    part_b[...] += lax.dot_general(weighted, paired, (((0,), (0,)), ((), ())), preferred_element_type=F32)
-    mixture = jnp.dot(weighted, b, preferred_element_type=F32)
+def in_pairs(k, each, a, c_ref):
+    return jnp.concatenate([c_ref[pl.ds(k + s, 1), :] * a for s in range(each)], axis=0)
+
+
+def weight_of(seen_ref, k, rows):
+    return seen_ref[pl.ds(k * HEIGHT, rows), :].astype(F32)
+
+
+def add_products(k, weighted, paired, a, bt, c_ref, part_a, part_b, part_c):
+    part_b[...] += lax.dot_general(paired, weighted, (((0,), (0,)), ((), ())), preferred_element_type=F32)
+    mixture = lax.dot_general(weighted, bt, (((1,), (1,)), ((), ())), preferred_element_type=F32)
     total = part_a[...]
-    for s in range(EACH):
+    for s in range(weighted.shape[0] // HEIGHT):
         slab = mixture[s * HEIGHT : (s + 1) * HEIGHT]
         total = total + slab * c_ref[pl.ds(k + s, 1), :]
         part_c[pl.ds(k + s, 1), :] = jnp.sum(slab * a, axis=0, keepdims=True)
@@ -104,23 +110,25 @@
     c_out[...] = part_c[...]
 
 
-def first_kernel(got_ref, fa_ref, values_ref, seen_ref, sent_ref, c_out, fb_ref, fbt_ref, fc_ref, part_a, part_b, part_c):
+def first_kernel(got_ref, fa_ref, values_ref, seen_ref, sent_ref, c_out, fbt_ref, fc_ref, part_a, part_b, part_c):
     c = jnp.concatenate([got_ref[z, 16:32, :].astype(F32) for z in range(N_Z)], axis=0)
     fc_ref[...] = c.T[HEIGHT : HEIGHT + DEPTH]
     bt = jnp.concatenate([got_ref[z, 0:16, :] for z in range(N_Z)], axis=0)
     fbt_ref[...] = bt
-    fb_ref[...] = bt.astype(F32).T.astype(BF16)
     part_a[...] = jnp.zeros_like(part_a)
     part_b[...] = jnp.zeros_like(part_b)
 
-    @pl.loop(0, DEPTH, step=EACH, unroll=True)
+    each = 16
+    rows = each * HEIGHT
+
+    @pl.loop(0, DEPTH, step=each, unroll=True)
     def _(k):
         a = fa_ref[...]
-        paired = in_pairs(k, a, fc_ref).astype(BF16)
+        paired = in_pairs(k, each, a, fc_ref).astype(BF16)
         fitted = jnp.dot(paired, fbt_ref[...], preferred_element_type=F32)
-        values = values_ref[pl.ds(k * HEIGHT, ROWS), :].astype(F32)
-        errors = (values - weight_of(seen_ref, k) * fitted).astype(BF16)
-        add_products(k, errors, paired, a, fb_ref[...], fc_ref, part_a, part_b, part_c)
+        values = values_ref[pl.ds(k * HEIGHT, rows), :].astype(F32)
+        errors = (values - weight_of(seen_ref, k, rows) * fitted).astype(BF16)
+        add_products(k, errors, paired, a, fbt_ref[...], fc_ref, part_a, part_b, part_c)
 
     hand_out(part_a, part_b, part_c, sent_ref, c_out)
 
@@ -145,8 +153,8 @@
     out[HEIGHT : HEIGHT + BC, :] = total
 
 
-def tangent_at(k, paired, fa_ref, fc_ref, fbt_ref, hat_a, hat_bt, hat_c):
-    sideways = (in_pairs(k, fa_ref[...], hat_c) + in_pairs(k, hat_a[...], fc_ref)).astype(BF16)
+def tangent_at(k, each, paired, fa_ref, fc_ref, fbt_ref, hat_a, hat_bt, hat_c):
+    sideways = (in_pairs(k, each, fa_ref[...], hat_c) + in_pairs(k, each, hat_a[...], fc_ref)).astype(BF16)
     return jnp.dot(paired, hat_bt[...], preferred_element_type=F32) + jnp.dot(
         sideways, fbt_ref[...], preferred_element_type=F32
     )
@@ -154,11 +162,11 @@
 
 def round_hats(direction, hat_a, hat_bt, hat_c):
     hat_a[...] = direction[0:HEIGHT].astype(BF16).astype(F32)
-    hat_bt[...] = direction[HEIGHT:AB].T.astype(BF16)
+    hat_bt[...] = direction[HEIGHT:AB].astype(BF16)
     hat_c[...] = direction[AB:].astype(BF16).astype(F32)
 
 
-def second_kernel(got_ref, a_sum, seen_ref, fa_ref, fb_ref, fbt_ref, fc_ref,
+def second_kernel(got_ref, a_sum, seen_ref, fa_ref, fbt_ref, fc_ref,
                   sent_ref, c_out, grad_ref, tangent_ref, sum_ref,
                   part_a, part_b, part_c, hat_a, hat_bt, hat_c):
     take_totals(got_ref, a_sum, grad_ref)
@@ -167,15 +175,18 @@
     part_b[...] = jnp.zeros_like(part_b)
     sum_ref[...] = jnp.zeros_like(sum_ref)
 
-    @pl.loop(0, DEPTH, step=EACH, unroll=True)
+    each = 8
+    rows = each * HEIGHT
+
+    @pl.loop(0, DEPTH, step=each, unroll=True)
     def _(k):
         a = fa_ref[...]
-        paired = in_pairs(k, a, fc_ref).astype(BF16)
-        tangent = tangent_at(k, paired, fa_ref, fc_ref, fbt_ref, hat_a, hat_bt, hat_c)
-        weighted = weight_of(seen_ref, k) * tangent
-        tangent_ref[pl.ds(k * HEIGHT, ROWS), :] = tangent
-        sum_ref[...] += jnp.sum((weighted * tangent).reshape(ROWS // 8, 8, WIDTH), axis=0)
-        add_products(k, weighted.astype(BF16), paired, a, fb_ref[...], fc_ref, part_a, part_b, part_c)
+        paired = in_pairs(k, each, a, fc_ref).astype(BF16)
+        tangent = tangent_at(k, each, paired, fa_ref, fc_ref, fbt_ref, hat_a, hat_bt, hat_c)
+        weighted = weight_of(seen_ref, k, rows) * tangent
+        tangent_ref[pl.ds(k * HEIGHT, rows), :] = tangent
+        sum_ref[...] += jnp.sum((weighted * tangent).reshape(rows // 8, 8, WIDTH), axis=0)
+        add_products(k, weighted.astype(BF16), paired, a, fbt_ref[...], fc_ref, part_a, part_b, part_c)
 
     hand_out(part_a, part_b, part_c, sent_ref, c_out)
 
@@ -204,14 +215,17 @@
     sum_rest[...] = jnp.zeros_like(sum_rest)
     sum_both[...] = jnp.zeros_like(sum_both)
 
-    @pl.loop(0, DEPTH, step=EACH, unroll=True)
+    each = 16
+    rows = each * HEIGHT
+
+    @pl.loop(0, DEPTH, step=each, unroll=True)
     def _(k):
-        paired = in_pairs(k, fa_ref[...], fc_ref).astype(BF16)
-        tangent = tangent_at(k, paired, fa_ref, fc_ref, fbt_ref, hat_a, hat_bt, hat_c)
-        weighted = weight_of(seen_ref, k) * tangent
-        before = tangent_ref[pl.ds(k * HEIGHT, ROWS), :]
-        sum_rest[...] += jnp.sum((weighted * tangent).reshape(ROWS // 8, 8, WIDTH), axis=0)
-        sum_both[...] += jnp.sum((weighted * before).reshape(ROWS // 8, 8, WIDTH), axis=0)
+        paired = in_pairs(k, each, fa_ref[...], fc_ref).astype(BF16)
+        tangent = tangent_at(k, each, paired, fa_ref, fc_ref, fbt_ref, hat_a, hat_bt, hat_c)
+        weighted = weight_of(seen_ref, k, rows) * tangent
+        before = tangent_ref[pl.ds(k * HEIGHT, rows), :]
+        sum_rest[...] += jnp.sum((weighted * tangent).reshape(rows // 8, 8, WIDTH), axis=0)
+        sum_both[...] += jnp.sum((weighted * before).reshape(rows // 8, 8, WIDTH), axis=0)
 
     lane = lax.broadcasted_iota(jnp.int32, (1, 128), 1)
     line = jnp.zeros((1, 128), F32)
@@ -232,14 +246,14 @@
         sent_ref[peer] = line
 
 
-def columns_kernel(place, grad_ref, rest_ref, out_ref):
-    z, jb, kb = place[1], place[0], place[2]
+def columns_kernel(grad_ref, rest_ref, out_ref):
+    z, jb, kb = position()
     for at, x in ((0, grad_ref), (16, rest_ref)):
         rows = pltpu.roll(x[0:HEIGHT, :], (128 - (jb * N_K + kb) * 4) % 128, 1).T
         out_ref[at : at + 4, 0:HEIGHT] = rows[0:4]
         rows = pltpu.roll(x[AB:, :], (128 - (z * N_J + jb) * 4) % 128, 1).T
         out_ref[at : at + 4, HEIGHT : HEIGHT + DEPTH] = rows[0:4]
-        rows = pltpu.roll(x[HEIGHT:AB, :], (128 - (z * N_K + kb) * 2) % 128, 1).T
+        rows = pltpu.roll(x[HEIGHT:AB, :], (128 - (z * N_K + kb) * 2) % 128, 0)
         out_ref[at + 8 : at + 10, :] = rows[0:2]
 
 
@@ -268,8 +282,6 @@
 
 
 def local(tensor, observed, factor_a, factor_b, factor_c):
-    z, jb, kb = lax.axis_index("ia"), lax.axis_index(JA), lax.axis_index(KA)
-    place = jnp.stack([jb, z, kb]).astype(jnp.int32)
     weight = (observed.astype(F32) * SCALE).astype(BF16).reshape(CELLS, WIDTH)
     values = tensor.reshape(CELLS, WIDTH) * weight
     tile = lambda rows: ((rows, RANK), F32)
@@ -280,14 +292,14 @@
         pack_kernel, [((N_J * N_K, 8, 128), F32)], factor_a.T, factor_b.T, factor_c.T, scratch=[tile(8)]
     )
     shards = exchange(sent, PLANE)
-    (sent,) = call(repack_kernel, [((N_Z, 32, 128), BF16)], place, shards, scratch=[tile(16), tile(16)])
+    (sent,) = call(repack_kernel, [((N_Z, 32, 128), BF16)], shards, scratch=[tile(16), tile(16)])
     got = exchange(sent, "ia")
     (fa,) = call(rows_kernel, [tile(HEIGHT)], shards, scratch=[tile(128)])
 
     sent_types = [((N_K, AB, RANK), BF16), tile(DEPTH)]
-    sent, part_c, fb, fbt, fc = call(
+    sent, part_c, fbt, fc = call(
         first_kernel,
-        sent_types + [((WIDTH, RANK), BF16), ((RANK, WIDTH), BF16), tile(DEPTH)],
+        sent_types + [((RANK, WIDTH), BF16), tile(DEPTH)],
         got, fa, values, weight, scratch=sums,
     )
 
@@ -301,14 +313,14 @@
     sent, part_c, grad, tangent, sum_gg = call(
         second_kernel,
         sent_types + [tile(AB + DEPTH), tile(CELLS), tile(8)],
-        *summed(sent, part_c), weight, fa, fb, fbt, fc, scratch=sums + hats,
+        *summed(sent, part_c), weight, fa, fbt, fc, scratch=sums + hats,
     )
     sent, own, rest = call(
         third_kernel,
         [((N_Z * N_J * N_K, 1, 128), F32), tile(8), tile(AB + DEPTH)],
         *summed(sent, part_c), weight, fa, fbt, fc, grad, tangent, sum_gg, scratch=hats + [tile(8), tile(8)],
     )
-    (columns,) = call(columns_kernel, [tile(32)], place, grad, rest)
+    (columns,) = call(columns_kernel, [tile(32)], grad, rest)
     got = exchange(sent, EVERY)
     steps = call(last_kernel, [((4, HEIGHT), F32), ((2, WIDTH), F32), ((4, DEPTH), F32)], got, own, columns)
     return tuple(x.T for x in steps)

time: 119 us -> 118 us (level)
  Pallas kernels: 10.9 us -> 9.11 us
    pallas_call x10, Pallas kernels: 10.9 us -> 9.11 us  [call(): pl.pallas_call(kernel, out_shape=[jax.ShapeDtypeStruct(shape, dtype) for...]
  transfers between devices with their start and end apart: 15 -> 15, of which waited for: 13 -> 13; matrix products, arithmetic and copies ran while one was open for 1% -> 1% of each run, Pallas kernels for 1% -> 0%
where the time goes in v5:
time: 118 us; the launch traced here: 117 us
  starting transfers between devices  58.7 us (50%)
  waiting for transfers between devices  46.6 us (39%)
  Pallas kernels  9.11 us (8%)
  other arithmetic  1.58 us (1%)
    all_to_all x7, starting transfers between devices, exchange(): return lax.all_to_all(blocks, axes, 0, 0, tiled=True)  43.8 us
    all_to_all x7, waiting for transfers between devices, exchange(): return lax.all_to_all(blocks, axes, 0, 0, tiled=True)  29.7 us
    ppermute x8, waiting for transfers between devices, swapped(): return lax.ppermute(x, axis, [(0, 1), (1, 0)])  16.9 us
    ppermute x8, starting transfers between devices, swapped(): return lax.ppermute(x, axis, [(0, 1), (1, 0)])  14.9 us
    pallas_call x10, Pallas kernels, call(): pl.pallas_call(kernel, out_shape=[jax.ShapeDtypeStruct(shape, dtype) for...  9.11 us
  transfers between devices with their start and end apart: 15, of which 13 were waited for; matrix products, arithmetic and copies ran while one was open for 1% of the time, Pallas kernels for 0%

profile of v5, /device:TPU:1, one launch (start us, length us, event | category | flops | bytes accessed | tf_op | source)
XLA Modules:
  0.0 117.4 jit_solution(10379172880660641442)
XLA Ops:
  2.1 8.6 %all-to-all-start = ((f32[32,8,128]{2,1,0:T(8,128)}), f32[32,8,128]{2,1,0:T(8,128)S(1)}, u32[]{:S(2)}, u32[]{:S(2)}) async-start(f32[32,8,128]{2,1,0:T(8,128)} %shard_map.76), calls=%async_computation | async-start | bytes 262144 | tf_op jit(solution)/shard_map/all_to_all | solution.py:25
  10.7 1.4 %multiply_convert_fusion = bf16[32,64,128]{2,1,0:T(8,128)(2,1)S(1)} fusion(s32[32,64,128]{2,1,0:T(8,128)} %param.6), kind=kLoop, calls=%fused_computation | loop fusion | flops 786432 | bytes 1572864 | tf_op jit(solution)/shard_map/convert_element_type | solution.py:285
  12.1 6.3 %all-to-all-done.got_ref = f32[32,8,128]{2,1,0:T(8,128)S(1)} async-done(((f32[32,8,128]{2,1,0:T(8,128)}), f32[32,8,128]{2,1,0:T(8,128)S(1)}, u32[]{:S(2)}, u32[]{:S(2)}) %all-to-all-start) | async-done | bytes 131104 | tf_op jit(solution)/shard_map/all_to_all | solution.py:25
  19.0 8.2 %all-to-all-start.1 = ((bf16[8,32,128]{2,1,0:T(8,128)(2,1)}), bf16[8,32,128]{2,1,0:T(8,128)(2,1)S(1)}, u32[]{:S(2)}, u32[]{:S(2)}) async-start(bf16[8,32,128]{2,1,0:T(8,128)(2,1)} %shard_map.77), calls=%async_computation.1 | async-start | bytes 131072 | tf_op jit(solution)/shard_map/all_to_all | solution.py:25
  27.4 7.0 %all-to-all-done.1.got_ref = bf16[8,32,128]{2,1,0:T(8,128)(2,1)S(1)} async-done(((bf16[8,32,128]{2,1,0:T(8,128)(2,1)}), bf16[8,32,128]{2,1,0:T(8,128)(2,1)S(1)}, u32[]{:S(2)}, u32[]{:S(2)}) %all-to-all-start.1) | async-done | bytes 65568 | tf_op jit(solution)/shard_map/all_to_all | solution.py:25
  34.4 1.7 %shard_map.79 = (bf16[8,192,128]{2,1,0:T(8,128)(2,1)}, f32[32,128]{1,0:T(8,128)S(1)}, bf16[128,128]{1,0:T(8,128)(2,1)S(1)}, f32[32,128]{1,0:T(8,128)S(1)}) custom-call(bf16[8,32,128]{2,1,0:T(8,128)(2,1)S(1)} %all-to-all-done.1.got_ref, f32[64,128]{1,0:T(8,128)S(1)} %shard_map.78.fa_ref, bf16[2048,128]{1,0:T(8,128)(2,1)S(1)} %bitcast_multiply_fusion.values_ref, ...), custom_call_target="tpu_custom_call" | custom-call | tf_op jit(solution)/shard_map/pallas_call | solution.py:46
  36.2 3.5 %all-to-all-start.2 = ((bf16[8,192,128]{2,1,0:T(8,128)(2,1)}), bf16[8,192,128]{2,1,0:T(8,128)(2,1)S(1)}, u32[]{:S(2)}, u32[]{:S(2)}) async-start(bf16[8,192,128]{2,1,0:T(8,128)(2,1)} %get-tuple-element.22), calls=%async_computation.2 | async-start | bytes 786432 | tf_op jit(solution)/shard_map/all_to_all | solution.py:25
  39.6 1.9 %collective-permute-start = (f32[32,128]{1,0:T(8,128)S(1)}, f32[32,128]{1,0:T(8,128)S(1)}, u32[]{:S(2)}, u32[]{:S(2)}) collective-permute-start(f32[32,128]{1,0:T(8,128)S(1)} %get-tuple-element.23), channel_id=1, source_target_pairs={{0,8},{8,0},{1,9},{9,1},{2,10},{10,2},{3,11},{11,3},{4,12},{12,4},... | collective-permute-start | bytes 49160 | tf_op jit(solution)/shard_map/ppermute | solution.py:37
  41.5 0.8 collective-permute-done
  43.1 3.3 %collective-permute-done.1 = f32[32,128]{1,0:T(8,128)S(1)} collective-permute-done((f32[32,128]{1,0:T(8,128)S(1)}, f32[32,128]{1,0:T(8,128)S(1)}, u32[]{:S(2)}, u32[]{:S(2)}) %collective-permute-start.1) | collective-permute-done | bytes 16416 | tf_op jit(solution)/shard_map/ppermute | solution.py:37
  47.3 3.4 %all-to-all-start.3 = ((bf16[8,160,128]{2,1,0:T(8,128)(2,1)}), bf16[8,160,128]{2,1,0:T(8,128)(2,1)S(1)}, u32[]{:S(2)}, u32[]{:S(2)}) async-start(bf16[8,160,128]{2,1,0:T(8,128)(2,1)} %get-tuple-element.24), calls=%async_computation.3 | async-start | bytes 655360 | tf_op jit(solution)/shard_map/all_to_all | solution.py:25
  50.7 3.1 %collective-permute-start.2 = (f32[64,128]{1,0:T(8,128)S(1)}, f32[64,128]{1,0:T(8,128)S(1)}, u32[]{:S(2)}, u32[]{:S(2)}) collective-permute-start(f32[64,128]{1,0:T(8,128)S(1)} %get-tuple-element.25), channel_id=1, source_target_pairs={{0,8},{8,0},{1,9},{9,1},{2,10},{10,2},{3,11},{11,3},{4,12},{12,4},... | collective-permute-start | bytes 98312 | tf_op jit(solution)/shard_map/ppermute | solution.py:37
  53.8 0.9 collective-permute-done.2
  55.4 3.6 %collective-permute-done.3 = f32[64,128]{1,0:T(8,128)S(1)} collective-permute-done((f32[64,128]{1,0:T(8,128)S(1)}, f32[64,128]{1,0:T(8,128)S(1)}, u32[]{:S(2)}, u32[]{:S(2)}) %collective-permute-start.3) | collective-permute-done | bytes 32800 | tf_op jit(solution)/shard_map/ppermute | solution.py:37
  59.0 1.8 %all-to-all-done.3.got_ref = bf16[8,160,128]{2,1,0:T(8,128)(2,1)S(1)} async-done(((bf16[8,160,128]{2,1,0:T(8,128)(2,1)}), bf16[8,160,128]{2,1,0:T(8,128)(2,1)S(1)}, u32[]{:S(2)}, u32[]{:S(2)}) %all-to-all-start.3) | async-done | bytes 327712 | tf_op jit(solution)/shard_map/all_to_all | solution.py:25
  60.8 1.7 %shard_map.81 = (bf16[8,192,128]{2,1,0:T(8,128)(2,1)}, f32[32,128]{1,0:T(8,128)S(1)}, f32[224,128]{1,0:T(8,128)S(1)}, f32[2048,128]{1,0:T(8,128)S(1)}, f32[8,128]{1,0:T(8,128)S(1)}) custom-call(bf16[8,160,128]{2,1,0:T(8,128)(2,1)S(1)} %all-to-all-done.3.got_ref, f32[64,128]{1,0:T(8,128)S(1)} %add.27.a_sum, bf16[2048,128]{1,0:T(8,128)(2,1)S(1)} %bitcast.11, ...), custom_call_target="tpu_custom_call" | custom-call | tf_op jit(solution)/shard_map/pallas_call | solution.py:46
  62.5 6.2 %all-to-all-start.4 = ((bf16[8,192,128]{2,1,0:T(8,128)(2,1)}), bf16[8,192,128]{2,1,0:T(8,128)(2,1)S(1)}, u32[]{:S(2)}, u32[]{:S(2)}) async-start(bf16[8,192,128]{2,1,0:T(8,128)(2,1)} %get-tuple-element.28), calls=%async_computation.4 | async-start | bytes 786432 | tf_op jit(solution)/shard_map/all_to_all | solution.py:25
  68.7 3.4 %collective-permute-start.4 = (f32[32,128]{1,0:T(8,128)S(1)}, f32[32,128]{1,0:T(8,128)S(1)}, u32[]{:S(2)}, u32[]{:S(2)}) collective-permute-start(f32[32,128]{1,0:T(8,128)S(1)} %get-tuple-element.29), channel_id=1, source_target_pairs={{0,8},{8,0},{1,9},{9,1},{2,10},{10,2},{3,11},{11,3},{4,12},{12,4},... | collective-permute-start | bytes 49160 | tf_op jit(solution)/shard_map/ppermute | solution.py:37
  72.1 0.8 collective-permute-done.4
  72.9 1.0 collective-permute-start.5
  73.9 3.1 %collective-permute-done.5 = f32[32,128]{1,0:T(8,128)S(1)} collective-permute-done((f32[32,128]{1,0:T(8,128)S(1)}, f32[32,128]{1,0:T(8,128)S(1)}, u32[]{:S(2)}, u32[]{:S(2)}) %collective-permute-start.5) | collective-permute-done | bytes 16416 | tf_op jit(solution)/shard_map/ppermute | solution.py:37
  77.0 0.8 shard_map.82
  77.8 3.4 %all-to-all-start.5 = ((bf16[8,160,128]{2,1,0:T(8,128)(2,1)}), bf16[8,160,128]{2,1,0:T(8,128)(2,1)S(1)}, u32[]{:S(2)}, u32[]{:S(2)}) async-start(bf16[8,160,128]{2,1,0:T(8,128)(2,1)} %get-tuple-element.30), calls=%async_computation.5 | async-start | bytes 655360 | tf_op jit(solution)/shard_map/all_to_all | solution.py:25
  81.2 3.3 %collective-permute-start.6 = (f32[64,128]{1,0:T(8,128)S(1)}, f32[64,128]{1,0:T(8,128)S(1)}, u32[]{:S(2)}, u32[]{:S(2)}) collective-permute-start(f32[64,128]{1,0:T(8,128)S(1)} %get-tuple-element.31), channel_id=1, source_target_pairs={{0,8},{8,0},{1,9},{9,1},{2,10},{10,2},{3,11},{11,3},{4,12},{12,4},... | collective-permute-start | bytes 98312 | tf_op jit(solution)/shard_map/ppermute | solution.py:37
  84.5 0.9 collective-permute-done.6
  85.4 0.8 collective-permute-start.7
  86.2 3.5 %collective-permute-done.7 = f32[64,128]{1,0:T(8,128)S(1)} collective-permute-done((f32[64,128]{1,0:T(8,128)S(1)}, f32[64,128]{1,0:T(8,128)S(1)}, u32[]{:S(2)}, u32[]{:S(2)}) %collective-permute-start.7) | collective-permute-done | bytes 32800 | tf_op jit(solution)/shard_map/ppermute | solution.py:37
  89.7 1.6 %all-to-all-done.5.got_ref = bf16[8,160,128]{2,1,0:T(8,128)(2,1)S(1)} async-done(((bf16[8,160,128]{2,1,0:T(8,128)(2,1)}), bf16[8,160,128]{2,1,0:T(8,128)(2,1)S(1)}, u32[]{:S(2)}, u32[]{:S(2)}) %all-to-all-start.5) | async-done | bytes 327712 | tf_op jit(solution)/shard_map/all_to_all | solution.py:25
  91.3 1.5 %shard_map.83 = (f32[256,1,128]{2,1,0:T(1,128)}, f32[8,128]{1,0:T(8,128)S(1)}, f32[224,128]{1,0:T(8,128)S(1)}) custom-call(bf16[8,160,128]{2,1,0:T(8,128)(2,1)S(1)} %all-to-all-done.5.got_ref, f32[64,128]{1,0:T(8,128)S(1)} %add.31.a_sum, bf16[2048,128]{1,0:T(8,128)(2,1)S(1)} %bitcast.12, f32[64,128]{1,0:T(8,128)S(1)} %shard_map.78.fa_ref, ...), custom_call_target="tpu_custom_call" | custom-call | tf_op jit(solution)/shard_map/pallas_call | solution.py:46
  92.7 10.5 %all-to-all-start.6 = ((f32[256,1,128]{2,1,0:T(1,128)}), f32[256,1,128]{2,1,0:T(1,128)S(1)}, u32[]{:S(2)}, u32[]{:S(2)}) async-start(f32[256,1,128]{2,1,0:T(1,128)} %get-tuple-element.35), calls=%async_computation.6 | async-start | bytes 262144 | tf_op jit(solution)/shard_map/all_to_all | solution.py:25
  103.5 13.0 %all-to-all-done.6.got_ref = f32[256,1,128]{2,1,0:T(1,128)S(1)} async-done(((f32[256,1,128]{2,1,0:T(1,128)}), f32[256,1,128]{2,1,0:T(1,128)S(1)}, u32[]{:S(2)}, u32[]{:S(2)}) %all-to-all-start.6) | async-done | bytes 131104 | tf_op jit(solution)/shard_map/all_to_all | solution.py:25
  116.4 1.0 shard_map.85
  (26 shorter events, 4.7 us)
Async XLA Ops:
  0.6 0.7 copy-start.1
  0.6 0.7 copy-start
  0.7 0.7 copy-start.2
  2.1 16.3 %all-to-all-start = ((f32[32,8,128]{2,1,0:T(8,128)}), f32[32,8,128]{2,1,0:T(8,128)S(1)}, u32[]{:S(2)}, u32[]{:S(2)}) async-start(f32[32,8,128]{2,1,0:T(8,128)} %shard_map.76), calls=%async_computation | async-start | bytes 262144 | tf_op jit(solution)/shard_map/all_to_all | solution.py:25
  10.7 16.5 %copy-start.3 = (bf16[32,64,128]{2,1,0:T(8,128)(2,1)S(1)}, bf16[32,64,128]{2,1,0:T(8,128)(2,1)}, u32[]{:S(2)}) copy-start(bf16[32,64,128]{2,1,0:T(8,128)(2,1)} %param.5) | copy-start | bytes 1572868
  19.0 15.4 %all-to-all-start.1 = ((bf16[8,32,128]{2,1,0:T(8,128)(2,1)}), bf16[8,32,128]{2,1,0:T(8,128)(2,1)S(1)}, u32[]{:S(2)}, u32[]{:S(2)}) async-start(bf16[8,32,128]{2,1,0:T(8,128)(2,1)} %shard_map.77), calls=%async_computation.1 | async-start | bytes 131072 | tf_op jit(solution)/shard_map/all_to_all | solution.py:25
  36.2 10.3 %all-to-all-start.2 = ((bf16[8,192,128]{2,1,0:T(8,128)(2,1)}), bf16[8,192,128]{2,1,0:T(8,128)(2,1)S(1)}, u32[]{:S(2)}, u32[]{:S(2)}) async-start(bf16[8,192,128]{2,1,0:T(8,128)(2,1)} %get-tuple-element.22), calls=%async_computation.2 | async-start | bytes 786432 | tf_op jit(solution)/shard_map/all_to_all | solution.py:25
  39.6 2.7 %collective-permute-start = (f32[32,128]{1,0:T(8,128)S(1)}, f32[32,128]{1,0:T(8,128)S(1)}, u32[]{:S(2)}, u32[]{:S(2)}) collective-permute-start(f32[32,128]{1,0:T(8,128)S(1)} %get-tuple-element.23), channel_id=1, source_target_pairs={{0,8},{8,0},{1,9},{9,1},{2,10},{10,2},{3,11},{11,3},{4,12},{12,4},... | collective-permute-start | bytes 49160 | tf_op jit(solution)/shard_map/ppermute | solution.py:37
  42.4 4.1 %collective-permute-start.1 = (f32[32,128]{1,0:T(8,128)S(1)}, f32[32,128]{1,0:T(8,128)S(1)}, u32[]{:S(2)}, u32[]{:S(2)}) collective-permute-start(f32[32,128]{1,0:T(8,128)S(1)} %add.24), channel_id=1, source_target_pairs={{0,16},{16,0},{1,17},{17,1},{2,18},{18,2},{3,19},{19,3},{4,20},{20... | collective-permute-start | bytes 49160 | tf_op jit(solution)/shard_map/ppermute | solution.py:37
  47.3 13.5 %all-to-all-start.3 = ((bf16[8,160,128]{2,1,0:T(8,128)(2,1)}), bf16[8,160,128]{2,1,0:T(8,128)(2,1)S(1)}, u32[]{:S(2)}, u32[]{:S(2)}) async-start(bf16[8,160,128]{2,1,0:T(8,128)(2,1)} %get-tuple-element.24), calls=%async_computation.3 | async-start | bytes 655360 | tf_op jit(solution)/shard_map/all_to_all | solution.py:25
  50.7 4.0 %collective-permute-start.2 = (f32[64,128]{1,0:T(8,128)S(1)}, f32[64,128]{1,0:T(8,128)S(1)}, u32[]{:S(2)}, u32[]{:S(2)}) collective-permute-start(f32[64,128]{1,0:T(8,128)S(1)} %get-tuple-element.25), channel_id=1, source_target_pairs={{0,8},{8,0},{1,9},{9,1},{2,10},{10,2},{3,11},{11,3},{4,12},{12,4},... | collective-permute-start | bytes 98312 | tf_op jit(solution)/shard_map/ppermute | solution.py:37
  54.7 4.3 %collective-permute-start.3 = (f32[64,128]{1,0:T(8,128)S(1)}, f32[64,128]{1,0:T(8,128)S(1)}, u32[]{:S(2)}, u32[]{:S(2)}) collective-permute-start(f32[64,128]{1,0:T(8,128)S(1)} %add.26), channel_id=1, source_target_pairs={{0,16},{16,0},{1,17},{17,1},{2,18},{18,2},{3,19},{19,3},{4,20},{20... | collective-permute-start | bytes 98312 | tf_op jit(solution)/shard_map/ppermute | solution.py:37
  62.5 14.5 %all-to-all-start.4 = ((bf16[8,192,128]{2,1,0:T(8,128)(2,1)}), bf16[8,192,128]{2,1,0:T(8,128)(2,1)S(1)}, u32[]{:S(2)}, u32[]{:S(2)}) async-start(bf16[8,192,128]{2,1,0:T(8,128)(2,1)} %get-tuple-element.28), calls=%async_computation.4 | async-start | bytes 786432 | tf_op jit(solution)/shard_map/all_to_all | solution.py:25
  68.7 4.2 %collective-permute-start.4 = (f32[32,128]{1,0:T(8,128)S(1)}, f32[32,128]{1,0:T(8,128)S(1)}, u32[]{:S(2)}, u32[]{:S(2)}) collective-permute-start(f32[32,128]{1,0:T(8,128)S(1)} %get-tuple-element.29), channel_id=1, source_target_pairs={{0,8},{8,0},{1,9},{9,1},{2,10},{10,2},{3,11},{11,3},{4,12},{12,4},... | collective-permute-start | bytes 49160 | tf_op jit(solution)/shard_map/ppermute | solution.py:37
  72.9 4.1 %collective-permute-start.5 = (f32[32,128]{1,0:T(8,128)S(1)}, f32[32,128]{1,0:T(8,128)S(1)}, u32[]{:S(2)}, u32[]{:S(2)}) collective-permute-start(f32[32,128]{1,0:T(8,128)S(1)} %add.28), channel_id=1, source_target_pairs={{0,16},{16,0},{1,17},{17,1},{2,18},{18,2},{3,19},{19,3},{4,20},{20... | collective-permute-start | bytes 49160 | tf_op jit(solution)/shard_map/ppermute | solution.py:37
  77.8 13.5 %all-to-all-start.5 = ((bf16[8,160,128]{2,1,0:T(8,128)(2,1)}), bf16[8,160,128]{2,1,0:T(8,128)(2,1)S(1)}, u32[]{:S(2)}, u32[]{:S(2)}) async-start(bf16[8,160,128]{2,1,0:T(8,128)(2,1)} %get-tuple-element.30), calls=%async_computation.5 | async-start | bytes 655360 | tf_op jit(solution)/shard_map/all_to_all | solution.py:25
  81.2 4.2 %collective-permute-start.6 = (f32[64,128]{1,0:T(8,128)S(1)}, f32[64,128]{1,0:T(8,128)S(1)}, u32[]{:S(2)}, u32[]{:S(2)}) collective-permute-start(f32[64,128]{1,0:T(8,128)S(1)} %get-tuple-element.31), channel_id=1, source_target_pairs={{0,8},{8,0},{1,9},{9,1},{2,10},{10,2},{3,11},{11,3},{4,12},{12,4},... | collective-permute-start | bytes 98312 | tf_op jit(solution)/shard_map/ppermute | solution.py:37
  85.4 4.3 %collective-permute-start.7 = (f32[64,128]{1,0:T(8,128)S(1)}, f32[64,128]{1,0:T(8,128)S(1)}, u32[]{:S(2)}, u32[]{:S(2)}) collective-permute-start(f32[64,128]{1,0:T(8,128)S(1)} %add.30), channel_id=1, source_target_pairs={{0,16},{16,0},{1,17},{17,1},{2,18},{18,2},{3,19},{19,3},{4,20},{20... | collective-permute-start | bytes 98312 | tf_op jit(solution)/shard_map/ppermute | solution.py:37
  92.7 23.7 %all-to-all-start.6 = ((f32[256,1,128]{2,1,0:T(1,128)}), f32[256,1,128]{2,1,0:T(1,128)S(1)}, u32[]{:S(2)}, u32[]{:S(2)}) async-start(f32[256,1,128]{2,1,0:T(1,128)} %get-tuple-element.35), calls=%async_computation.6 | async-start | bytes 262144 | tf_op jit(solution)/shard_map/all_to_all | solution.py:25

commit v6 on v5

--- a/solution.py
+++ b/solution.py
@@ -62,15 +62,15 @@
     block[0:4, HEIGHT : HEIGHT + DEPTH] = ct_ref[...].astype(F32)
     block[4:6, :] = bt_ref[...].astype(F32)
     for peer in range(N_J * N_K):
-        sent_ref[peer] = block[...]
+        sent_ref[peer] = block[...].astype(BF16)
 
 
 def repack_kernel(got_ref, sent_ref, rows_b, rows_c):
     _, jb, kb = position()
     for k in range(N_K):
-        rows_b[2 * k : 2 * k + 2, :] = got_ref[jb * N_K + k, 4:6, :]
+        rows_b[2 * k : 2 * k + 2, :] = got_ref[jb * N_K + k].astype(F32)[4:6]
     for j in range(N_J):
-        rows_c[4 * j : 4 * j + 4, :] = got_ref[j * N_K + kb, 0:4, :]
+        rows_c[4 * j : 4 * j + 4, :] = got_ref[j * N_K + kb].astype(F32)[0:4]
     b, c = rows_b[...].astype(BF16), rows_c[...].astype(BF16)
     for peer in range(N_Z):
         sent_ref[peer, 0:16, :] = b
@@ -79,7 +79,7 @@
 
 def rows_kernel(got_ref, fa_ref, rows_a):
     for peer in range(N_J * N_K):
-        rows_a[4 * peer : 4 * peer + 4, :] = got_ref[peer, 0:4, :]
+        rows_a[4 * peer : 4 * peer + 4, :] = got_ref[peer].astype(F32)[0:4]
     fa_ref[...] = rows_a[...].T[0:HEIGHT]
 
 
@@ -166,7 +166,7 @@
     hat_c[...] = direction[AB:].astype(BF16).astype(F32)
 
 
-def second_kernel(got_ref, a_sum, seen_ref, fa_ref, fbt_ref, fc_ref,
+def second_kernel(got_ref, a_sum, pairs_ref, seen_ref, fa_ref, fbt_ref, fc_ref,
                   sent_ref, c_out, grad_ref, tangent_ref, sum_ref,
                   part_a, part_b, part_c, hat_a, hat_bt, hat_c):
     take_totals(got_ref, a_sum, grad_ref)
@@ -181,7 +181,7 @@
     @pl.loop(0, DEPTH, step=each, unroll=True)
     def _(k):
         a = fa_ref[...]
-        paired = in_pairs(k, each, a, fc_ref).astype(BF16)
+        paired = pairs_ref[pl.ds(k * HEIGHT, rows), :]
         tangent = tangent_at(k, each, paired, fa_ref, fc_ref, fbt_ref, hat_a, hat_bt, hat_c)
         weighted = weight_of(seen_ref, k, rows) * tangent
         tangent_ref[pl.ds(k * HEIGHT, rows), :] = tangent
@@ -203,7 +203,7 @@
     )
 
 
-def third_kernel(got_ref, a_sum, seen_ref, fa_ref, fbt_ref, fc_ref, grad_ref, tangent_ref, sum_ref,
+def third_kernel(got_ref, a_sum, pairs_ref, seen_ref, fa_ref, fbt_ref, fc_ref, grad_ref, tangent_ref, sum_ref,
                  sent_ref, own_ref, rest_ref, hat_a, hat_bt, hat_c, sum_rest, sum_both):
     take_totals(got_ref, a_sum, rest_ref)
     grad, product = grad_ref[...], rest_ref[...]
@@ -220,7 +220,7 @@
 
     @pl.loop(0, DEPTH, step=each, unroll=True)
     def _(k):
-        paired = in_pairs(k, each, fa_ref[...], fc_ref).astype(BF16)
+        paired = pairs_ref[pl.ds(k * HEIGHT, rows), :]
         tangent = tangent_at(k, each, paired, fa_ref, fc_ref, fbt_ref, hat_a, hat_bt, hat_c)
         weighted = weight_of(seen_ref, k, rows) * tangent
         before = tangent_ref[pl.ds(k * HEIGHT, rows), :]
@@ -246,18 +246,31 @@
         sent_ref[peer] = line
 
 
-def columns_kernel(grad_ref, rest_ref, out_ref):
+def take_columns(x, out_ref):
     z, jb, kb = position()
-    for at, x in ((0, grad_ref), (16, rest_ref)):
-        rows = pltpu.roll(x[0:HEIGHT, :], (128 - (jb * N_K + kb) * 4) % 128, 1).T
-        out_ref[at : at + 4, 0:HEIGHT] = rows[0:4]
-        rows = pltpu.roll(x[AB:, :], (128 - (z * N_J + jb) * 4) % 128, 1).T
-        out_ref[at : at + 4, HEIGHT : HEIGHT + DEPTH] = rows[0:4]
-        rows = pltpu.roll(x[HEIGHT:AB, :], (128 - (z * N_K + kb) * 2) % 128, 0)
-        out_ref[at + 8 : at + 10, :] = rows[0:2]
-
-
-def last_kernel(got_ref, own_ref, columns_ref, a_ref, b_ref, c_ref):
+    rows = pltpu.roll(x[0:HEIGHT, :], (128 - (jb * N_K + kb) * 4) % 128, 1).T
+    out_ref[0:4, 0:HEIGHT] = rows[0:4]
+    rows = pltpu.roll(x[AB:, :], (128 - (z * N_J + jb) * 4) % 128, 1).T
+    out_ref[0:4, HEIGHT : HEIGHT + DEPTH] = rows[0:4]
+    out_ref[8:10, :] = pltpu.roll(x[HEIGHT:AB, :], (128 - (z * N_K + kb) * 2) % 128, 0)[0:2]
+
+
+def columns_kernel(rest_ref, out_ref):
+    take_columns(rest_ref, out_ref)
+
+
+def add_pairs_kernel(x_ref, y_ref, fa_ref, fc_ref, sum_ref, pairs_ref):
+    sum_ref[...] = x_ref[...] + y_ref[...]
+    for k in range(0, DEPTH, 8):
+        pairs_ref[k * HEIGHT : (k + 8) * HEIGHT, :] = in_pairs(k, 8, fa_ref[...], fc_ref).astype(BF16)
+
+
+def add_columns_kernel(x_ref, y_ref, grad_ref, sum_ref, out_ref):
+    sum_ref[...] = x_ref[...] + y_ref[...]
+    take_columns(grad_ref, out_ref)
+
+
+def last_kernel(got_ref, own_ref, grad_ref, rest_ref, a_ref, b_ref, c_ref):
     table = got_ref[:, 0, :].T
     level, gg, gv, vv, s_gg, s_gv, s_vv = (table[i : i + 1] for i in range(7))
 
@@ -275,7 +288,7 @@
     curve = (s_rr + rr) + 2.0 * beta * (s_rg + rg) + beta * beta * (norm_seen + norm)
     step = rr / curve
     own_near = 1.0 - alpha * (1.0 + own_ref[0:1, 0:1])
-    x = (alpha + step * (own_near + beta)) * columns_ref[0:16, :] - (step * alpha) * columns_ref[16:32, :]
+    x = (alpha + step * (own_near + beta)) * grad_ref[...] - (step * alpha) * rest_ref[...]
     a_ref[...] = x[0:4, 0:HEIGHT]
     c_ref[...] = x[0:4, HEIGHT : HEIGHT + DEPTH]
     b_ref[...] = x[8:10, :]
@@ -289,7 +302,7 @@
     hats = [tile(HEIGHT), ((RANK, WIDTH), BF16), tile(DEPTH)]
 
     (sent,) = call(
-        pack_kernel, [((N_J * N_K, 8, 128), F32)], factor_a.T, factor_b.T, factor_c.T, scratch=[tile(8)]
+        pack_kernel, [((N_J * N_K, 8, 128), BF16)], factor_a.T, factor_b.T, factor_c.T, scratch=[tile(8)]
     )
     shards = exchange(sent, PLANE)
     (sent,) = call(repack_kernel, [((N_Z, 32, 128), BF16)], shards, scratch=[tile(16), tile(16)])
@@ -303,26 +316,29 @@
         got, fa, values, weight, scratch=sums,
     )
 
-    def summed(sent, part_c):
+    def summed(sent, part_c, add, extra, *operands):
         got = exchange(sent, KA)
         sent, part_a = call(
             middle_kernel, [((N_Z, BC, RANK), BF16), tile(HEIGHT)], got, over_ja(part_c)
         )
-        return exchange(sent, "ia"), over_ja(part_a)
-
+        part_a, made = call(add, [tile(HEIGHT), extra], part_a, swapped(part_a, "ja_1"), *operands)
+        return exchange(sent, "ia"), part_a + swapped(part_a, "ja_0"), made
+
+    got, a_sum, pairs = summed(sent, part_c, add_pairs_kernel, ((CELLS, RANK), BF16), fa, fc)
     sent, part_c, grad, tangent, sum_gg = call(
         second_kernel,
         sent_types + [tile(AB + DEPTH), tile(CELLS), tile(8)],
-        *summed(sent, part_c), weight, fa, fbt, fc, scratch=sums + hats,
-    )
+        got, a_sum, pairs, weight, fa, fbt, fc, scratch=sums + hats,
+    )
+    got, a_sum, columns_g = summed(sent, part_c, add_columns_kernel, tile(16), grad)
     sent, own, rest = call(
         third_kernel,
         [((N_Z * N_J * N_K, 1, 128), F32), tile(8), tile(AB + DEPTH)],
-        *summed(sent, part_c), weight, fa, fbt, fc, grad, tangent, sum_gg, scratch=hats + [tile(8), tile(8)],
-    )
-    (columns,) = call(columns_kernel, [tile(32)], grad, rest)
+        got, a_sum, pairs, weight, fa, fbt, fc, grad, tangent, sum_gg, scratch=hats + [tile(8), tile(8)],
+    )
+    (columns_r,) = call(columns_kernel, [tile(16)], rest)
     got = exchange(sent, EVERY)
-    steps = call(last_kernel, [((4, HEIGHT), F32), ((2, WIDTH), F32), ((4, DEPTH), F32)], got, own, columns)
+    steps = call(last_kernel, [((4, HEIGHT), F32), ((2, WIDTH), F32), ((4, DEPTH), F32)], got, own, columns_g, columns_r)
     return tuple(x.T for x in steps)
 
 

time: 118 us -> 118 us (level)
    pallas_call x10 -> x12, Pallas kernels: 9.11 us -> 9.28 us  [call(): pl.pallas_call(kernel, out_shape=[jax.ShapeDtypeStruct(shape, dtype) for...]
where the time goes in v6:
time: 118 us; the launch traced here: 117 us
  starting transfers between devices  58.9 us (50%)
  waiting for transfers between devices  45.9 us (39%)
  Pallas kernels  9.28 us (8%)
  other arithmetic  1.57 us (1%)
    all_to_all x7, starting transfers between devices, exchange(): return lax.all_to_all(blocks, axes, 0, 0, tiled=True)  43.8 us
    all_to_all x7, waiting for transfers between devices, exchange(): return lax.all_to_all(blocks, axes, 0, 0, tiled=True)  29 us
    ppermute x8, waiting for transfers between devices, swapped(): return lax.ppermute(x, axis, [(0, 1), (1, 0)])  16.8 us
    ppermute x8, starting transfers between devices, swapped(): return lax.ppermute(x, axis, [(0, 1), (1, 0)])  15.1 us
    pallas_call x12, Pallas kernels, call(): pl.pallas_call(kernel, out_shape=[jax.ShapeDtypeStruct(shape, dtype) for...  9.28 us
  transfers between devices with their start and end apart: 15, of which 13 were waited for; matrix products, arithmetic and copies ran while one was open for 1% of the time, Pallas kernels for 0%

profile of v6, /device:TPU:1, one launch (start us, length us, event | category | flops | bytes accessed | tf_op | source)
XLA Modules:
  0.0 117.0 jit_solution(16506461838538509469)
XLA Ops:
  2.0 8.6 %all-to-all-start = ((bf16[32,8,128]{2,1,0:T(8,128)(2,1)}), bf16[32,8,128]{2,1,0:T(8,128)(2,1)S(1)}, u32[]{:S(2)}, u32[]{:S(2)}) async-start(bf16[32,8,128]{2,1,0:T(8,128)(2,1)} %shard_map.76), calls=%async_computation | async-start | bytes 131072 | tf_op jit(solution)/shard_map/all_to_all | solution.py:25
  10.6 1.4 %multiply_convert_fusion = bf16[32,64,128]{2,1,0:T(8,128)(2,1)S(1)} fusion(s32[32,64,128]{2,1,0:T(8,128)} %param.6), kind=kLoop, calls=%fused_computation | loop fusion | flops 786432 | bytes 1572864 | tf_op jit(solution)/shard_map/convert_element_type | solution.py:298
  12.1 5.9 %all-to-all-done.got_ref = bf16[32,8,128]{2,1,0:T(8,128)(2,1)S(1)} async-done(((bf16[32,8,128]{2,1,0:T(8,128)(2,1)}), bf16[32,8,128]{2,1,0:T(8,128)(2,1)S(1)}, u32[]{:S(2)}, u32[]{:S(2)}) %all-to-all-start) | async-done | bytes 65568 | tf_op jit(solution)/shard_map/all_to_all | solution.py:25
  18.6 8.2 %all-to-all-start.1 = ((bf16[8,32,128]{2,1,0:T(8,128)(2,1)}), bf16[8,32,128]{2,1,0:T(8,128)(2,1)S(1)}, u32[]{:S(2)}, u32[]{:S(2)}) async-start(bf16[8,32,128]{2,1,0:T(8,128)(2,1)} %shard_map.77), calls=%async_computation.1 | async-start | bytes 131072 | tf_op jit(solution)/shard_map/all_to_all | solution.py:25
  27.0 7.0 %all-to-all-done.1.got_ref = bf16[8,32,128]{2,1,0:T(8,128)(2,1)S(1)} async-done(((bf16[8,32,128]{2,1,0:T(8,128)(2,1)}), bf16[8,32,128]{2,1,0:T(8,128)(2,1)S(1)}, u32[]{:S(2)}, u32[]{:S(2)}) %all-to-all-start.1) | async-done | bytes 65568 | tf_op jit(solution)/shard_map/all_to_all | solution.py:25
  34.1 1.7 %shard_map.79 = (bf16[8,192,128]{2,1,0:T(8,128)(2,1)}, f32[32,128]{1,0:T(8,128)S(1)}, bf16[128,128]{1,0:T(8,128)(2,1)S(1)}, f32[32,128]{1,0:T(8,128)S(1)}) custom-call(bf16[8,32,128]{2,1,0:T(8,128)(2,1)S(1)} %all-to-all-done.1.got_ref, f32[64,128]{1,0:T(8,128)S(1)} %shard_map.78.fa_ref, bf16[2048,128]{1,0:T(8,128)(2,1)S(1)} %bitcast_multiply_fusion.values_ref, ...), custom_call_target="tpu_custom_call" | custom-call | tf_op jit(solution)/shard_map/pallas_call | solution.py:46
  35.8 3.5 %all-to-all-start.2 = ((bf16[8,192,128]{2,1,0:T(8,128)(2,1)}), bf16[8,192,128]{2,1,0:T(8,128)(2,1)S(1)}, u32[]{:S(2)}, u32[]{:S(2)}) async-start(bf16[8,192,128]{2,1,0:T(8,128)(2,1)} %get-tuple-element.26), calls=%async_computation.2 | async-start | bytes 786432 | tf_op jit(solution)/shard_map/all_to_all | solution.py:25
  39.2 1.9 %collective-permute-start = (f32[32,128]{1,0:T(8,128)S(1)}, f32[32,128]{1,0:T(8,128)S(1)}, u32[]{:S(2)}, u32[]{:S(2)}) collective-permute-start(f32[32,128]{1,0:T(8,128)S(1)} %get-tuple-element.27), channel_id=1, source_target_pairs={{0,8},{8,0},{1,9},{9,1},{2,10},{10,2},{3,11},{11,3},{4,12},{12,4},... | collective-permute-start | bytes 49160 | tf_op jit(solution)/shard_map/ppermute | solution.py:37
  41.1 0.8 collective-permute-done
  42.0 0.8 collective-permute-start.1
  42.8 3.3 %collective-permute-done.1 = f32[32,128]{1,0:T(8,128)S(1)} collective-permute-done((f32[32,128]{1,0:T(8,128)S(1)}, f32[32,128]{1,0:T(8,128)S(1)}, u32[]{:S(2)}, u32[]{:S(2)}) %collective-permute-start.1) | collective-permute-done | bytes 16416 | tf_op jit(solution)/shard_map/ppermute | solution.py:37
  46.9 3.4 %all-to-all-start.3 = ((bf16[8,160,128]{2,1,0:T(8,128)(2,1)}), bf16[8,160,128]{2,1,0:T(8,128)(2,1)S(1)}, u32[]{:S(2)}, u32[]{:S(2)}) async-start(bf16[8,160,128]{2,1,0:T(8,128)(2,1)} %get-tuple-element.28), calls=%async_computation.3 | async-start | bytes 655360 | tf_op jit(solution)/shard_map/all_to_all | solution.py:25
  50.3 3.1 %collective-permute-start.2 = (f32[64,128]{1,0:T(8,128)S(1)}, f32[64,128]{1,0:T(8,128)S(1)}, u32[]{:S(2)}, u32[]{:S(2)}) collective-permute-start(f32[64,128]{1,0:T(8,128)S(1)} %get-tuple-element.29.x_ref), channel_id=1, source_target_pairs={{0,8},{8,0},{1,9},{9,1},{2,10},{10,2},{3,11},{11,3},{4,12},{12,4},... | collective-permute-start | bytes 98312 | tf_op jit(solution)/shard_map/ppermute | solution.py:37
  53.4 0.9 collective-permute-done.2.y_ref
  55.1 3.6 %collective-permute-done.3 = f32[64,128]{1,0:T(8,128)S(1)} collective-permute-done((f32[64,128]{1,0:T(8,128)S(1)}, f32[64,128]{1,0:T(8,128)S(1)}, u32[]{:S(2)}, u32[]{:S(2)}) %collective-permute-start.3) | collective-permute-done | bytes 32800 | tf_op jit(solution)/shard_map/ppermute | solution.py:37
  58.7 1.7 %all-to-all-done.3.got_ref = bf16[8,160,128]{2,1,0:T(8,128)(2,1)S(1)} async-done(((bf16[8,160,128]{2,1,0:T(8,128)(2,1)}), bf16[8,160,128]{2,1,0:T(8,128)(2,1)S(1)}, u32[]{:S(2)}, u32[]{:S(2)}) %all-to-all-start.3) | async-done | bytes 327712 | tf_op jit(solution)/shard_map/all_to_all | solution.py:25
  60.4 1.7 %shard_map.82 = (bf16[8,192,128]{2,1,0:T(8,128)(2,1)}, f32[32,128]{1,0:T(8,128)S(1)}, f32[224,128]{1,0:T(8,128)S(1)}, f32[2048,128]{1,0:T(8,128)S(1)}, f32[8,128]{1,0:T(8,128)S(1)}) custom-call(bf16[8,160,128]{2,1,0:T(8,128)(2,1)S(1)} %all-to-all-done.3.got_ref, f32[64,128]{1,0:T(8,128)S(1)} %add.20.a_sum, ...), custom_call_target="tpu_custom_call" | custom-call | tf_op jit(solution)/shard_map/pallas_call | solution.py:46
  62.0 6.2 %all-to-all-start.4 = ((bf16[8,192,128]{2,1,0:T(8,128)(2,1)}), bf16[8,192,128]{2,1,0:T(8,128)(2,1)S(1)}, u32[]{:S(2)}, u32[]{:S(2)}) async-start(bf16[8,192,128]{2,1,0:T(8,128)(2,1)} %get-tuple-element.34), calls=%async_computation.4 | async-start | bytes 786432 | tf_op jit(solution)/shard_map/all_to_all | solution.py:25
  68.2 3.4 %collective-permute-start.4 = (f32[32,128]{1,0:T(8,128)S(1)}, f32[32,128]{1,0:T(8,128)S(1)}, u32[]{:S(2)}, u32[]{:S(2)}) collective-permute-start(f32[32,128]{1,0:T(8,128)S(1)} %get-tuple-element.35), channel_id=1, source_target_pairs={{0,8},{8,0},{1,9},{9,1},{2,10},{10,2},{3,11},{11,3},{4,12},{12,4},... | collective-permute-start | bytes 49160 | tf_op jit(solution)/shard_map/ppermute | solution.py:37
  71.6 0.8 collective-permute-done.4
  72.5 1.0 collective-permute-start.5
  73.5 3.1 %collective-permute-done.5 = f32[32,128]{1,0:T(8,128)S(1)} collective-permute-done((f32[32,128]{1,0:T(8,128)S(1)}, f32[32,128]{1,0:T(8,128)S(1)}, u32[]{:S(2)}, u32[]{:S(2)}) %collective-permute-start.5) | collective-permute-done | bytes 16416 | tf_op jit(solution)/shard_map/ppermute | solution.py:37
  77.4 3.4 %all-to-all-start.5 = ((bf16[8,160,128]{2,1,0:T(8,128)(2,1)}), bf16[8,160,128]{2,1,0:T(8,128)(2,1)S(1)}, u32[]{:S(2)}, u32[]{:S(2)}) async-start(bf16[8,160,128]{2,1,0:T(8,128)(2,1)} %get-tuple-element.36), calls=%async_computation.5 | async-start | bytes 655360 | tf_op jit(solution)/shard_map/all_to_all | solution.py:25
  80.8 3.3 %collective-permute-start.6 = (f32[64,128]{1,0:T(8,128)S(1)}, f32[64,128]{1,0:T(8,128)S(1)}, u32[]{:S(2)}, u32[]{:S(2)}) collective-permute-start(f32[64,128]{1,0:T(8,128)S(1)} %get-tuple-element.37.x_ref), channel_id=1, source_target_pairs={{0,8},{8,0},{1,9},{9,1},{2,10},{10,2},{3,11},{11,3},{4,12},{12,4},... | collective-permute-start | bytes 98312 | tf_op jit(solution)/shard_map/ppermute | solution.py:37
  84.1 0.9 collective-permute-done.6.y_ref
  85.1 0.8 collective-permute-start.7
  86.0 3.5 %collective-permute-done.7 = f32[64,128]{1,0:T(8,128)S(1)} collective-permute-done((f32[64,128]{1,0:T(8,128)S(1)}, f32[64,128]{1,0:T(8,128)S(1)}, u32[]{:S(2)}, u32[]{:S(2)}) %collective-permute-start.7) | collective-permute-done | bytes 32800 | tf_op jit(solution)/shard_map/ppermute | solution.py:37
  89.4 1.4 %all-to-all-done.5.got_ref = bf16[8,160,128]{2,1,0:T(8,128)(2,1)S(1)} async-done(((bf16[8,160,128]{2,1,0:T(8,128)(2,1)}), bf16[8,160,128]{2,1,0:T(8,128)(2,1)S(1)}, u32[]{:S(2)}, u32[]{:S(2)}) %all-to-all-start.5) | async-done | bytes 327712 | tf_op jit(solution)/shard_map/all_to_all | solution.py:25
  90.8 1.5 %shard_map.85 = (f32[256,1,128]{2,1,0:T(1,128)}, f32[8,128]{1,0:T(8,128)S(1)}, f32[224,128]{1,0:T(8,128)S(1)}) custom-call(bf16[8,160,128]{2,1,0:T(8,128)(2,1)S(1)} %all-to-all-done.5.got_ref, f32[64,128]{1,0:T(8,128)S(1)} %add.23.a_sum, bf16[2048,128]{1,0:T(8,128)(2,1)S(1)} %get-tuple-element.32.pairs_ref, bf16[2048,128]{1,0:T(8,128)(2,1)S(1)} %bitcast.12, ...), custom_call_target="tpu_custom_call" | custom-call | tf_op jit(solution)/shard_map/pallas_call | solution.py:46
  92.3 10.5 %all-to-all-start.6 = ((f32[256,1,128]{2,1,0:T(1,128)}), f32[256,1,128]{2,1,0:T(1,128)S(1)}, u32[]{:S(2)}, u32[]{:S(2)}) async-start(f32[256,1,128]{2,1,0:T(1,128)} %get-tuple-element.42), calls=%async_computation.6 | async-start | bytes 262144 | tf_op jit(solution)/shard_map/all_to_all | solution.py:25
  103.0 13.0 %all-to-all-done.6.got_ref = f32[256,1,128]{2,1,0:T(1,128)S(1)} async-done(((f32[256,1,128]{2,1,0:T(1,128)}), f32[256,1,128]{2,1,0:T(1,128)S(1)}, u32[]{:S(2)}, u32[]{:S(2)}) %all-to-all-start.6) | async-done | bytes 131104 | tf_op jit(solution)/shard_map/all_to_all | solution.py:25
  116.0 1.0 shard_map.87
  (26 shorter events, 5.0 us)
Async XLA Ops:
  0.6 0.7 copy-start.1
  0.6 0.7 copy-start
  0.7 0.7 copy-start.2
  2.0 16.0 %all-to-all-start = ((bf16[32,8,128]{2,1,0:T(8,128)(2,1)}), bf16[32,8,128]{2,1,0:T(8,128)(2,1)S(1)}, u32[]{:S(2)}, u32[]{:S(2)}) async-start(bf16[32,8,128]{2,1,0:T(8,128)(2,1)} %shard_map.76), calls=%async_computation | async-start | bytes 131072 | tf_op jit(solution)/shard_map/all_to_all | solution.py:25
  10.6 16.2 %copy-start.3 = (bf16[32,64,128]{2,1,0:T(8,128)(2,1)S(1)}, bf16[32,64,128]{2,1,0:T(8,128)(2,1)}, u32[]{:S(2)}) copy-start(bf16[32,64,128]{2,1,0:T(8,128)(2,1)} %param.5) | copy-start | bytes 1572868
  18.6 15.4 %all-to-all-start.1 = ((bf16[8,32,128]{2,1,0:T(8,128)(2,1)}), bf16[8,32,128]{2,1,0:T(8,128)(2,1)S(1)}, u32[]{:S(2)}, u32[]{:S(2)}) async-start(bf16[8,32,128]{2,1,0:T(8,128)(2,1)} %shard_map.77), calls=%async_computation.1 | async-start | bytes 131072 | tf_op jit(solution)/shard_map/all_to_all | solution.py:25
  35.8 10.3 %all-to-all-start.2 = ((bf16[8,192,128]{2,1,0:T(8,128)(2,1)}), bf16[8,192,128]{2,1,0:T(8,128)(2,1)S(1)}, u32[]{:S(2)}, u32[]{:S(2)}) async-start(bf16[8,192,128]{2,1,0:T(8,128)(2,1)} %get-tuple-element.26), calls=%async_computation.2 | async-start | bytes 786432 | tf_op jit(solution)/shard_map/all_to_all | solution.py:25
  39.2 2.7 %collective-permute-start = (f32[32,128]{1,0:T(8,128)S(1)}, f32[32,128]{1,0:T(8,128)S(1)}, u32[]{:S(2)}, u32[]{:S(2)}) collective-permute-start(f32[32,128]{1,0:T(8,128)S(1)} %get-tuple-element.27), channel_id=1, source_target_pairs={{0,8},{8,0},{1,9},{9,1},{2,10},{10,2},{3,11},{11,3},{4,12},{12,4},... | collective-permute-start | bytes 49160 | tf_op jit(solution)/shard_map/ppermute | solution.py:37
  42.0 4.1 %collective-permute-start.1 = (f32[32,128]{1,0:T(8,128)S(1)}, f32[32,128]{1,0:T(8,128)S(1)}, u32[]{:S(2)}, u32[]{:S(2)}) collective-permute-start(f32[32,128]{1,0:T(8,128)S(1)} %add.18), channel_id=1, source_target_pairs={{0,16},{16,0},{1,17},{17,1},{2,18},{18,2},{3,19},{19,3},{4,20},{20... | collective-permute-start | bytes 49160 | tf_op jit(solution)/shard_map/ppermute | solution.py:37
  46.9 13.5 %all-to-all-start.3 = ((bf16[8,160,128]{2,1,0:T(8,128)(2,1)}), bf16[8,160,128]{2,1,0:T(8,128)(2,1)S(1)}, u32[]{:S(2)}, u32[]{:S(2)}) async-start(bf16[8,160,128]{2,1,0:T(8,128)(2,1)} %get-tuple-element.28), calls=%async_computation.3 | async-start | bytes 655360 | tf_op jit(solution)/shard_map/all_to_all | solution.py:25
  50.3 4.0 %collective-permute-start.2 = (f32[64,128]{1,0:T(8,128)S(1)}, f32[64,128]{1,0:T(8,128)S(1)}, u32[]{:S(2)}, u32[]{:S(2)}) collective-permute-start(f32[64,128]{1,0:T(8,128)S(1)} %get-tuple-element.29.x_ref), channel_id=1, source_target_pairs={{0,8},{8,0},{1,9},{9,1},{2,10},{10,2},{3,11},{11,3},{4,12},{12,4},... | collective-permute-start | bytes 98312 | tf_op jit(solution)/shard_map/ppermute | solution.py:37
  54.3 4.4 %collective-permute-start.3 = (f32[64,128]{1,0:T(8,128)S(1)}, f32[64,128]{1,0:T(8,128)S(1)}, u32[]{:S(2)}, u32[]{:S(2)}) collective-permute-start(f32[64,128]{1,0:T(8,128)S(1)} %get-tuple-element.31), channel_id=1, source_target_pairs={{0,16},{16,0},{1,17},{17,1},{2,18},{18,2},{3,19},{19,3},{4,20},{20... | collective-permute-start | bytes 98312 | tf_op jit(solution)/shard_map/ppermute | solution.py:37
  62.0 14.5 %all-to-all-start.4 = ((bf16[8,192,128]{2,1,0:T(8,128)(2,1)}), bf16[8,192,128]{2,1,0:T(8,128)(2,1)S(1)}, u32[]{:S(2)}, u32[]{:S(2)}) async-start(bf16[8,192,128]{2,1,0:T(8,128)(2,1)} %get-tuple-element.34), calls=%async_computation.4 | async-start | bytes 786432 | tf_op jit(solution)/shard_map/all_to_all | solution.py:25
  68.2 4.2 %collective-permute-start.4 = (f32[32,128]{1,0:T(8,128)S(1)}, f32[32,128]{1,0:T(8,128)S(1)}, u32[]{:S(2)}, u32[]{:S(2)}) collective-permute-start(f32[32,128]{1,0:T(8,128)S(1)} %get-tuple-element.35), channel_id=1, source_target_pairs={{0,8},{8,0},{1,9},{9,1},{2,10},{10,2},{3,11},{11,3},{4,12},{12,4},... | collective-permute-start | bytes 49160 | tf_op jit(solution)/shard_map/ppermute | solution.py:37
  72.5 4.1 %collective-permute-start.5 = (f32[32,128]{1,0:T(8,128)S(1)}, f32[32,128]{1,0:T(8,128)S(1)}, u32[]{:S(2)}, u32[]{:S(2)}) collective-permute-start(f32[32,128]{1,0:T(8,128)S(1)} %add.21), channel_id=1, source_target_pairs={{0,16},{16,0},{1,17},{17,1},{2,18},{18,2},{3,19},{19,3},{4,20},{20... | collective-permute-start | bytes 49160 | tf_op jit(solution)/shard_map/ppermute | solution.py:37
  77.4 13.5 %all-to-all-start.5 = ((bf16[8,160,128]{2,1,0:T(8,128)(2,1)}), bf16[8,160,128]{2,1,0:T(8,128)(2,1)S(1)}, u32[]{:S(2)}, u32[]{:S(2)}) async-start(bf16[8,160,128]{2,1,0:T(8,128)(2,1)} %get-tuple-element.36), calls=%async_computation.5 | async-start | bytes 655360 | tf_op jit(solution)/shard_map/all_to_all | solution.py:25
  80.8 4.2 %collective-permute-start.6 = (f32[64,128]{1,0:T(8,128)S(1)}, f32[64,128]{1,0:T(8,128)S(1)}, u32[]{:S(2)}, u32[]{:S(2)}) collective-permute-start(f32[64,128]{1,0:T(8,128)S(1)} %get-tuple-element.37.x_ref), channel_id=1, source_target_pairs={{0,8},{8,0},{1,9},{9,1},{2,10},{10,2},{3,11},{11,3},{4,12},{12,4},... | collective-permute-start | bytes 98312 | tf_op jit(solution)/shard_map/ppermute | solution.py:37
  85.1 4.3 %collective-permute-start.7 = (f32[64,128]{1,0:T(8,128)S(1)}, f32[64,128]{1,0:T(8,128)S(1)}, u32[]{:S(2)}, u32[]{:S(2)}) collective-permute-start(f32[64,128]{1,0:T(8,128)S(1)} %get-tuple-element.39), channel_id=1, source_target_pairs={{0,16},{16,0},{1,17},{17,1},{2,18},{18,2},{3,19},{19,3},{4,20},{20... | collective-permute-start | bytes 98312 | tf_op jit(solution)/shard_map/ppermute | solution.py:37
  92.3 23.7 %all-to-all-start.6 = ((f32[256,1,128]{2,1,0:T(1,128)}), f32[256,1,128]{2,1,0:T(1,128)S(1)}, u32[]{:S(2)}, u32[]{:S(2)}) async-start(f32[256,1,128]{2,1,0:T(1,128)} %get-tuple-element.42), calls=%async_computation.6 | async-start | bytes 262144 | tf_op jit(solution)/shard_map/all_to_all | solution.py:25

commit v7 on v6

--- a/solution.py
+++ b/solution.py
@@ -56,8 +56,16 @@
     )(*operands)
 
 
-def pack_kernel(at_ref, bt_ref, ct_ref, sent_ref, block):
+def pack_kernel(at_hbm, bt_hbm, ct_hbm, sent_ref, block, at_ref, bt_ref, ct_ref, sems):
+    copies = [
+        pltpu.make_async_copy(source, target, sems.at[i])
+        for i, (source, target) in enumerate(((at_hbm, at_ref), (bt_hbm, bt_ref), (ct_hbm, ct_ref)))
+    ]
+    for copy in copies:
+        copy.start()
     block[...] = jnp.zeros_like(block)
+    for copy in copies:
+        copy.wait()
     block[0:4, 0:HEIGHT] = at_ref[...].astype(F32)
     block[0:4, HEIGHT : HEIGHT + DEPTH] = ct_ref[...].astype(F32)
     block[4:6, :] = bt_ref[...].astype(F32)
@@ -301,9 +309,16 @@
     sums = [tile(HEIGHT), tile(WIDTH), tile(DEPTH)]
     hats = [tile(HEIGHT), ((RANK, WIDTH), BF16), tile(DEPTH)]
 
-    (sent,) = call(
-        pack_kernel, [((N_J * N_K, 8, 128), BF16)], factor_a.T, factor_b.T, factor_c.T, scratch=[tile(8)]
-    )
+    shards_t = (factor_a.T, factor_b.T, factor_c.T)
+    sent = pl.pallas_call(
+        pack_kernel,
+        out_shape=jax.ShapeDtypeStruct((N_J * N_K, 8, 128), BF16),
+        in_specs=[pl.BlockSpec(memory_space=pl.ANY)] * 3,
+        out_specs=pl.BlockSpec(memory_space=pltpu.VMEM),
+        scratch_shapes=[pltpu.VMEM((8, 128), F32)]
+        + [pltpu.VMEM(x.shape, BF16) for x in shards_t]
+        + [pltpu.SemaphoreType.DMA((3,))],
+    )(*shards_t)
     shards = exchange(sent, PLANE)
     (sent,) = call(repack_kernel, [((N_Z, 32, 128), BF16)], shards, scratch=[tile(16), tile(16)])
     got = exchange(sent, "ia")

time: 118 us -> 118 us (level)
    pallas_call x0 -> x1, Pallas kernels: none -> 1.44 us  [local(): pl.pallas_call(pack_kernel, out_shape=jax.ShapeDtypeStruct((N_J * N_K, 8,...]
    pallas_call x12 -> x11, Pallas kernels: 9.28 us -> 8.63 us  [call(): pl.pallas_call(kernel, out_shape=[jax.ShapeDtypeStruct(shape, dtype) for...]
where the time goes in v7:
time: 118 us; the launch traced here: 117 us
  starting transfers between devices  58.9 us (50%)
  waiting for transfers between devices  45.9 us (39%)
  Pallas kernels  10.1 us (9%)
  other arithmetic  1.57 us (1%)
    all_to_all x7, starting transfers between devices, exchange(): return lax.all_to_all(blocks, axes, 0, 0, tiled=True)  43.8 us
    all_to_all x7, waiting for transfers between devices, exchange(): return lax.all_to_all(blocks, axes, 0, 0, tiled=True)  29 us
    ppermute x8, waiting for transfers between devices, swapped(): return lax.ppermute(x, axis, [(0, 1), (1, 0)])  16.8 us
    ppermute x8, starting transfers between devices, swapped(): return lax.ppermute(x, axis, [(0, 1), (1, 0)])  15.1 us
    pallas_call x11, Pallas kernels, call(): pl.pallas_call(kernel, out_shape=[jax.ShapeDtypeStruct(shape, dtype) for...  8.63 us
  transfers between devices with their start and end apart: 15, of which 13 were waited for; matrix products, arithmetic and copies ran while one was open for 1% of the time, Pallas kernels for 0%

profile of v7, /device:TPU:1, one launch (start us, length us, event | category | flops | bytes accessed | tf_op | source)
XLA Modules:
  0.0 117.1 jit_solution(11772386635652610918)
XLA Ops:
  0.6 1.4 %shard_map.76 = bf16[32,8,128]{2,1,0:T(8,128)(2,1)} custom-call(bf16[4,64]{1,0:T(4,128)(2,1)} %bitcast.13, bf16[2,128]{1,0:T(2,128)(2,1)} %bitcast.15, bf16[4,32]{1,0:T(4,128)(2,1)} %bitcast.14), custom_call_target="tpu_custom_call" | custom-call | tf_op jit(solution)/shard_map/pallas_call | solution.py:313
  2.1 8.6 %all-to-all-start = ((bf16[32,8,128]{2,1,0:T(8,128)(2,1)}), bf16[32,8,128]{2,1,0:T(8,128)(2,1)S(1)}, u32[]{:S(2)}, u32[]{:S(2)}) async-start(bf16[32,8,128]{2,1,0:T(8,128)(2,1)} %shard_map.76), calls=%async_computation | async-start | bytes 131072 | tf_op jit(solution)/shard_map/all_to_all | solution.py:25
  10.7 1.4 %multiply_convert_fusion = bf16[32,64,128]{2,1,0:T(8,128)(2,1)S(1)} fusion(s32[32,64,128]{2,1,0:T(8,128)} %param.6), kind=kLoop, calls=%fused_computation | loop fusion | flops 786432 | bytes 1572864 | tf_op jit(solution)/shard_map/convert_element_type | solution.py:306
  12.1 5.9 %all-to-all-done.got_ref = bf16[32,8,128]{2,1,0:T(8,128)(2,1)S(1)} async-done(((bf16[32,8,128]{2,1,0:T(8,128)(2,1)}), bf16[32,8,128]{2,1,0:T(8,128)(2,1)S(1)}, u32[]{:S(2)}, u32[]{:S(2)}) %all-to-all-start) | async-done | bytes 65568 | tf_op jit(solution)/shard_map/all_to_all | solution.py:25
  18.7 8.2 %all-to-all-start.1 = ((bf16[8,32,128]{2,1,0:T(8,128)(2,1)}), bf16[8,32,128]{2,1,0:T(8,128)(2,1)S(1)}, u32[]{:S(2)}, u32[]{:S(2)}) async-start(bf16[8,32,128]{2,1,0:T(8,128)(2,1)} %shard_map.77), calls=%async_computation.1 | async-start | bytes 131072 | tf_op jit(solution)/shard_map/all_to_all | solution.py:25
  27.1 7.0 %all-to-all-done.1.got_ref = bf16[8,32,128]{2,1,0:T(8,128)(2,1)S(1)} async-done(((bf16[8,32,128]{2,1,0:T(8,128)(2,1)}), bf16[8,32,128]{2,1,0:T(8,128)(2,1)S(1)}, u32[]{:S(2)}, u32[]{:S(2)}) %all-to-all-start.1) | async-done | bytes 65568 | tf_op jit(solution)/shard_map/all_to_all | solution.py:25
  34.1 1.7 %shard_map.79 = (bf16[8,192,128]{2,1,0:T(8,128)(2,1)}, f32[32,128]{1,0:T(8,128)S(1)}, bf16[128,128]{1,0:T(8,128)(2,1)S(1)}, f32[32,128]{1,0:T(8,128)S(1)}) custom-call(bf16[8,32,128]{2,1,0:T(8,128)(2,1)S(1)} %all-to-all-done.1.got_ref, f32[64,128]{1,0:T(8,128)S(1)} %shard_map.78.fa_ref, bf16[2048,128]{1,0:T(8,128)(2,1)S(1)} %bitcast_multiply_fusion.values_ref, ...), custom_call_target="tpu_custom_call" | custom-call | tf_op jit(solution)/shard_map/pallas_call | solution.py:46
  35.8 3.5 %all-to-all-start.2 = ((bf16[8,192,128]{2,1,0:T(8,128)(2,1)}), bf16[8,192,128]{2,1,0:T(8,128)(2,1)S(1)}, u32[]{:S(2)}, u32[]{:S(2)}) async-start(bf16[8,192,128]{2,1,0:T(8,128)(2,1)} %get-tuple-element.26), calls=%async_computation.2 | async-start | bytes 786432 | tf_op jit(solution)/shard_map/all_to_all | solution.py:25
  39.3 1.9 %collective-permute-start = (f32[32,128]{1,0:T(8,128)S(1)}, f32[32,128]{1,0:T(8,128)S(1)}, u32[]{:S(2)}, u32[]{:S(2)}) collective-permute-start(f32[32,128]{1,0:T(8,128)S(1)} %get-tuple-element.27), channel_id=1, source_target_pairs={{0,8},{8,0},{1,9},{9,1},{2,10},{10,2},{3,11},{11,3},{4,12},{12,4},... | collective-permute-start | bytes 49160 | tf_op jit(solution)/shard_map/ppermute | solution.py:37
  41.2 0.8 collective-permute-done
  42.0 0.8 collective-permute-start.1
  42.9 3.3 %collective-permute-done.1 = f32[32,128]{1,0:T(8,128)S(1)} collective-permute-done((f32[32,128]{1,0:T(8,128)S(1)}, f32[32,128]{1,0:T(8,128)S(1)}, u32[]{:S(2)}, u32[]{:S(2)}) %collective-permute-start.1) | collective-permute-done | bytes 16416 | tf_op jit(solution)/shard_map/ppermute | solution.py:37
  46.9 3.4 %all-to-all-start.3 = ((bf16[8,160,128]{2,1,0:T(8,128)(2,1)}), bf16[8,160,128]{2,1,0:T(8,128)(2,1)S(1)}, u32[]{:S(2)}, u32[]{:S(2)}) async-start(bf16[8,160,128]{2,1,0:T(8,128)(2,1)} %get-tuple-element.28), calls=%async_computation.3 | async-start | bytes 655360 | tf_op jit(solution)/shard_map/all_to_all | solution.py:25
  50.4 3.1 %collective-permute-start.2 = (f32[64,128]{1,0:T(8,128)S(1)}, f32[64,128]{1,0:T(8,128)S(1)}, u32[]{:S(2)}, u32[]{:S(2)}) collective-permute-start(f32[64,128]{1,0:T(8,128)S(1)} %get-tuple-element.29.x_ref), channel_id=1, source_target_pairs={{0,8},{8,0},{1,9},{9,1},{2,10},{10,2},{3,11},{11,3},{4,12},{12,4},... | collective-permute-start | bytes 98312 | tf_op jit(solution)/shard_map/ppermute | solution.py:37
  53.5 0.9 collective-permute-done.2.y_ref
  55.2 3.6 %collective-permute-done.3 = f32[64,128]{1,0:T(8,128)S(1)} collective-permute-done((f32[64,128]{1,0:T(8,128)S(1)}, f32[64,128]{1,0:T(8,128)S(1)}, u32[]{:S(2)}, u32[]{:S(2)}) %collective-permute-start.3) | collective-permute-done | bytes 32800 | tf_op jit(solution)/shard_map/ppermute | solution.py:37
  58.8 1.7 %all-to-all-done.3.got_ref = bf16[8,160,128]{2,1,0:T(8,128)(2,1)S(1)} async-done(((bf16[8,160,128]{2,1,0:T(8,128)(2,1)}), bf16[8,160,128]{2,1,0:T(8,128)(2,1)S(1)}, u32[]{:S(2)}, u32[]{:S(2)}) %all-to-all-start.3) | async-done | bytes 327712 | tf_op jit(solution)/shard_map/all_to_all | solution.py:25
  60.4 1.7 %shard_map.82 = (bf16[8,192,128]{2,1,0:T(8,128)(2,1)}, f32[32,128]{1,0:T(8,128)S(1)}, f32[224,128]{1,0:T(8,128)S(1)}, f32[2048,128]{1,0:T(8,128)S(1)}, f32[8,128]{1,0:T(8,128)S(1)}) custom-call(bf16[8,160,128]{2,1,0:T(8,128)(2,1)S(1)} %all-to-all-done.3.got_ref, f32[64,128]{1,0:T(8,128)S(1)} %add.20.a_sum, ...), custom_call_target="tpu_custom_call" | custom-call | tf_op jit(solution)/shard_map/pallas_call | solution.py:46
  62.1 6.2 %all-to-all-start.4 = ((bf16[8,192,128]{2,1,0:T(8,128)(2,1)}), bf16[8,192,128]{2,1,0:T(8,128)(2,1)S(1)}, u32[]{:S(2)}, u32[]{:S(2)}) async-start(bf16[8,192,128]{2,1,0:T(8,128)(2,1)} %get-tuple-element.34), calls=%async_computation.4 | async-start | bytes 786432 | tf_op jit(solution)/shard_map/all_to_all | solution.py:25
  68.3 3.4 %collective-permute-start.4 = (f32[32,128]{1,0:T(8,128)S(1)}, f32[32,128]{1,0:T(8,128)S(1)}, u32[]{:S(2)}, u32[]{:S(2)}) collective-permute-start(f32[32,128]{1,0:T(8,128)S(1)} %get-tuple-element.35), channel_id=1, source_target_pairs={{0,8},{8,0},{1,9},{9,1},{2,10},{10,2},{3,11},{11,3},{4,12},{12,4},... | collective-permute-start | bytes 49160 | tf_op jit(solution)/shard_map/ppermute | solution.py:37
  71.7 0.8 collective-permute-done.4
  72.6 1.0 collective-permute-start.5
  73.6 3.1 %collective-permute-done.5 = f32[32,128]{1,0:T(8,128)S(1)} collective-permute-done((f32[32,128]{1,0:T(8,128)S(1)}, f32[32,128]{1,0:T(8,128)S(1)}, u32[]{:S(2)}, u32[]{:S(2)}) %collective-permute-start.5) | collective-permute-done | bytes 16416 | tf_op jit(solution)/shard_map/ppermute | solution.py:37
  77.5 3.4 %all-to-all-start.5 = ((bf16[8,160,128]{2,1,0:T(8,128)(2,1)}), bf16[8,160,128]{2,1,0:T(8,128)(2,1)S(1)}, u32[]{:S(2)}, u32[]{:S(2)}) async-start(bf16[8,160,128]{2,1,0:T(8,128)(2,1)} %get-tuple-element.36), calls=%async_computation.5 | async-start | bytes 655360 | tf_op jit(solution)/shard_map/all_to_all | solution.py:25
  80.9 3.3 %collective-permute-start.6 = (f32[64,128]{1,0:T(8,128)S(1)}, f32[64,128]{1,0:T(8,128)S(1)}, u32[]{:S(2)}, u32[]{:S(2)}) collective-permute-start(f32[64,128]{1,0:T(8,128)S(1)} %get-tuple-element.37.x_ref), channel_id=1, source_target_pairs={{0,8},{8,0},{1,9},{9,1},{2,10},{10,2},{3,11},{11,3},{4,12},{12,4},... | collective-permute-start | bytes 98312 | tf_op jit(solution)/shard_map/ppermute | solution.py:37
  84.2 0.9 collective-permute-done.6.y_ref
  86.1 3.5 %collective-permute-done.7 = f32[64,128]{1,0:T(8,128)S(1)} collective-permute-done((f32[64,128]{1,0:T(8,128)S(1)}, f32[64,128]{1,0:T(8,128)S(1)}, u32[]{:S(2)}, u32[]{:S(2)}) %collective-permute-start.7) | collective-permute-done | bytes 32800 | tf_op jit(solution)/shard_map/ppermute | solution.py:37
  89.5 1.4 %all-to-all-done.5.got_ref = bf16[8,160,128]{2,1,0:T(8,128)(2,1)S(1)} async-done(((bf16[8,160,128]{2,1,0:T(8,128)(2,1)}), bf16[8,160,128]{2,1,0:T(8,128)(2,1)S(1)}, u32[]{:S(2)}, u32[]{:S(2)}) %all-to-all-start.5) | async-done | bytes 327712 | tf_op jit(solution)/shard_map/all_to_all | solution.py:25
  91.0 1.5 %shard_map.85 = (f32[256,1,128]{2,1,0:T(1,128)}, f32[8,128]{1,0:T(8,128)S(1)}, f32[224,128]{1,0:T(8,128)S(1)}) custom-call(bf16[8,160,128]{2,1,0:T(8,128)(2,1)S(1)} %all-to-all-done.5.got_ref, f32[64,128]{1,0:T(8,128)S(1)} %add.23.a_sum, bf16[2048,128]{1,0:T(8,128)(2,1)S(1)} %get-tuple-element.32.pairs_ref, bf16[2048,128]{1,0:T(8,128)(2,1)S(1)} %bitcast.12, ...), custom_call_target="tpu_custom_call" | custom-call | tf_op jit(solution)/shard_map/pallas_call | solution.py:46
  92.4 10.5 %all-to-all-start.6 = ((f32[256,1,128]{2,1,0:T(1,128)}), f32[256,1,128]{2,1,0:T(1,128)S(1)}, u32[]{:S(2)}, u32[]{:S(2)}) async-start(f32[256,1,128]{2,1,0:T(1,128)} %get-tuple-element.42), calls=%async_computation.6 | async-start | bytes 262144 | tf_op jit(solution)/shard_map/all_to_all | solution.py:25
  103.1 13.0 %all-to-all-done.6.got_ref = f32[256,1,128]{2,1,0:T(1,128)S(1)} async-done(((f32[256,1,128]{2,1,0:T(1,128)}), f32[256,1,128]{2,1,0:T(1,128)S(1)}, u32[]{:S(2)}, u32[]{:S(2)}) %all-to-all-start.6) | async-done | bytes 131104 | tf_op jit(solution)/shard_map/all_to_all | solution.py:25
  116.1 1.0 shard_map.87
  (20 shorter events, 4.5 us)
Async XLA Ops:
  2.1 16.0 %all-to-all-start = ((bf16[32,8,128]{2,1,0:T(8,128)(2,1)}), bf16[32,8,128]{2,1,0:T(8,128)(2,1)S(1)}, u32[]{:S(2)}, u32[]{:S(2)}) async-start(bf16[32,8,128]{2,1,0:T(8,128)(2,1)} %shard_map.76), calls=%async_computation | async-start | bytes 131072 | tf_op jit(solution)/shard_map/all_to_all | solution.py:25
  10.7 16.2 %copy-start = (bf16[32,64,128]{2,1,0:T(8,128)(2,1)S(1)}, bf16[32,64,128]{2,1,0:T(8,128)(2,1)}, u32[]{:S(2)}) copy-start(bf16[32,64,128]{2,1,0:T(8,128)(2,1)} %param.5) | copy-start | bytes 1572868
  18.7 15.4 %all-to-all-start.1 = ((bf16[8,32,128]{2,1,0:T(8,128)(2,1)}), bf16[8,32,128]{2,1,0:T(8,128)(2,1)S(1)}, u32[]{:S(2)}, u32[]{:S(2)}) async-start(bf16[8,32,128]{2,1,0:T(8,128)(2,1)} %shard_map.77), calls=%async_computation.1 | async-start | bytes 131072 | tf_op jit(solution)/shard_map/all_to_all | solution.py:25
  35.8 10.3 %all-to-all-start.2 = ((bf16[8,192,128]{2,1,0:T(8,128)(2,1)}), bf16[8,192,128]{2,1,0:T(8,128)(2,1)S(1)}, u32[]{:S(2)}, u32[]{:S(2)}) async-start(bf16[8,192,128]{2,1,0:T(8,128)(2,1)} %get-tuple-element.26), calls=%async_computation.2 | async-start | bytes 786432 | tf_op jit(solution)/shard_map/all_to_all | solution.py:25
  39.3 2.7 %collective-permute-start = (f32[32,128]{1,0:T(8,128)S(1)}, f32[32,128]{1,0:T(8,128)S(1)}, u32[]{:S(2)}, u32[]{:S(2)}) collective-permute-start(f32[32,128]{1,0:T(8,128)S(1)} %get-tuple-element.27), channel_id=1, source_target_pairs={{0,8},{8,0},{1,9},{9,1},{2,10},{10,2},{3,11},{11,3},{4,12},{12,4},... | collective-permute-start | bytes 49160 | tf_op jit(solution)/shard_map/ppermute | solution.py:37
  42.0 4.1 %collective-permute-start.1 = (f32[32,128]{1,0:T(8,128)S(1)}, f32[32,128]{1,0:T(8,128)S(1)}, u32[]{:S(2)}, u32[]{:S(2)}) collective-permute-start(f32[32,128]{1,0:T(8,128)S(1)} %add.18), channel_id=1, source_target_pairs={{0,16},{16,0},{1,17},{17,1},{2,18},{18,2},{3,19},{19,3},{4,20},{20... | collective-permute-start | bytes 49160 | tf_op jit(solution)/shard_map/ppermute | solution.py:37
  46.9 13.5 %all-to-all-start.3 = ((bf16[8,160,128]{2,1,0:T(8,128)(2,1)}), bf16[8,160,128]{2,1,0:T(8,128)(2,1)S(1)}, u32[]{:S(2)}, u32[]{:S(2)}) async-start(bf16[8,160,128]{2,1,0:T(8,128)(2,1)} %get-tuple-element.28), calls=%async_computation.3 | async-start | bytes 655360 | tf_op jit(solution)/shard_map/all_to_all | solution.py:25
  50.4 4.0 %collective-permute-start.2 = (f32[64,128]{1,0:T(8,128)S(1)}, f32[64,128]{1,0:T(8,128)S(1)}, u32[]{:S(2)}, u32[]{:S(2)}) collective-permute-start(f32[64,128]{1,0:T(8,128)S(1)} %get-tuple-element.29.x_ref), channel_id=1, source_target_pairs={{0,8},{8,0},{1,9},{9,1},{2,10},{10,2},{3,11},{11,3},{4,12},{12,4},... | collective-permute-start | bytes 98312 | tf_op jit(solution)/shard_map/ppermute | solution.py:37
  54.4 4.4 %collective-permute-start.3 = (f32[64,128]{1,0:T(8,128)S(1)}, f32[64,128]{1,0:T(8,128)S(1)}, u32[]{:S(2)}, u32[]{:S(2)}) collective-permute-start(f32[64,128]{1,0:T(8,128)S(1)} %get-tuple-element.31), channel_id=1, source_target_pairs={{0,16},{16,0},{1,17},{17,1},{2,18},{18,2},{3,19},{19,3},{4,20},{20... | collective-permute-start | bytes 98312 | tf_op jit(solution)/shard_map/ppermute | solution.py:37
  62.1 14.5 %all-to-all-start.4 = ((bf16[8,192,128]{2,1,0:T(8,128)(2,1)}), bf16[8,192,128]{2,1,0:T(8,128)(2,1)S(1)}, u32[]{:S(2)}, u32[]{:S(2)}) async-start(bf16[8,192,128]{2,1,0:T(8,128)(2,1)} %get-tuple-element.34), calls=%async_computation.4 | async-start | bytes 786432 | tf_op jit(solution)/shard_map/all_to_all | solution.py:25
  68.3 4.2 %collective-permute-start.4 = (f32[32,128]{1,0:T(8,128)S(1)}, f32[32,128]{1,0:T(8,128)S(1)}, u32[]{:S(2)}, u32[]{:S(2)}) collective-permute-start(f32[32,128]{1,0:T(8,128)S(1)} %get-tuple-element.35), channel_id=1, source_target_pairs={{0,8},{8,0},{1,9},{9,1},{2,10},{10,2},{3,11},{11,3},{4,12},{12,4},... | collective-permute-start | bytes 49160 | tf_op jit(solution)/shard_map/ppermute | solution.py:37
  72.6 4.1 %collective-permute-start.5 = (f32[32,128]{1,0:T(8,128)S(1)}, f32[32,128]{1,0:T(8,128)S(1)}, u32[]{:S(2)}, u32[]{:S(2)}) collective-permute-start(f32[32,128]{1,0:T(8,128)S(1)} %add.21), channel_id=1, source_target_pairs={{0,16},{16,0},{1,17},{17,1},{2,18},{18,2},{3,19},{19,3},{4,20},{20... | collective-permute-start | bytes 49160 | tf_op jit(solution)/shard_map/ppermute | solution.py:37
  77.5 13.5 %all-to-all-start.5 = ((bf16[8,160,128]{2,1,0:T(8,128)(2,1)}), bf16[8,160,128]{2,1,0:T(8,128)(2,1)S(1)}, u32[]{:S(2)}, u32[]{:S(2)}) async-start(bf16[8,160,128]{2,1,0:T(8,128)(2,1)} %get-tuple-element.36), calls=%async_computation.5 | async-start | bytes 655360 | tf_op jit(solution)/shard_map/all_to_all | solution.py:25
  80.9 4.2 %collective-permute-start.6 = (f32[64,128]{1,0:T(8,128)S(1)}, f32[64,128]{1,0:T(8,128)S(1)}, u32[]{:S(2)}, u32[]{:S(2)}) collective-permute-start(f32[64,128]{1,0:T(8,128)S(1)} %get-tuple-element.37.x_ref), channel_id=1, source_target_pairs={{0,8},{8,0},{1,9},{9,1},{2,10},{10,2},{3,11},{11,3},{4,12},{12,4},... | collective-permute-start | bytes 98312 | tf_op jit(solution)/shard_map/ppermute | solution.py:37
  85.3 4.3 %collective-permute-start.7 = (f32[64,128]{1,0:T(8,128)S(1)}, f32[64,128]{1,0:T(8,128)S(1)}, u32[]{:S(2)}, u32[]{:S(2)}) collective-permute-start(f32[64,128]{1,0:T(8,128)S(1)} %get-tuple-element.39), channel_id=1, source_target_pairs={{0,16},{16,0},{1,17},{17,1},{2,18},{18,2},{3,19},{19,3},{4,20},{20... | collective-permute-start | bytes 98312 | tf_op jit(solution)/shard_map/ppermute | solution.py:37
  92.4 23.7 %all-to-all-start.6 = ((f32[256,1,128]{2,1,0:T(1,128)}), f32[256,1,128]{2,1,0:T(1,128)S(1)}, u32[]{:S(2)}, u32[]{:S(2)}) async-start(f32[256,1,128]{2,1,0:T(1,128)} %get-tuple-element.42), calls=%async_computation.6 | async-start | bytes 262144 | tf_op jit(solution)/shard_map/all_to_all | solution.py:25
